TPU v7x, 256 devices: a whole 4x4x8 slice. The times are simulated.
256 devices in a mesh: seq: 64 (over z_hi, x, y, core), chan: 4 (over z_lo).
Axes of the slice: x: 4, y: 4, z: 8 (z_hi: 2, z_lo: 4; z = z_hi * 4 + z_lo), core: 2. Of those that a mesh axis runs over, the one named last changes fastest.
Arguments:
- query_stream: bfloat16 [16384, 4096], P('seq', 'chan'), may hold values from -6 to 6
- key_stream: bfloat16 [16384, 4096], P('seq', 'chan'), may hold values from -6 to 6
- value_stream: bfloat16 [16384, 4096], P('seq', 'chan'), may hold values from -6 to 6
- short_filter: float32 [3, 3, 4096], P(None, None, 'chan'), may hold values from -3 to 3
- decay_rate: float32 [4096, 16], P('chan'), may hold values from 1.2207031e-05 to 0.034, as said below
- residues: float32 [4096, 16], P('chan'), may hold values from -0.3 to 0.3
- skip_bias: float32 [4096], P('chan'), may hold values from -4 to 4
- out_weight: bfloat16 [4096, 4096], P('chan'), may hold values from -0.09375 to 0.09375
Outputs:
- mixed: bfloat16 [16384, 4096], P(('seq', 'chan'))
Inputs may be any that keep to these rules, and one draw needn't show every extreme that they name: `decay_rate`: each mode's rate is positive; some modes decay within a few tens of positions, others keep a large share of their weight over the whole sequence.
All inputs are finite; a program needn't handle non-finite values.
Results may differ from a plain program's by a relative error of at most 0.015.
Values may be sent and summed in bfloat16 or wider, within the bound.
No kernel may reach another device: no remote copies, remote signals or barrier semaphores. Data moves between devices by JAX's collectives and lax.ppermute only.
A program may use at most 256 MiB of HBM per device.

v0:
```python
import math

import jax
import jax.numpy as jnp
from jax import lax
from jax.sharding import PartitionSpec as P

MODES = 16
SHORT = 3


def passed_along(array, axis, by):
    length = lax.axis_size(axis)
    pairs = [(i, i + by) for i in range(length) if 0 <= i + by < length]
    return lax.ppermute(array, axis, pairs)


def unit_table(first, second, period):
    product = first[:, None] * second[None, :] % period
    angle = product.astype(jnp.float32) * (2.0 * math.pi / period)
    return (jnp.cos(angle), jnp.sin(angle))


def precise(form, left, right):
    return jnp.einsum(form, left, right, precision=lax.Precision.HIGHEST)


def rotate(real_part, imag_part, cosine, sine):
    return (real_part * cosine + imag_part * sine, imag_part * cosine - real_part * sine)


def transform_path(gated, decay_rate, residues):
    seq_count = lax.axis_size("seq")
    seq_place = lax.axis_index("seq")
    tok_rows = gated.shape[0]
    piece_rows = tok_rows // seq_count
    period = 2 * seq_count * tok_rows
    sources = jnp.arange(seq_count, dtype=jnp.int32)
    frequencies = jnp.arange(2 * seq_count, dtype=jnp.int32)
    cos_one, sin_one = unit_table(frequencies, sources, 2 * seq_count)
    spread_rows = seq_place * piece_rows + jnp.arange(piece_rows, dtype=jnp.int32)
    wide_cos, wide_sin = unit_table(frequencies, spread_rows, period)
    wide_cos = wide_cos[:, :, None]
    wide_sin = wide_sin[:, :, None]
    owned_freqs = 2 * seq_place + jnp.arange(2, dtype=jnp.int32)
    all_rows = jnp.arange(tok_rows, dtype=jnp.int32)
    near_cos, near_sin = unit_table(owned_freqs, all_rows, period)
    near_cos = near_cos[:, :, None]
    near_sin = near_sin[:, :, None]
    cos_two, sin_two = unit_table(all_rows, all_rows, tok_rows)

    def first_section(signal):
        real_part = precise("ks,sic->kic", cos_one, signal)
        imag_part = -precise("ks,sic->kic", sin_one, signal)
        return rotate(real_part, imag_part, wide_cos, wide_sin)

    def second_section(real_part, imag_part):
        return (
            precise("ki,sic->skc", cos_two, real_part) + precise("ki,sic->skc", sin_two, imag_part),
            precise("ki,sic->skc", cos_two, imag_part) - precise("ki,sic->skc", sin_two, real_part),
        )

    moments = (seq_place * tok_rows + all_rows).astype(jnp.float32)[:, None]
    kernel = jnp.zeros(gated.shape, jnp.float32)
    for mode_index in range(MODES):
        kernel = kernel + residues[:, mode_index] * jnp.exp(-decay_rate[:, mode_index] * moments)
    signal_rows, kernel_rows = (
        lax.all_to_all(
            gated.astype(jnp.float32)[None], "seq", split_axis=1, concat_axis=0, tiled=True
        ),
        lax.all_to_all(kernel[None], "seq", split_axis=1, concat_axis=0, tiled=True),
    )
    signal_real, signal_imag = first_section(signal_rows)
    kernel_real, kernel_imag = first_section(kernel_rows)
    signal_real, signal_imag, kernel_real, kernel_imag = (
        lax.all_to_all(signal_real, "seq", split_axis=0, concat_axis=1, tiled=True),
        lax.all_to_all(signal_imag, "seq", split_axis=0, concat_axis=1, tiled=True),
        lax.all_to_all(kernel_real, "seq", split_axis=0, concat_axis=1, tiled=True),
        lax.all_to_all(kernel_imag, "seq", split_axis=0, concat_axis=1, tiled=True),
    )
    signal_real, signal_imag = second_section(signal_real, signal_imag)
    kernel_real, kernel_imag = second_section(kernel_real, kernel_imag)
    prod_real = signal_real * kernel_real - signal_imag * kernel_imag
    prod_imag = signal_real * kernel_imag + signal_imag * kernel_real
    back_real = precise("ik,skc->sic", cos_two, prod_real) - precise(
        "ik,skc->sic", sin_two, prod_imag
    )
    back_imag = precise("ik,skc->sic", cos_two, prod_imag) + precise(
        "ik,skc->sic", sin_two, prod_real
    )
    back_real, back_imag = rotate(back_real, back_imag, near_cos, -near_sin)
    back_real, back_imag = (
        lax.all_to_all(back_real, "seq", split_axis=1, concat_axis=0, tiled=True),
        lax.all_to_all(back_imag, "seq", split_axis=1, concat_axis=0, tiled=True),
    )
    long_term = (
        precise("ks,kic->sic", cos_one, back_real) - precise("ks,kic->sic", sin_one, back_imag)
    ) * (1.0 / period)
    return lax.all_to_all(long_term, "seq", split_axis=0, concat_axis=1, tiled=True)[0]


def on_device(
    query_stream,
    key_stream,
    value_stream,
    short_filter,
    decay_rate,
    residues,
    skip_bias,
    out_weight,
):
    tok_rows = query_stream.shape[0]
    streams = jnp.stack([query_stream, key_stream, value_stream])
    border = passed_along(streams[:, tok_rows - (SHORT - 1) :, :], "seq", 1)
    extended = jnp.concatenate([border, streams], axis=1).astype(jnp.float32)
    filtered = short_filter[:, 0, None, :] * extended[:, SHORT - 1 :, :]
    for offset in range(1, SHORT):
        filtered = (
            filtered
            + short_filter[:, offset, None, :]
            * extended[:, SHORT - 1 - offset : SHORT - 1 - offset + tok_rows, :]
        )
    short_query = filtered[0]
    gated = (filtered[1] * filtered[2]).astype(jnp.bfloat16)
    long_term = transform_path(gated, decay_rate, residues)
    mixed_in = ((long_term + skip_bias * gated.astype(jnp.float32)) * short_query).astype(
        jnp.bfloat16
    )
    summed = lax.psum_scatter(
        jnp.dot(mixed_in, out_weight, preferred_element_type=jnp.float32),
        "chan",
        scatter_dimension=0,
        tiled=True,
    )
    return summed.astype(jnp.bfloat16)


def solution(mesh):
    return jax.shard_map(
        on_device,
        mesh=mesh,
        in_specs=(
            P("seq", "chan"),
            P("seq", "chan"),
            P("seq", "chan"),
            P(None, None, "chan"),
            P("chan", None),
            P("chan", None),
            P("chan"),
            P("chan", None),
        ),
        out_specs=P(("seq", "chan"), None),
        check_vma=False,
    )
```

profile of v0, /device:TPU:32, one launch (start us, length us, event | category | flops | bytes accessed | tf_op | source)
XLA Modules:
  0.0 647.9 jit_solution(8416999596388380801)
XLA Ops:
  14.0 13.8 %all-to-all-start.3 = ((f32[1,256,1024]{2,0,1:T(1,128)}), f32[1,256,1024]{2,0,1:T(1,128)S(1)}, u32[]{:S(2)}, u32[]{:S(2)}) async-start(f32[1,256,1024]{2,0,1:T(1,128)} %copy.71), calls=%async_computation.3 | async-start | bytes 2097152 | tf_op jit(solution)/shard_map/all_to_all | solution.py:71
  35.9 23.5 %all-to-all-done.3 = f32[1,256,1024]{2,0,1:T(1,128)S(1)} async-done(((f32[1,256,1024]{2,0,1:T(1,128)}), f32[1,256,1024]{2,0,1:T(1,128)S(1)}, u32[]{:S(2)}, u32[]{:S(2)}) %all-to-all-start.3) | async-done | bytes 1048608 | tf_op jit(solution)/shard_map/all_to_all | solution.py:71
  59.5 10.1 %all-to-all-start = ((f32[1,256,1024]{2,0,1:T(1,128)}), f32[1,256,1024]{2,0,1:T(1,128)S(1)}, u32[]{:S(2)}, u32[]{:S(2)}) async-start(f32[1,256,1024]{2,0,1:T(1,128)} %copy.62), calls=%async_computation | async-start | bytes 2097152 | tf_op jit(solution)/shard_map/all_to_all | solution.py:68
  78.7 17.7 %all-to-all-done = f32[1,256,1024]{2,0,1:T(1,128)S(1)} async-done(((f32[1,256,1024]{2,0,1:T(1,128)}), f32[1,256,1024]{2,0,1:T(1,128)S(1)}, u32[]{:S(2)}, u32[]{:S(2)}) %all-to-all-start) | async-done | bytes 1048608 | tf_op jit(solution)/shard_map/all_to_all | solution.py:68
  106.7 5.9 multiply_subtract_fusion.1
  115.2 5.7 all-to-all-start.5
  123.7 50.7 %all-to-all-done.5 = f32[128,4,1024]{2,1,0:T(4,128)} async-done(((f32[128,4,1024]{2,1,0:T(4,128)}), f32[128,4,1024]{2,1,0:T(4,128)}, u32[]{:S(2)}, u32[]{:S(2)}) %all-to-all-start.5) | async-done | bytes 2097184 | tf_op jit(solution)/shard_map/all_to_all | solution.py:79
  174.4 5.6 all-to-all-start.4
  182.7 51.0 %all-to-all-done.4 = f32[128,4,1024]{2,1,0:T(4,128)} async-done(((f32[128,4,1024]{2,1,0:T(4,128)}), f32[128,4,1024]{2,1,0:T(4,128)}, u32[]{:S(2)}, u32[]{:S(2)}) %all-to-all-start.4) | async-done | bytes 2097184 | tf_op jit(solution)/shard_map/all_to_all | solution.py:78
  233.7 5.8 all-to-all-start.2
  242.2 51.0 %all-to-all-done.2 = f32[128,4,1024]{2,1,0:T(4,128)} async-done(((f32[128,4,1024]{2,1,0:T(4,128)}), f32[128,4,1024]{2,1,0:T(4,128)}, u32[]{:S(2)}, u32[]{:S(2)}) %all-to-all-start.2) | async-done | bytes 2097184 | tf_op jit(solution)/shard_map/all_to_all | solution.py:77
  293.2 5.6 all-to-all-start.1
  311.0 4.8 copy.69
  319.0 4.6 fusion.44
  339.1 13.3 %all-to-all-done.1 = f32[128,4,1024]{2,1,0:T(4,128)} async-done(((f32[128,4,1024]{2,1,0:T(4,128)}), f32[128,4,1024]{2,1,0:T(4,128)}, u32[]{:S(2)}, u32[]{:S(2)}) %all-to-all-start.1) | async-done | bytes 2097184 | tf_op jit(solution)/shard_map/all_to_all | solution.py:76
  352.5 4.8 copy.66
  361.4 4.6 fusion.50
  389.8 5.6 all-to-all-start.7
  397.8 51.3 %all-to-all-done.7 = f32[2,256,1024]{2,0,1:T(2,128)} async-done(((f32[2,256,1024]{2,0,1:T(2,128)}), f32[2,256,1024]{2,0,1:T(2,128)}, u32[]{:S(2)}, u32[]{:S(2)}) %all-to-all-start.7) | async-done | bytes 2097184 | tf_op jit(solution)/shard_map/all_to_all | solution.py:94
  449.1 5.0 all-to-all-start.6
  461.8 46.2 %all-to-all-done.6 = f32[2,256,1024]{2,0,1:T(2,128)S(1)} async-done(((f32[2,256,1024]{2,0,1:T(2,128)}), f32[2,256,1024]{2,0,1:T(2,128)S(1)}, u32[]{:S(2)}, u32[]{:S(2)}) %all-to-all-start.6) | async-done | bytes 2097184 | tf_op jit(solution)/shard_map/all_to_all | solution.py:93
  516.5 36.9 %all_to_all.141 = f32[64,4,1024]{2,1,0:T(4,128)S(1)} all-to-all(f32[64,4,1024]{2,1,0:T(4,128)S(1)} %copy.88), channel_id=1, replica_groups=mesh['seq'=64,'chan'=4] {'seq'}, dimensions={0} | all-to-all | bytes 2097152 | tf_op jit(solution)/shard_map/all_to_all | solution.py:99
  553.8 8.0 %fusion.30 = f32[256,4096]{1,0:T(8,128)} fusion(bf16[1024,4096]{1,0:T(8,128)(2,1)} %param.15, f32[3,256,1024]{2,1,0:T(8,128)} %copy-done.3, f32[256,1024]{1,0:T(8,128)S(1)} %squeeze.4, f32[1,256,1024]{2,1,0:T(8,128)S(1)} %fusion.29, f32[1024]{0:T(1024)S(1)} %copy-done.15), kind=kOutput, calls=%fused_computation.47 | convolution fusion | flops 2148532224 | bytes 15732736 | tf_op jit(solution)/shard_map/dot_general | solution.py:130
  561.8 77.0 %reduce-scatter.2.cloned.1.call-done = f32[64,4096]{1,0:T(8,128)} async-done(((f32[256,4096]{1,0:T(8,128)}), f32[64,4096]{1,0:T(8,128)}) %reduce-scatter.2.cloned.1.call-update) | async-done | bytes 1048592 | tf_op jit(solution)/shard_map/reduce_scatter | solution.py:129
  (93 shorter events, 125.4 us)
Async XLA Ops:
  11.9 15.9 %copy-start.12 = (bf16[256,1024]{1,0:T(8,128)(2,1)S(1)}, bf16[256,1024]{1,0:T(8,128)(2,1)}, u32[]{:S(2)}) copy-start(bf16[256,1024]{1,0:T(8,128)(2,1)} %param.10) | copy-start | bytes 1572868
  11.9 15.9 %copy-start.13 = (bf16[256,1024]{1,0:T(8,128)(2,1)S(1)}, bf16[256,1024]{1,0:T(8,128)(2,1)}, u32[]{:S(2)}) copy-start(bf16[256,1024]{1,0:T(8,128)(2,1)} %param.9) | copy-start | bytes 1572868
  11.9 15.9 %copy-start.14 = (bf16[256,1024]{1,0:T(8,128)(2,1)S(1)}, bf16[256,1024]{1,0:T(8,128)(2,1)}, u32[]{:S(2)}) copy-start(bf16[256,1024]{1,0:T(8,128)(2,1)} %param.8) | copy-start | bytes 1572868
  14.0 15.8 %copy-start.16 = (f32[3,3,1024]{2,1,0:T(4,128)S(1)}, f32[3,3,1024]{2,1,0:T(4,128)}, u32[]{:S(2)}) copy-start(f32[3,3,1024]{2,1,0:T(4,128)} %param.11) | copy-start | bytes 110596
  14.0 45.4 %all-to-all-start.3 = ((f32[1,256,1024]{2,0,1:T(1,128)}), f32[1,256,1024]{2,0,1:T(1,128)S(1)}, u32[]{:S(2)}, u32[]{:S(2)}) async-start(f32[1,256,1024]{2,0,1:T(1,128)} %copy.71), calls=%async_computation.3 | async-start | bytes 2097152 | tf_op jit(solution)/shard_map/all_to_all | solution.py:71
  27.9 2.8 collective-permute-start
  59.5 36.9 %all-to-all-start = ((f32[1,256,1024]{2,0,1:T(1,128)}), f32[1,256,1024]{2,0,1:T(1,128)S(1)}, u32[]{:S(2)}, u32[]{:S(2)}) async-start(f32[1,256,1024]{2,0,1:T(1,128)} %copy.62), calls=%async_computation | async-start | bytes 2097152 | tf_op jit(solution)/shard_map/all_to_all | solution.py:68
  115.2 5.7 copy-start.10
  115.2 59.2 %all-to-all-start.5 = ((f32[128,4,1024]{2,1,0:T(4,128)}), f32[128,4,1024]{2,1,0:T(4,128)}, u32[]{:S(2)}, u32[]{:S(2)}) async-start(f32[128,4,1024]{2,1,0:T(4,128)} %copy.77), calls=%async_computation.5 | async-start | bytes 4194304 | tf_op jit(solution)/shard_map/all_to_all | solution.py:79
  123.7 56.3 %copy-start.7 = (f32[128,4,1024]{2,0,1:T(8,128)S(1)}, f32[128,4,1024]{2,0,1:T(8,128)}, u32[]{:S(2)}) copy-start(f32[128,4,1024]{2,0,1:T(8,128)} %get-tuple-element.48) | copy-start | bytes 6291460
  174.4 59.3 %all-to-all-start.4 = ((f32[128,4,1024]{2,1,0:T(4,128)}), f32[128,4,1024]{2,1,0:T(4,128)}, u32[]{:S(2)}, u32[]{:S(2)}) async-start(f32[128,4,1024]{2,1,0:T(4,128)} %copy.74), calls=%async_computation.4 | async-start | bytes 4194304 | tf_op jit(solution)/shard_map/all_to_all | solution.py:78
  182.7 56.8 %copy-start.6 = (f32[128,4,1024]{2,0,1:T(8,128)S(1)}, f32[128,4,1024]{2,0,1:T(8,128)}, u32[]{:S(2)}) copy-start(f32[128,4,1024]{2,0,1:T(8,128)} %get-tuple-element.49) | copy-start | bytes 6291460
  233.7 59.5 %all-to-all-start.2 = ((f32[128,4,1024]{2,1,0:T(4,128)}), f32[128,4,1024]{2,1,0:T(4,128)}, u32[]{:S(2)}, u32[]{:S(2)}) async-start(f32[128,4,1024]{2,1,0:T(4,128)} %copy.68), calls=%async_computation.2 | async-start | bytes 4194304 | tf_op jit(solution)/shard_map/all_to_all | solution.py:77
  293.2 59.3 %all-to-all-start.1 = ((f32[128,4,1024]{2,1,0:T(4,128)}), f32[128,4,1024]{2,1,0:T(4,128)}, u32[]{:S(2)}, u32[]{:S(2)}) async-start(f32[128,4,1024]{2,1,0:T(4,128)} %copy.65), calls=%async_computation.1 | async-start | bytes 4194304 | tf_op jit(solution)/shard_map/all_to_all | solution.py:76
  319.0 4.6 copy-start.2
  330.6 4.2 copy-start
  361.4 7.5 %copy-start.9 = (f32[2,1024,256]{2,1,0:T(8,128)S(1)}, f32[2,1024,256]{2,1,0:T(8,128)}, u32[]{:S(2)}) copy-start(f32[2,1024,256]{2,1,0:T(8,128)} %fusion.46) | copy-start | bytes 6291460
  366.0 2.9 copy-start.1
  366.0 2.9 copy-start.4
  366.0 2.9 copy-start.5
  389.8 59.3 %all-to-all-start.7 = ((f32[2,256,1024]{2,0,1:T(2,128)}), f32[2,256,1024]{2,0,1:T(2,128)}, u32[]{:S(2)}, u32[]{:S(2)}) async-start(f32[2,256,1024]{2,0,1:T(2,128)} %copy.86), calls=%async_computation.7 | async-start | bytes 4194304 | tf_op jit(solution)/shard_map/all_to_all | solution.py:94
  449.1 58.9 %all-to-all-start.6 = ((f32[2,256,1024]{2,0,1:T(2,128)}), f32[2,256,1024]{2,0,1:T(2,128)S(1)}, u32[]{:S(2)}, u32[]{:S(2)}) async-start(f32[2,256,1024]{2,0,1:T(2,128)} %copy.84), calls=%async_computation.6 | async-start | bytes 4194304 | tf_op jit(solution)/shard_map/all_to_all | solution.py:93
  454.1 184.7 %reduce-scatter.2.cloned.1.call-start = ((), (), s32[]{:S(2)}) async-start(), calls=%async_computation.10 | async-start | bytes 5242880 | tf_op jit(solution)/shard_map/reduce_scatter | solution.py:129
  516.5 37.3 %copy-start.15 = (f32[1024]{0:T(1024)S(1)}, f32[1024]{0:T(1024)}, u32[]{:S(2)}) copy-start(f32[1024]{0:T(1024)} %param.14) | copy-start | bytes 12292
  (3 other events, 5.9 us)
Sparse Core Ops, SparseCore 0:
  561.9 76.8 reduce-scatter.1
where the time goes:
time: 657 us; the launch traced here: 648 us
  waiting for transfers between devices  383 us (58%)
  local copies, waits for them, and re-layouts  70.3 us (11%)
  matrix products  69.5 us (11%)
  starting transfers between devices  59.2 us (9%)
  blocking collectives  36.9 us (6%)
  other arithmetic  15.3 us (2%)
  between operations  14.1 us (2%)
    reduce_scatter x1, waiting for transfers between devices, on_device(): lax.psum_scatter(jnp.dot(mixed_in, out_weight, preferred_element_type=jnp...  77 us
    dot_general x18, matrix products, precise(): return jnp.einsum(form, left, right, precision=lax.Precision.HIGHEST)  61.5 us
    all_to_all x1, waiting for transfers between devices, transform_path(): lax.all_to_all(back_imag, 'seq', split_axis=1, concat_axis=0, tiled=True)  51.3 us
    all_to_all x1, waiting for transfers between devices, transform_path(): lax.all_to_all(kernel_real, 'seq', split_axis=0, concat_axis=1, tiled=True)  51 us
    all_to_all x1, waiting for transfers between devices, transform_path(): lax.all_to_all(signal_imag, 'seq', split_axis=0, concat_axis=1, tiled=True)  51 us
    all_to_all x1, waiting for transfers between devices, transform_path(): lax.all_to_all(kernel_imag, 'seq', split_axis=0, concat_axis=1, tiled=True)  50.7 us
    all_to_all x1, waiting for transfers between devices, transform_path(): lax.all_to_all(back_real, 'seq', split_axis=1, concat_axis=0, tiled=True)  46.2 us
    all_to_all x1, blocking collectives, transform_path(): lax.all_to_all(long_term, 'seq', split_axis=0, concat_axis=1, tiled=True)[0]  36.9 us
  transfers between devices with their start and end apart: 10, of which 10 were waited for; matrix products, arithmetic and copies ran while one was open for 10% of the time, Pallas kernels for 0%

commit v1 on v0

v1 whole, which is shorter than its diff:
```python
import functools

import jax
import jax.numpy as jnp
from jax import lax
from jax.experimental import pallas as pl
from jax.experimental.pallas import tpu as pltpu
from jax.sharding import PartitionSpec as P

MODES = 16
SHORT = 3
F32 = jnp.float32
BF16 = jnp.bfloat16
LANES = 128
SUB = 8
PAD = 8
VMEM_LIMIT = 40 * 1024 * 1024


def short_taps(ext, taps_ref, stream, lanes, first, count):
    return (
        taps_ref[stream, 0:1, lanes] * ext[pl.ds(PAD + first, count), :]
        + taps_ref[stream, 1:2, lanes] * ext[pl.ds(PAD + first - 1, count), :]
        + taps_ref[stream, 2:3, lanes] * ext[pl.ds(PAD + first - 2, count), :]
    )


def fill_ext(ext, border_ref, stream_ref, stream, lanes, rows):
    ext[0:PAD, :] = jnp.zeros((PAD, LANES), F32)
    ext[PAD - 2 : PAD, :] = border_ref[stream, :, lanes].astype(F32)
    ext[PAD : PAD + rows, :] = stream_ref[:, lanes].astype(F32)


def state_kernel(border_ref, key_ref, value_ref, taps_ref, rate_ref, state_ref, gated_ref, ext_key, ext_value):
    rows = key_ref.shape[0]
    pitch = rows + PAD
    for group in range(SUB):
        lanes = slice(group * LANES, (group + 1) * LANES)
        fill_ext(ext_key, border_ref, key_ref, 1, lanes, rows)
        fill_ext(ext_value, border_ref, value_ref, 2, lanes, rows)
        gated = short_taps(ext_key, taps_ref, 1, lanes, 0, rows) * short_taps(ext_value, taps_ref, 2, lanes, 0, rows)
        gated_ref[group * pitch : group * pitch + rows, :] = gated.astype(BF16).astype(F32)
        gated_ref[group * pitch + rows : (group + 1) * pitch, :] = jnp.zeros((PAD, LANES), F32)
    decay = [jnp.exp(-rate_ref[m]) for m in range(MODES)]

    def step(t, carry):
        now = gated_ref[pl.ds(t, SUB, stride=pitch), :]
        return tuple(decay[m] * carry[m] + now for m in range(MODES))

    final = lax.fori_loop(0, rows, step, tuple(jnp.zeros((SUB, LANES), F32) for _ in range(MODES)), unroll=8)
    for m in range(MODES):
        state_ref[m] = final[m]


def local_kernel(border_ref, query_ref, gated_ref, taps_ref, rate_ref, residue_ref, skip_ref, local_ref, query_out_ref, ext, conv):
    rows = query_ref.shape[0]
    pitch = rows + PAD
    decay = [jnp.exp(-rate_ref[m]) for m in range(MODES)]

    def step(t, carry):
        now = gated_ref[pl.ds(t, SUB, stride=pitch), :]
        fresh = tuple(decay[m] * carry[m] + now for m in range(MODES))
        terms = [residue_ref[m] * fresh[m] for m in range(MODES)]
        while len(terms) > 1:
            terms = [terms[i] + terms[i + 1] for i in range(0, len(terms), 2)]
        conv[pl.ds(t, SUB, stride=pitch), :] = terms[0]
        return fresh

    lax.fori_loop(0, rows, step, tuple(jnp.zeros((SUB, LANES), F32) for _ in range(MODES)), unroll=4)
    for group in range(SUB):
        lanes = slice(group * LANES, (group + 1) * LANES)
        spot = slice(group * pitch, group * pitch + rows)
        local_ref[:, lanes] = conv[spot, :] + skip_ref[0:1, lanes] * gated_ref[spot, :]
        fill_ext(ext, border_ref, query_ref, 0, lanes, rows)
        query_out_ref[:, lanes] = short_taps(ext, taps_ref, 0, lanes, 0, rows)


def mix_kernel(local_ref, query_ref, start_ref, rate_ref, residue_ref, mixed_ref):
    rows = local_ref.shape[0]
    phase = lax.broadcasted_iota(jnp.int32, (SUB, LANES), 0).astype(F32) + 1.0
    for group in range(SUB):
        lanes = slice(group * LANES, (group + 1) * LANES)
        line = slice(group, group + 1)
        carry, decay = [], []
        for m in range(MODES):
            rate = rate_ref[m, line, :]
            carry.append(jnp.exp(-rate * phase) * (residue_ref[m, line, :] * start_ref[m, line, :]))
            decay.append(jnp.broadcast_to(jnp.exp(-rate * float(SUB)), (SUB, LANES)))
        for tile in range(0, rows, 2 * SUB):
            parts = []
            for half in range(2):
                spot = slice(tile + half * SUB, tile + (half + 1) * SUB)
                terms = list(carry)
                while len(terms) > 1:
                    terms = [terms[i] + terms[i + 1] for i in range(0, len(terms), 2)]
                parts.append((local_ref[spot, lanes] + terms[0]) * query_ref[spot, lanes])
                carry = [carry[m] * decay[m] for m in range(MODES)]
            mixed_ref[tile : tile + 2 * SUB, lanes] = jnp.concatenate(parts, axis=0).astype(BF16)


def whole(count):
    return [pl.BlockSpec(memory_space=pltpu.VMEM)] * count


def levels_of(count):
    levels, left = [], count
    if left % 2 == 0:
        levels.append(2)
        left //= 2
    while left % 4 == 0:
        levels.append(4)
        left //= 4
    if left > 1:
        levels.append(left)
    return levels


def scan_states(state, rate, rows):
    count = lax.axis_size("seq")
    place = lax.axis_index("seq")
    total, start, width = state, jnp.zeros_like(state), 1
    levels = levels_of(count)
    for position, radix in enumerate(levels):
        me = (place // width) % radix
        low = (place % width).astype(F32)
        others = [
            lax.ppermute(total.astype(BF16), "seq", [(j, j ^ (width * s)) for j in range(count)])
            for s in range(1, radix)
        ]
        for s in range(1, radix):
            other = me ^ s
            gap = jnp.maximum(me - 1 - other, 0).astype(F32)
            weight = jnp.where(other < me, jnp.exp(-rate * (rows * (width * gap + low))), 0.0)
            start = start + weight * others[s - 1].astype(F32)
        if position < len(levels) - 1:
            fresh = total * jnp.exp(-rate * (rows * width * (radix - 1 - me).astype(F32)))
            for s in range(1, radix):
                other = me ^ s
                fresh = fresh + others[s - 1].astype(F32) * jnp.exp(
                    -rate * (rows * width * (radix - 1 - other).astype(F32))
                )
            total = fresh
        width *= radix
    return start


def on_device(query_stream, key_stream, value_stream, short_filter, decay_rate, residues, skip_bias, out_weight):
    rows, channels = query_stream.shape
    assert channels == SUB * LANES
    pitch = rows + PAD
    count = lax.axis_size("seq")
    tails = jnp.stack([query_stream[rows - 2 :], key_stream[rows - 2 :], value_stream[rows - 2 :]])
    border = lax.ppermute(tails, "seq", [(j, j + 1) for j in range(count - 1)])
    rate = decay_rate.T.reshape(MODES, SUB, LANES)
    residue = residues.T.reshape(MODES, SUB, LANES)
    params = pltpu.CompilerParams(vmem_limit_bytes=VMEM_LIMIT)
    state, gated = pl.pallas_call(
        state_kernel,
        out_shape=(
            jax.ShapeDtypeStruct((MODES, SUB, LANES), F32),
            jax.ShapeDtypeStruct((SUB * pitch, LANES), F32),
        ),
        in_specs=whole(5),
        out_specs=tuple(whole(2)),
        scratch_shapes=[pltpu.VMEM((pitch, LANES), F32)] * 2,
        compiler_params=params,
    )(border, key_stream, value_stream, short_filter, rate)
    local, query = pl.pallas_call(
        local_kernel,
        out_shape=(jax.ShapeDtypeStruct((rows, channels), F32),) * 2,
        in_specs=whole(7),
        out_specs=tuple(whole(2)),
        scratch_shapes=[pltpu.VMEM((pitch, LANES), F32), pltpu.VMEM((SUB * pitch, LANES), F32)],
        compiler_params=params,
    )(border, query_stream, gated, short_filter, rate, residue, skip_bias[None])
    start = scan_states(state, rate, float(rows))
    mixed_in = pl.pallas_call(
        mix_kernel,
        out_shape=jax.ShapeDtypeStruct((rows, channels), BF16),
        in_specs=whole(5),
        out_specs=whole(1)[0],
        compiler_params=params,
    )(local, query, start, rate, residue)
    parts = lax.axis_size("chan")
    mine = lax.axis_index("chan")
    piece = rows // parts
    partial = jnp.dot(mixed_in, out_weight, preferred_element_type=F32)
    blocks = partial.astype(BF16).reshape(parts, piece, -1)
    summed = lax.dynamic_slice_in_dim(partial, mine * piece, piece, 0)
    for step in (2, 3, 1):
        block = lax.dynamic_index_in_dim(blocks, mine ^ step, 0, False)
        summed = summed + lax.ppermute(block, "chan", [(j, j ^ step) for j in range(parts)]).astype(F32)
    return summed.astype(BF16)


def solution(mesh):
    return jax.shard_map(
        on_device,
        mesh=mesh,
        in_specs=(
            P("seq", "chan"),
            P("seq", "chan"),
            P("seq", "chan"),
            P(None, None, "chan"),
            P("chan", None),
            P("chan", None),
            P("chan"),
            P("chan", None),
        ),
        out_specs=P(("seq", "chan"), None),
        check_vma=False,
    )
```

time: 657 us -> 105 us (0.16); the launches traced: 648 us -> 104 us
  waiting for transfers between devices: 383 us -> 51.6 us
  matrix products: 69.5 us -> 7.66 us
  local copies, waits for them, and re-layouts: 70.3 us -> 8.72 us
  blocking collectives: 36.9 us -> 0 us
  starting transfers between devices: 59.2 us -> 26.6 us
  between operations: 14.1 us -> 0.14 us
  other arithmetic: 15.3 us -> 2.64 us
  Pallas kernels: 0 us -> 6.61 us
    all_to_all x8 -> x0, waiting for transfers between devices: 305 us -> none  [the longest x1 51.3 us: transform_path(): lax.all_to_all(back_imag, 'seq', split_axis=1, concat_axis=0, tiled=True)]
    reduce_scatter x1 -> x0, waiting for transfers between devices: 77 us -> none  [on_device(): lax.psum_scatter(jnp.dot(mixed_in, out_weight, preferred_element_type=jnp...]
    dot_general x19 -> x1, matrix products: 69.5 us -> 7.66 us  [on_device(): partial = jnp.dot(mixed_in, out_weight, preferred_element_type=F32)]
    all_to_all x8 -> x0, starting transfers between devices: 57.1 us -> none  [the longest x1 13.8 us: transform_path(): lax.all_to_all(kernel[None], 'seq', split_axis=1, concat_axis=0, tiled=True)]
    ppermute x1 -> x12, waiting for transfers between devices: 0.74 us -> 51.6 us  [the longest x3 41.8 us: on_device(): lax.ppermute(block, 'chan', [(j, j ^ step) for j in range(parts)])]
    all_to_all x14 -> x0, local copies, waits for them, and re-layouts: 44.4 us -> none  [the longest x2 8.94 us: transform_path(): lax.all_to_all(signal_real, 'seq', split_axis=0, concat_axis=1, tiled=True)]
    all_to_all x1 -> x0, blocking collectives: 36.9 us -> none  [transform_path(): lax.all_to_all(long_term, 'seq', split_axis=0, concat_axis=1, tiled=True)[0]]
    ppermute x1 -> x12, starting transfers between devices: 1.96 us -> 26.6 us  [the longest x8 21.2 us: scan_states(): lax.ppermute(total.astype(BF16), 'seq', [(j, j ^ width * s) for j in rang...]
  transfers between devices with their start and end apart: 10 -> 12, of which waited for: 10 -> 8; matrix products, arithmetic and copies ran while one was open for 10% -> 2% of each run, Pallas kernels for 0% -> 3%
where the time goes in v1:
time: 105 us; the launch traced here: 104 us
  waiting for transfers between devices  51.6 us (49%)
  starting transfers between devices  26.6 us (25%)
  local copies, waits for them, and re-layouts  8.72 us (8%)
  matrix products  7.66 us (7%)
  Pallas kernels  6.61 us (6%)
  other arithmetic  2.64 us (3%)
    ppermute x3, waiting for transfers between devices, on_device(): lax.ppermute(block, 'chan', [(j, j ^ step) for j in range(parts)])  41.8 us
    ppermute x8, starting transfers between devices, scan_states(): lax.ppermute(total.astype(BF16), 'seq', [(j, j ^ width * s) for j in rang...  21.2 us
    ppermute x8, waiting for transfers between devices, scan_states(): lax.ppermute(total.astype(BF16), 'seq', [(j, j ^ width * s) for j in rang...  9.79 us
    dot_general x1, matrix products, on_device(): partial = jnp.dot(mixed_in, out_weight, preferred_element_type=F32)  7.66 us
    unnamed x14, local copies, waits for them, and re-layouts  7.11 us
    ppermute x3, starting transfers between devices, on_device(): lax.ppermute(block, 'chan', [(j, j ^ step) for j in range(parts)])  3.58 us
    pallas_call x1, Pallas kernels, on_device(): pl.pallas_call(local_kernel, out_shape=(jax.ShapeDtypeStruct((rows, chann...  3.22 us
    convert_element_type x1, other arithmetic, on_device(): return summed.astype(BF16)  2.29 us
  transfers between devices with their start and end apart: 12, of which 8 were waited for; matrix products, arithmetic and copies ran while one was open for 2% of the time, Pallas kernels for 3%

profile of v1, /device:TPU:32, one launch (start us, length us, event | category | flops | bytes accessed | tf_op | source)
XLA Modules:
  0.0 103.9 jit_solution(9008250809369829485)
XLA Ops:
  1.5 1.7 %collective-permute-start = (bf16[3,2,1024]{2,1,0:T(2,128)(2,1)S(1)}, bf16[3,2,1024]{2,1,0:T(2,128)(2,1)S(1)}, u32[]{:S(2)}, u32[]{:S(2)}) collective-permute-start(bf16[3,2,1024]{2,1,0:T(2,128)(2,1)S(1)} %pad_maximum_fusion), channel_id=1, source_target_pairs={{0,4},{4,8},{8,12},{12,16},{16,20},{20,24},{24,28},{28,32},{32,36}... | collective-permute-start | bytes 36872 | tf_op jit(solution)/shard_map/ppermute | solution.py:153
  4.1 1.0 copy-done.1
  5.2 1.0 %copy-done.2 = bf16[256,1024]{1,0:T(8,128)(2,1)S(1)} copy-done((bf16[256,1024]{1,0:T(8,128)(2,1)S(1)}, bf16[256,1024]{1,0:T(8,128)(2,1)}, u32[]{:S(2)}) %copy-start.2) | copy-done | bytes 524312
  7.0 2.0 %shard_map.82 = (f32[16,8,128]{2,1,0:T(8,128)S(1)}, f32[2112,128]{1,0:T(8,128)S(1)}) custom-call(bf16[3,2,1024]{2,1,0:T(2,128)(2,1)S(1)} %collective-permute-done.border_ref, bf16[256,1024]{1,0:T(8,128)(2,1)S(1)} %copy-done.2, bf16[256,1024]{1,0:T(8,128)(2,1)S(1)} %copy-done.1, f32[3,3,1024]{2,1,0:T(4,128)S(1)} %copy-done.3, f32[16,8,128]{2,1,0:T(8,128)S(1)} %bitcast.27), custom_call_target="tpu_custom_call" | custom-call | tf_op jit(solution)/shard_map/pallas_call | solution.py:157
  9.1 1.9 %collective-permute-start.1 = (bf16[16,8,128]{2,1,0:T(8,128)(2,1)S(1)}, bf16[16,8,128]{2,1,0:T(8,128)(2,1)S(1)}, u32[]{:S(2)}, u32[]{:S(2)}) collective-permute-start(bf16[16,8,128]{2,1,0:T(8,128)(2,1)S(1)} %convert_element_type.127), channel_id=1, source_target_pairs={{0,4},{4,0},{8,12},{12,8},{16,20},{20,16},{24,28},{28,24},{32,36},... | collective-permute-start | bytes 98312 | tf_op jit(solution)/shard_map/ppermute | solution.py:127
  11.9 4.0 %collective-permute-start.4 = (bf16[16,8,128]{2,1,0:T(8,128)(2,1)S(1)}, bf16[16,8,128]{2,1,0:T(8,128)(2,1)S(1)}, u32[]{:S(2)}, u32[]{:S(2)}) collective-permute-start(bf16[16,8,128]{2,1,0:T(8,128)(2,1)S(1)} %fusion.15), channel_id=1, source_target_pairs={{0,24},{4,28},{8,16},{12,20},{16,8},{20,12},{24,0},{28,4},{32,56},... | collective-permute-start | bytes 98312 | tf_op jit(solution)/shard_map/ppermute | solution.py:127
  16.9 0.9 collective-permute-done.4
  17.8 3.5 %collective-permute-done.3 = bf16[16,8,128]{2,1,0:T(8,128)(2,1)S(1)} collective-permute-done((bf16[16,8,128]{2,1,0:T(8,128)(2,1)S(1)}, bf16[16,8,128]{2,1,0:T(8,128)(2,1)S(1)}, u32[]{:S(2)}, u32[]{:S(2)}) %collective-permute-start.3) | collective-permute-done | bytes 32800 | tf_op jit(solution)/shard_map/ppermute | solution.py:127
  21.4 6.2 %collective-permute-start.7 = (bf16[16,8,128]{2,1,0:T(8,128)(2,1)S(1)}, bf16[16,8,128]{2,1,0:T(8,128)(2,1)S(1)}, u32[]{:S(2)}, u32[]{:S(2)}) collective-permute-start(bf16[16,8,128]{2,1,0:T(8,128)(2,1)S(1)} %get-tuple-element.13), channel_id=1, source_target_pairs={{0,96},{4,100},{8,104},{12,108},{16,112},{20,116},{24,120},{28,124... | collective-permute-start | bytes 98312 | tf_op jit(solution)/shard_map/ppermute | solution.py:127
  27.7 1.0 collective-permute-start.5
  28.6 0.9 collective-permute-done.7
  29.5 3.5 %collective-permute-done.6 = bf16[16,8,128]{2,1,0:T(8,128)(2,1)S(1)} collective-permute-done((bf16[16,8,128]{2,1,0:T(8,128)(2,1)S(1)}, bf16[16,8,128]{2,1,0:T(8,128)(2,1)S(1)}, u32[]{:S(2)}, u32[]{:S(2)}) %collective-permute-start.6) | collective-permute-done | bytes 32800 | tf_op jit(solution)/shard_map/ppermute | solution.py:127
  33.1 7.1 %collective-permute-start.8 = (bf16[16,8,128]{2,1,0:T(8,128)(2,1)S(1)}, bf16[16,8,128]{2,1,0:T(8,128)(2,1)S(1)}, u32[]{:S(2)}, u32[]{:S(2)}) collective-permute-start(bf16[16,8,128]{2,1,0:T(8,128)(2,1)S(1)} %fusion.14), channel_id=1, source_target_pairs={{0,128},{4,132},{8,136},{12,140},{16,144},{20,148},{24,152},{28,15... | collective-permute-start | bytes 98312 | tf_op jit(solution)/shard_map/ppermute | solution.py:127
  41.2 1.0 copy-done
  43.7 3.2 %shard_map.83 = (f32[256,1024]{1,0:T(8,128)S(1)}, f32[256,1024]{1,0:T(8,128)S(1)}) custom-call(bf16[3,2,1024]{2,1,0:T(2,128)(2,1)S(1)} %collective-permute-done.border_ref, bf16[256,1024]{1,0:T(8,128)(2,1)S(1)} %copy-done, f32[2112,128]{1,0:T(8,128)S(1)} %get-tuple-element.9.gated_ref, f32[3,3,1024]{2,1,0:T(4,128)S(1)} %copy-done.4, ...), custom_call_target="tpu_custom_call" | custom-call | tf_op jit(solution)/shard_map/pallas_call | solution.py:168
  47.1 1.4 %shard_map.84 = bf16[256,1024]{1,0:T(8,128)(2,1)S(1)} custom-call(f32[256,1024]{1,0:T(8,128)S(1)} %get-tuple-element.10.local_ref, f32[256,1024]{1,0:T(8,128)S(1)} %get-tuple-element.11.query_ref, f32[16,8,128]{2,1,0:T(8,128)S(1)} %fusion.6.start_ref, f32[16,8,128]{2,1,0:T(8,128)S(1)} %bitcast.29, f32[16,8,128]{2,1,0:T(8,128)S(1)} %bitcast.31), custom_call_target="tpu_custom_call" | custom-call | tf_op jit(solution)/shard_map/pallas_call | solution.py:177
  48.4 7.7 %fusion.18 = (bf16[256,4096]{1,0:T(8,128)(2,1)S(1)}, f32[256,4096]{1,0:T(8,128)}) fusion(bf16[256,1024]{1,0:T(8,128)(2,1)S(1)} %shard_map.84, bf16[1024,4096]{1,0:T(8,128)(2,1)} %param.15), kind=kOutput, calls=%fused_computation.39 | convolution fusion | flops 2148532224 | bytes 15204352 | tf_op jit(solution)/shard_map/dot_general | solution.py:187
  56.3 1.6 %collective-permute-start.9 = (bf16[64,4096]{1,0:T(8,128)(2,1)S(1)}, bf16[64,4096]{1,0:T(8,128)(2,1)S(1)}, u32[]{:S(2)}, u32[]{:S(2)}) collective-permute-start(bf16[64,4096]{1,0:T(8,128)(2,1)S(1)} %get-tuple-element.15), channel_id=1, source_target_pairs={{0,2},{1,3},{2,0},{3,1},{4,6},{5,7},{6,4},{7,5},{8,10},{9,11},{10,... | collective-permute-start | bytes 1572872 | tf_op jit(solution)/shard_map/ppermute | solution.py:192
  57.8 1.0 collective-permute-start.11
  58.8 1.0 collective-permute-start.10
  59.8 21.8 %collective-permute-done.9 = bf16[64,4096]{1,0:T(8,128)(2,1)S(1)} collective-permute-done((bf16[64,4096]{1,0:T(8,128)(2,1)S(1)}, bf16[64,4096]{1,0:T(8,128)(2,1)S(1)}, u32[]{:S(2)}, u32[]{:S(2)}) %collective-permute-start.9) | collective-permute-done | bytes 524320 | tf_op jit(solution)/shard_map/ppermute | solution.py:192
  81.6 1.3 %collective-permute-done.11 = bf16[64,4096]{1,0:T(8,128)(2,1)S(1)} collective-permute-done((bf16[64,4096]{1,0:T(8,128)(2,1)S(1)}, bf16[64,4096]{1,0:T(8,128)(2,1)S(1)}, u32[]{:S(2)}, u32[]{:S(2)}) %collective-permute-start.11) | collective-permute-done | bytes 524320 | tf_op jit(solution)/shard_map/ppermute | solution.py:192
  82.9 18.7 %collective-permute-done.10 = bf16[64,4096]{1,0:T(8,128)(2,1)S(1)} collective-permute-done((bf16[64,4096]{1,0:T(8,128)(2,1)S(1)}, bf16[64,4096]{1,0:T(8,128)(2,1)S(1)}, u32[]{:S(2)}, u32[]{:S(2)}) %collective-permute-start.10) | collective-permute-done | bytes 524320 | tf_op jit(solution)/shard_map/ppermute | solution.py:192
  101.6 2.3 %add_convert_fusion = bf16[64,4096]{1,0:T(8,128)(2,1)} fusion(bf16[64,4096]{1,0:T(8,128)(2,1)S(1)} %collective-permute-done.11, bf16[64,4096]{1,0:T(8,128)(2,1)S(1)} %collective-permute-done.10, bf16[64,4096]{1,0:T(8,128)(2,1)S(1)} %collective-permute-done.9, f32[256,4096]{1,0:T(8,128)} %get-tuple-element.19, s32[]{:T(128)S(6)} %select_n.130), kind=kLoop, calls=%fused_computation | loop fusion | flops 1835008 | bytes 3145732 | tf_op jit(solution)/shard_map/convert_element_type | solution.py:193
  (28 shorter events, 7.8 us)
Async XLA Ops:
  1.5 2.6 %collective-permute-start = (bf16[3,2,1024]{2,1,0:T(2,128)(2,1)S(1)}, bf16[3,2,1024]{2,1,0:T(2,128)(2,1)S(1)}, u32[]{:S(2)}, u32[]{:S(2)}) collective-permute-start(bf16[3,2,1024]{2,1,0:T(2,128)(2,1)S(1)} %pad_maximum_fusion), channel_id=1, source_target_pairs={{0,4},{4,8},{8,12},{12,16},{16,20},{20,24},{24,28},{28,32},{32,36}... | collective-permute-start | bytes 36872 | tf_op jit(solution)/shard_map/ppermute | solution.py:153
  4.1 1.0 %copy-start.1 = (bf16[256,1024]{1,0:T(8,128)(2,1)S(1)}, bf16[256,1024]{1,0:T(8,128)(2,1)}, u32[]{:S(2)}) copy-start(bf16[256,1024]{1,0:T(8,128)(2,1)} %value_ref.1) | copy-start | bytes 1572868
  5.2 1.0 %copy-start.2 = (bf16[256,1024]{1,0:T(8,128)(2,1)S(1)}, bf16[256,1024]{1,0:T(8,128)(2,1)}, u32[]{:S(2)}) copy-start(bf16[256,1024]{1,0:T(8,128)(2,1)} %key_ref.1) | copy-start | bytes 1572868
  6.2 0.8 copy-start.3
  9.1 2.8 %collective-permute-start.1 = (bf16[16,8,128]{2,1,0:T(8,128)(2,1)S(1)}, bf16[16,8,128]{2,1,0:T(8,128)(2,1)S(1)}, u32[]{:S(2)}, u32[]{:S(2)}) collective-permute-start(bf16[16,8,128]{2,1,0:T(8,128)(2,1)S(1)} %convert_element_type.127), channel_id=1, source_target_pairs={{0,4},{4,0},{8,12},{12,8},{16,20},{20,16},{24,28},{28,24},{32,36},... | collective-permute-start | bytes 98312 | tf_op jit(solution)/shard_map/ppermute | solution.py:127
  11.9 5.9 %collective-permute-start.4 = (bf16[16,8,128]{2,1,0:T(8,128)(2,1)S(1)}, bf16[16,8,128]{2,1,0:T(8,128)(2,1)S(1)}, u32[]{:S(2)}, u32[]{:S(2)}) collective-permute-start(bf16[16,8,128]{2,1,0:T(8,128)(2,1)S(1)} %fusion.15), channel_id=1, source_target_pairs={{0,24},{4,28},{8,16},{12,20},{16,8},{20,12},{24,0},{28,4},{32,56},... | collective-permute-start | bytes 98312 | tf_op jit(solution)/shard_map/ppermute | solution.py:127
  15.9 5.4 %collective-permute-start.3 = (bf16[16,8,128]{2,1,0:T(8,128)(2,1)S(1)}, bf16[16,8,128]{2,1,0:T(8,128)(2,1)S(1)}, u32[]{:S(2)}, u32[]{:S(2)}) collective-permute-start(bf16[16,8,128]{2,1,0:T(8,128)(2,1)S(1)} %fusion.15), channel_id=1, source_target_pairs={{0,16},{4,20},{8,24},{12,28},{16,0},{20,4},{24,8},{28,12},{32,48},... | collective-permute-start | bytes 98312 | tf_op jit(solution)/shard_map/ppermute | solution.py:127
  16.5 4.8 %collective-permute-start.2 = (bf16[16,8,128]{2,1,0:T(8,128)(2,1)S(1)}, bf16[16,8,128]{2,1,0:T(8,128)(2,1)S(1)}, u32[]{:S(2)}, u32[]{:S(2)}) collective-permute-start(bf16[16,8,128]{2,1,0:T(8,128)(2,1)S(1)} %fusion.15), channel_id=1, source_target_pairs={{0,8},{4,12},{8,0},{12,4},{16,24},{20,28},{24,16},{28,20},{32,40},... | collective-permute-start | bytes 98312 | tf_op jit(solution)/shard_map/ppermute | solution.py:127
  21.4 8.1 %collective-permute-start.7 = (bf16[16,8,128]{2,1,0:T(8,128)(2,1)S(1)}, bf16[16,8,128]{2,1,0:T(8,128)(2,1)S(1)}, u32[]{:S(2)}, u32[]{:S(2)}) collective-permute-start(bf16[16,8,128]{2,1,0:T(8,128)(2,1)S(1)} %get-tuple-element.13), channel_id=1, source_target_pairs={{0,96},{4,100},{8,104},{12,108},{16,112},{20,116},{24,120},{28,124... | collective-permute-start | bytes 98312 | tf_op jit(solution)/shard_map/ppermute | solution.py:127
  27.7 5.4 %collective-permute-start.6 = (bf16[16,8,128]{2,1,0:T(8,128)(2,1)S(1)}, bf16[16,8,128]{2,1,0:T(8,128)(2,1)S(1)}, u32[]{:S(2)}, u32[]{:S(2)}) collective-permute-start(bf16[16,8,128]{2,1,0:T(8,128)(2,1)S(1)} %get-tuple-element.13), channel_id=1, source_target_pairs={{0,64},{4,68},{8,72},{12,76},{16,80},{20,84},{24,88},{28,92},{32,9... | collective-permute-start | bytes 98312 | tf_op jit(solution)/shard_map/ppermute | solution.py:127
  27.7 5.4 %collective-permute-start.5 = (bf16[16,8,128]{2,1,0:T(8,128)(2,1)S(1)}, bf16[16,8,128]{2,1,0:T(8,128)(2,1)S(1)}, u32[]{:S(2)}, u32[]{:S(2)}) collective-permute-start(bf16[16,8,128]{2,1,0:T(8,128)(2,1)S(1)} %get-tuple-element.13), channel_id=1, source_target_pairs={{0,32},{4,36},{8,40},{12,44},{16,48},{20,52},{24,56},{28,60},{32,0... | collective-permute-start | bytes 98312 | tf_op jit(solution)/shard_map/ppermute | solution.py:127
  33.1 13.8 %collective-permute-start.8 = (bf16[16,8,128]{2,1,0:T(8,128)(2,1)S(1)}, bf16[16,8,128]{2,1,0:T(8,128)(2,1)S(1)}, u32[]{:S(2)}, u32[]{:S(2)}) collective-permute-start(bf16[16,8,128]{2,1,0:T(8,128)(2,1)S(1)} %fusion.14), channel_id=1, source_target_pairs={{0,128},{4,132},{8,136},{12,140},{16,144},{20,148},{24,152},{28,15... | collective-permute-start | bytes 98312 | tf_op jit(solution)/shard_map/ppermute | solution.py:127
  41.2 1.0 %copy-start = (bf16[256,1024]{1,0:T(8,128)(2,1)S(1)}, bf16[256,1024]{1,0:T(8,128)(2,1)}, u32[]{:S(2)}) copy-start(bf16[256,1024]{1,0:T(8,128)(2,1)} %query_ref.1) | copy-start | bytes 1572868
  42.2 0.8 copy-start.4
  43.0 0.7 copy-start.5
  56.3 25.4 %collective-permute-start.9 = (bf16[64,4096]{1,0:T(8,128)(2,1)S(1)}, bf16[64,4096]{1,0:T(8,128)(2,1)S(1)}, u32[]{:S(2)}, u32[]{:S(2)}) collective-permute-start(bf16[64,4096]{1,0:T(8,128)(2,1)S(1)} %get-tuple-element.15), channel_id=1, source_target_pairs={{0,2},{1,3},{2,0},{3,1},{4,6},{5,7},{6,4},{7,5},{8,10},{9,11},{10,... | collective-permute-start | bytes 1572872 | tf_op jit(solution)/shard_map/ppermute | solution.py:192
  57.8 25.1 %collective-permute-start.11 = (bf16[64,4096]{1,0:T(8,128)(2,1)S(1)}, bf16[64,4096]{1,0:T(8,128)(2,1)S(1)}, u32[]{:S(2)}, u32[]{:S(2)}) collective-permute-start(bf16[64,4096]{1,0:T(8,128)(2,1)S(1)} %get-tuple-element.16), channel_id=1, source_target_pairs={{0,1},{1,0},{2,3},{3,2},{4,5},{5,4},{6,7},{7,6},{8,9},{9,8},{10,11... | collective-permute-start | bytes 1572872 | tf_op jit(solution)/shard_map/ppermute | solution.py:192
  58.8 42.8 %collective-permute-start.10 = (bf16[64,4096]{1,0:T(8,128)(2,1)S(1)}, bf16[64,4096]{1,0:T(8,128)(2,1)S(1)}, u32[]{:S(2)}, u32[]{:S(2)}) collective-permute-start(bf16[64,4096]{1,0:T(8,128)(2,1)S(1)} %get-tuple-element.17), channel_id=1, source_target_pairs={{0,3},{1,2},{2,1},{3,0},{4,7},{5,6},{6,5},{7,4},{8,11},{9,10},{10,... | collective-permute-start | bytes 1572872 | tf_op jit(solution)/shard_map/ppermute | solution.py:192

commit v2 on v1

v2 whole, which is shorter than its diff:
```python
import jax
import jax.numpy as jnp
from jax import lax
from jax.experimental import pallas as pl
from jax.experimental.pallas import tpu as pltpu
from jax.sharding import PartitionSpec as P

MODES = 16
SHORT = 3
F32 = jnp.float32
BF16 = jnp.bfloat16
LANES = 128
SUB = 8
PAD = 8
STATE_ROWS = MODES * SUB
HEADS = 4
TAILS = 6
PAYLOAD = STATE_ROWS + SUB * (HEADS + TAILS)
COLUMN_TILE = 512
CUTS = 4
WEIGHT_CUTS = 8
VMEM_LIMIT = 28 * 1024 * 1024
HBM = pl.BlockSpec(memory_space=pltpu.HBM)
VMEM = pl.BlockSpec(memory_space=pltpu.VMEM)
SMEM = pl.BlockSpec(memory_space=pltpu.SMEM)


def summed(terms):
    terms = list(terms)
    while len(terms) > 1:
        terms = [terms[i] + terms[i + 1] for i in range(0, len(terms), 2)]
    return terms[0]


def short_taps(ext, taps_ref, stream, lanes, count):
    return (
        taps_ref[stream, 0:1, lanes] * ext[PAD : PAD + count, :]
        + taps_ref[stream, 1:2, lanes] * ext[PAD - 1 : PAD - 1 + count, :]
        + taps_ref[stream, 2:3, lanes] * ext[PAD - 2 : PAD - 2 + count, :]
    )


def to_rows(source, target):
    for group in range(SUB):
        target[pl.ds(group, MODES, stride=SUB), :] = source[:, group * LANES : (group + 1) * LANES]


def copies(pairs, sems):
    made = [pltpu.make_async_copy(a, b, sems.at[i]) for i, (a, b) in enumerate(pairs)]
    for one in made:
        one.start()
    return made


def state_kernel(
    query_hbm, key_hbm, value_hbm, taps_hbm, rate_hbm,
    payload_ref, sent_ref, rate_ref, gated_ref, taps_ref,
    key_buf, value_buf, query_buf, taps_buf, rate_buf, ext_key, ext_value, sems,
):
    rows, channels = key_buf.shape
    pitch = rows + PAD
    width = channels // CUTS
    made = copies(
        [(rate_hbm, rate_buf), (taps_hbm, taps_buf)]
        + [
            (hbm.at[:, pl.ds(part * width, width)], buf.at[:, pl.ds(part * width, width)])
            for part in range(CUTS)
            for hbm, buf in ((key_hbm, key_buf), (value_hbm, value_buf))
        ]
        + [(query_hbm.at[pl.ds(rows - 16, 16), :], query_buf)],
        sems,
    )
    ext_key[0:PAD, :] = jnp.zeros((PAD, LANES), F32)
    ext_value[0:PAD, :] = jnp.zeros((PAD, LANES), F32)
    made[0].wait()
    to_rows(rate_buf, rate_ref)
    made[1].wait()
    for group in range(SUB):
        if group % (SUB // CUTS) == 0:
            part = group // (SUB // CUTS)
            made[2 + 2 * part].wait()
            made[3 + 2 * part].wait()
        lanes = slice(group * LANES, (group + 1) * LANES)
        ext_key[PAD : PAD + rows, :] = key_buf[:, lanes].astype(F32)
        ext_value[PAD : PAD + rows, :] = value_buf[:, lanes].astype(F32)
        gated = short_taps(ext_key, taps_buf, 1, lanes, rows) * short_taps(ext_value, taps_buf, 2, lanes, rows)
        base = group * pitch
        gated_ref[base : base + rows, :] = gated.astype(BF16).astype(F32)
        gated_ref[base : base + 2, :] = jnp.zeros((2, LANES), F32)
        gated_ref[base + rows : base + pitch, :] = jnp.zeros((PAD, LANES), F32)
        for place, (ext, row) in enumerate(
            ((ext_key, 0), (ext_key, 1), (ext_value, 0), (ext_value, 1))
        ):
            at = STATE_ROWS + place * SUB + group
            payload_ref[at : at + 1, :] = ext[PAD + row : PAD + row + 1, :]
        for place, (ext, row) in enumerate(
            ((ext_key, rows - 2), (ext_key, rows - 1), (ext_value, rows - 2), (ext_value, rows - 1))
        ):
            at = STATE_ROWS + (HEADS + 2 + place) * SUB + group
            payload_ref[at : at + 1, :] = ext[PAD + row : PAD + row + 1, :]
    decay = [jnp.exp(-rate_ref[m * SUB : (m + 1) * SUB, :]) for m in range(MODES)]

    def step(t, carry):
        now = gated_ref[pl.ds(t, SUB, stride=pitch), :]
        return tuple(decay[m] * carry[m] + now for m in range(MODES))

    final = lax.fori_loop(0, rows, step, tuple(jnp.zeros((SUB, LANES), F32) for _ in range(MODES)), unroll=8)
    for m in range(MODES):
        payload_ref[m * SUB : (m + 1) * SUB, :] = final[m]
    made[2 + 2 * CUTS].wait()
    last = query_buf[...].astype(F32)
    for place, row in enumerate((14, 15)):
        for group in range(SUB):
            at = STATE_ROWS + (HEADS + place) * SUB + group
            payload_ref[at : at + 1, :] = last[row : row + 1, group * LANES : (group + 1) * LANES]
    sent_ref[...] = payload_ref[...].astype(BF16)
    for stream in range(3):
        for tap in range(SHORT):
            for group in range(SUB):
                at = (stream * SHORT + tap) * SUB + group
                taps_ref[at : at + 1, :] = taps_buf[stream, tap : tap + 1, group * LANES : (group + 1) * LANES]


def local_kernel(
    query_hbm, residue_hbm, skip_hbm, weight_hbm, gated_ref, rate_ref, taps_ref,
    local_ref, query_ref, residue_ref, weight_ref,
    query_buf, residue_buf, skip_buf, ext, conv, sems,
):
    rows = query_buf.shape[0]
    pitch = rows + PAD
    depth = weight_ref.shape[0] // WEIGHT_CUTS
    made = copies(
        [(residue_hbm, residue_buf), (query_hbm, query_buf), (skip_hbm, skip_buf)]
        + [
            (weight_hbm.at[pl.ds(i * depth, depth), :], weight_ref.at[pl.ds(i * depth, depth), :])
            for i in range(WEIGHT_CUTS)
        ],
        sems,
    )
    decay = [jnp.exp(-rate_ref[m * SUB : (m + 1) * SUB, :]) for m in range(MODES)]
    made[0].wait()
    to_rows(residue_buf, residue_ref)

    def step(t, carry):
        now = gated_ref[pl.ds(t, SUB, stride=pitch), :]
        fresh = tuple(decay[m] * carry[m] + now for m in range(MODES))
        conv[pl.ds(t, SUB, stride=pitch), :] = summed(
            residue_ref[m * SUB : (m + 1) * SUB, :] * fresh[m] for m in range(MODES)
        )
        return fresh

    lax.fori_loop(0, rows, step, tuple(jnp.zeros((SUB, LANES), F32) for _ in range(MODES)), unroll=4)
    made[1].wait()
    made[2].wait()
    ext[0:PAD, :] = jnp.zeros((PAD, LANES), F32)
    for group in range(SUB):
        lanes = slice(group * LANES, (group + 1) * LANES)
        spot = slice(group * pitch, group * pitch + rows)
        local_ref[:, lanes] = conv[spot, :] + skip_buf[group : group + 1, :] * gated_ref[spot, :]
        ext[PAD : PAD + rows, :] = query_buf[:, lanes].astype(F32)
        tap = [taps_ref[p * SUB + group : p * SUB + group + 1, :] for p in range(SHORT)]
        query_ref[:, lanes] = (
            tap[0] * ext[PAD : PAD + rows, :]
            + tap[1] * ext[PAD - 1 : PAD - 1 + rows, :]
            + tap[2] * ext[PAD - 2 : PAD - 2 + rows, :]
        )
    for one in made[3:]:
        one.wait()


def mix_kernel(
    place_ref, local_ref, query_ref, after_ref, fix_ref, rate_ref, residue_ref, weight_ref,
    first_ref, second_ref,
    mixed, coef,
):
    half_rows, depth = mixed.shape
    piece = half_rows // 2
    columns = weight_ref.shape[1]
    base = place_ref[0]
    swap = place_ref[1]
    before = (base - 1).astype(F32)
    coef[...] = residue_ref[...] * after_ref[...] * jnp.exp(-rate_ref[...] * before)
    phase = lax.broadcasted_iota(jnp.int32, (SUB, LANES), 0)
    at_start = base == 0
    row_zero = jnp.logical_and(phase == 0, at_start)
    row_one = jnp.logical_and(phase == 1, at_start)
    zero = jnp.zeros((SUB, LANES), F32)
    for group in range(SUB):
        lanes = slice(group * LANES, (group + 1) * LANES)
        carry, decay = [], []
        for m in range(MODES):
            line = slice(m * SUB + group, m * SUB + group + 1)
            rate = rate_ref[line, :]
            carry.append(jnp.exp(-rate * phase.astype(F32)) * coef[line, :])
            decay.append(jnp.broadcast_to(jnp.exp(-rate * float(SUB)), (SUB, LANES)))

        def fix(i):
            return jnp.broadcast_to(fix_ref[i * SUB + group : i * SUB + group + 1, :], (SUB, LANES))

        for tile in range(0, half_rows, 2 * SUB):
            parts = []
            for inner in range(2):
                offset = tile + inner * SUB
                spot = pl.ds(pl.multiple_of(base + offset, SUB), SUB)
                carried = summed(carry)
                query = query_ref[spot, lanes]
                if offset == 0:
                    carried = jnp.where(row_zero, fix(0), carried) + jnp.where(row_one, fix(1), zero)
                    query = query + jnp.where(row_zero, fix(2), zero) + jnp.where(row_one, fix(3), zero)
                parts.append((local_ref[spot, lanes] + carried) * query)
                carry = [carry[m] * decay[m] for m in range(MODES)]
            block = tile // piece
            row = pl.multiple_of((block ^ swap) * piece + tile % piece, 2 * SUB)
            mixed[pl.ds(row, 2 * SUB), lanes] = jnp.concatenate(parts, axis=0).astype(BF16)
    for i in range(columns // COLUMN_TILE):
        where = slice(i * COLUMN_TILE, (i + 1) * COLUMN_TILE)
        product = jnp.dot(mixed[...], weight_ref[:, where], preferred_element_type=F32)
        first_ref[:, where] = product[:piece].astype(first_ref.dtype)
        second_ref[:, where] = product[piece:].astype(second_ref.dtype)


def scan_states(payload, sent, rate, taps, rows, place, count):
    tap = taps.reshape(3, SHORT, SUB, LANES)

    def head_gated(tail, head):
        def filtered(s, first, second, older, newer):
            return (
                tap[s][0] * first + tap[s][1] * newer + tap[s][2] * older,
                tap[s][0] * second + tap[s][1] * first + tap[s][2] * newer,
            )

        keys = filtered(1, head[0], head[1], tail[2], tail[3])
        values = filtered(2, head[2], head[3], tail[4], tail[5])
        return [(k * v).astype(BF16).astype(F32) for k, v in zip(keys, values, strict=True)]

    def decayed(steps):
        return jnp.exp(-rate * steps)

    def joined(pair):
        return decayed(1.0) * pair[0] + pair[1]

    mine = payload.reshape(-1, SUB, LANES)
    own_head = mine[MODES : MODES + HEADS]
    total, head, tail = mine[:MODES], own_head, mine[MODES + HEADS :]
    start = jnp.zeros_like(total)
    border = jnp.zeros_like(tail)
    bits = (count - 1).bit_length()
    for bit in range(bits):
        width = 1 << bit
        mask = width
        if bit >= 2 and bit % 2 == 0 and bit < bits:
            mask = width | (width >> 1)
        got = lax.ppermute(sent, "seq", [(j, j ^ mask) for j in range(count)])
        theirs = got.reshape(-1, SUB, LANES).astype(F32)
        upper = ((place >> bit) & 1) == 1
        low = place % width
        length = rows * width
        other_total, other_head, other_tail = theirs[:MODES], theirs[MODES : MODES + HEADS], theirs[MODES + HEADS :]
        low_total = jnp.where(upper, other_total, total)
        low_tail = jnp.where(upper, other_tail, tail)
        high_head = jnp.where(upper, head, other_head)
        entry = joined(head_gated(low_tail, high_head))
        gone = (rows * low).astype(F32)
        start = start + jnp.where(
            upper,
            decayed(gone) * other_total
            + jnp.where(low > 0, decayed(jnp.maximum(gone - 2.0, 0.0)) * entry, 0.0),
            0.0,
        )
        border = jnp.where(jnp.logical_and(upper, low == 0), other_tail, border)
        if bit < bits - 1:
            high_total = jnp.where(upper, total, other_total)
            total = decayed(float(length)) * low_total + high_total + decayed(float(length - 2)) * entry
            tail = jnp.where(upper, tail, other_tail)
        head = jnp.where(upper, other_head, head)
        if bit < bits - 1:
            sent = jnp.concatenate([total, head, tail]).reshape(-1, LANES).astype(BF16)
    first = joined(head_gated(jnp.zeros_like(border), head))
    gone = (rows * place).astype(F32)
    start = start + jnp.where(place > 0, decayed(jnp.maximum(gone - 2.0, 0.0)) * first, 0.0)
    return start, border, head_gated(border, own_head), tap


def on_device(query_stream, key_stream, value_stream, short_filter, decay_rate, residues, skip_bias, out_weight):
    rows, channels = query_stream.shape
    assert channels == SUB * LANES
    columns = out_weight.shape[1]
    pitch = rows + PAD
    count = lax.axis_size("seq")
    place = lax.axis_index("seq")
    parts = lax.axis_size("chan")
    mine = lax.axis_index("chan")
    assert parts == 4
    piece = rows // parts
    query_stream, key_stream, value_stream, short_filter, out_weight, rates, residues, skips = (
        pltpu.with_memory_space_constraint(array, pltpu.HBM)
        for array in (
            query_stream, key_stream, value_stream, short_filter, out_weight,
            decay_rate.T, residues.T, skip_bias.reshape(SUB, LANES),
        )
    )
    params = pltpu.CompilerParams(vmem_limit_bytes=VMEM_LIMIT)
    dma = pltpu.SemaphoreType.DMA
    payload, sent, rate, gated, taps = pl.pallas_call(
        state_kernel,
        out_shape=(
            jax.ShapeDtypeStruct((PAYLOAD, LANES), F32),
            jax.ShapeDtypeStruct((PAYLOAD, LANES), BF16),
            jax.ShapeDtypeStruct((STATE_ROWS, LANES), F32),
            jax.ShapeDtypeStruct((SUB * pitch, LANES), F32),
            jax.ShapeDtypeStruct((3 * SHORT * SUB, LANES), F32),
        ),
        in_specs=[HBM] * 5,
        out_specs=(VMEM,) * 5,
        scratch_shapes=[
            pltpu.VMEM((rows, channels), BF16),
            pltpu.VMEM((rows, channels), BF16),
            pltpu.VMEM((16, channels), BF16),
            pltpu.VMEM((3, SHORT, channels), F32),
            pltpu.VMEM((MODES, channels), F32),
            pltpu.VMEM((pitch, LANES), F32),
            pltpu.VMEM((pitch, LANES), F32),
            dma((3 + 2 * CUTS,)),
        ],
        compiler_params=params,
        cost_estimate=pl.CostEstimate(flops=20_000_000, bytes_accessed=3_000_000, transcendentals=0),
    )(query_stream, key_stream, value_stream, short_filter, rates)
    local, query, residue, weight = pl.pallas_call(
        local_kernel,
        out_shape=(
            jax.ShapeDtypeStruct((rows, channels), F32),
            jax.ShapeDtypeStruct((rows, channels), F32),
            jax.ShapeDtypeStruct((STATE_ROWS, LANES), F32),
            jax.ShapeDtypeStruct(out_weight.shape, BF16),
        ),
        in_specs=[HBM] * 4 + [VMEM] * 3,
        out_specs=(VMEM,) * 4,
        scratch_shapes=[
            pltpu.VMEM((rows, channels), BF16),
            pltpu.VMEM((MODES, channels), F32),
            pltpu.VMEM((SUB, LANES), F32),
            pltpu.VMEM((pitch, LANES), F32),
            pltpu.VMEM((SUB * pitch, LANES), F32),
            dma((3 + WEIGHT_CUTS,)),
        ],
        compiler_params=params,
        cost_estimate=pl.CostEstimate(flops=20_000_000, bytes_accessed=6_000_000, transcendentals=0),
    )(query_stream, residues, skips, out_weight, gated, rate, taps)
    rate_rows = rate.reshape(MODES, SUB, LANES)
    residue_rows = residue.reshape(MODES, SUB, LANES)
    start, border, gates, tap = scan_states(payload, sent, rate_rows, taps, rows, place, count)
    skip = skip_bias.reshape(SUB, LANES)
    after_zero = jnp.exp(-rate_rows) * start + gates[0]
    after_one = jnp.exp(-rate_rows) * after_zero + gates[1]
    fixes = jnp.concatenate(
        [
            jnp.sum(residue_rows * after_zero, axis=0) + skip * gates[0],
            skip * gates[1],
            tap[0][1] * border[1] + tap[0][2] * border[0],
            tap[0][2] * border[1],
        ]
    )

    def mix(half, swap, second_type):
        return pl.pallas_call(
            mix_kernel,
            out_shape=(
                jax.ShapeDtypeStruct((piece, columns), BF16),
                jax.ShapeDtypeStruct((piece, columns), second_type),
            ),
            in_specs=[SMEM] + [VMEM] * 7,
            out_specs=(VMEM,) * 2,
            scratch_shapes=[
                pltpu.VMEM((2 * piece, channels), BF16),
                pltpu.VMEM((STATE_ROWS, LANES), F32),
            ],
            compiler_params=params,
            cost_estimate=pl.CostEstimate(flops=1_000_000_000, bytes_accessed=10_000_000, transcendentals=0),
        )(
            jnp.stack([half * 2 * piece, swap]).astype(jnp.int32),
            local, query, after_one.reshape(STATE_ROWS, LANES), fixes, rate, residue, weight,
        )

    own_half, odd = mine // 2, mine % 2
    across_two, across_three = mix(1 - own_half, odd, BF16)
    beside, own = mix(own_half, 1 - odd, F32)

    def sent_by(block, step):
        return lax.ppermute(block, "chan", [(j, j ^ step) for j in range(parts)]).astype(F32)

    total = own + sent_by(across_two, 2) + sent_by(across_three, 3) + sent_by(beside, 1)
    return total.astype(BF16)


def solution(mesh):
    return jax.shard_map(
        on_device,
        mesh=mesh,
        in_specs=(
            P("seq", "chan"),
            P("seq", "chan"),
            P("seq", "chan"),
            P(None, None, "chan"),
            P("chan", None),
            P("chan", None),
            P("chan"),
            P("chan", None),
        ),
        out_specs=P(("seq", "chan"), None),
        check_vma=False,
    )
```

time: 105 us -> 82.9 us (0.79)
  local copies, waits for them, and re-layouts: 8.72 us -> 0.01 us
  matrix products: 7.66 us -> 0 us
  starting transfers between devices: 26.6 us -> 20.2 us
  Pallas kernels: 6.61 us -> 12.5 us
  waiting for transfers between devices: 51.6 us -> 47.5 us
    dot_general x1 -> x0, matrix products: 7.66 us -> none  [on_device(): partial = jnp.dot(mixed_in, out_weight, preferred_element_type=F32)]
    unnamed x14 -> x2, local copies, waits for them, and re-layouts: 7.11 us -> 0.01 us
    ppermute x12 -> x9, starting transfers between devices: 26.6 us -> 20.2 us  [the longest x6 15.7 us: scan_states(): got = lax.ppermute(sent, 'seq', [(j, j ^ mask) for j in range(count)])]
    pallas_call x2 -> x3, Pallas kernels: 3.39 us -> 8.39 us  [the longest x2 5.14 us: mix(): pl.pallas_call(mix_kernel, out_shape=(jax.ShapeDtypeStruct((piece, column...]
    ppermute x12 -> x9, waiting for transfers between devices: 51.6 us -> 47.5 us  [the longest x3 36.3 us: sent_by(): lax.ppermute(block, 'chan', [(j, j ^ step) for j in range(parts)])]
    another operation x2 -> x0, local copies, waits for them, and re-layouts: 1.47 us -> none  [on_device(): jnp.stack([query_stream[rows - 2:], key_stream[rows - 2:], value_stream[r...]
    convert_element_type x5 -> x26, other arithmetic: 2.47 us -> 1.31 us  [the longest x1 1.06 us: on_device(): return total.astype(BF16)]
  transfers between devices with their start and end apart: 12 -> 9, of which waited for: 8 -> 7; matrix products, arithmetic and copies ran while one was open for 2% -> 0% of each run, Pallas kernels for 3% -> 8%
where the time goes in v2:
time: 82.9 us; the launch traced here: 82.8 us
  waiting for transfers between devices  47.5 us (57%)
  starting transfers between devices  20.2 us (24%)
  Pallas kernels  12.5 us (15%)
  other arithmetic  2.19 us (3%)
    ppermute x3, waiting for transfers between devices, sent_by(): lax.ppermute(block, 'chan', [(j, j ^ step) for j in range(parts)])  36.3 us
    ppermute x6, starting transfers between devices, scan_states(): got = lax.ppermute(sent, 'seq', [(j, j ^ mask) for j in range(count)])  15.7 us
    ppermute x6, waiting for transfers between devices, scan_states(): got = lax.ppermute(sent, 'seq', [(j, j ^ mask) for j in range(count)])  11.3 us
    pallas_call x2, Pallas kernels, mix(): pl.pallas_call(mix_kernel, out_shape=(jax.ShapeDtypeStruct((piece, column...  5.14 us
    ppermute x3, starting transfers between devices, sent_by(): lax.ppermute(block, 'chan', [(j, j ^ step) for j in range(parts)])  4.56 us
    pallas_call x1, Pallas kernels, on_device(): pl.pallas_call(local_kernel, out_shape=(jax.ShapeDtypeStruct((rows, chann...  4.11 us
    pallas_call x1, Pallas kernels, on_device(): pl.pallas_call(state_kernel, out_shape=(jax.ShapeDtypeStruct((PAYLOAD, LA...  3.25 us
  transfers between devices with their start and end apart: 9, of which 7 were waited for; matrix products, arithmetic and copies ran while one was open for 0% of the time, Pallas kernels for 8%

profile of v2, /device:TPU:32, one launch (start us, length us, event | category | flops | bytes accessed | tf_op | source)
XLA Modules:
  0.0 82.8 jit_solution(10200445898861320074)
XLA Ops:
  0.0 3.2 %shard_map.82 = (f32[208,128]{1,0:T(8,128)S(1)}, bf16[208,128]{1,0:T(8,128)(2,1)S(1)}, f32[128,128]{1,0:T(8,128)S(1)}, f32[2112,128]{1,0:T(8,128)S(1)}, f32[72,128]{1,0:T(8,128)S(1)}) custom-call(bf16[256,1024]{1,0:T(8,128)(2,1)} %query_hbm.3, bf16[256,1024]{1,0:T(8,128)(2,1)} %key_hbm.1, bf16[256,1024]{1,0:T(8,128)(2,1)} %value_hbm.1, ...), custom_call_target="tpu_custom_call" | custom-call | flops 20000000 | bytes 3000000 | tf_op jit(solution)/shard_map/pallas_call | solution.py:304
  3.3 0.1 collective-permute-start
  3.4 1.2 %collective-permute-done = bf16[208,128]{1,0:T(8,128)(2,1)S(1)} collective-permute-done((bf16[208,128]{1,0:T(8,128)(2,1)S(1)}, bf16[208,128]{1,0:T(8,128)(2,1)S(1)}, u32[]{:S(2)}, u32[]{:S(2)}) %collective-permute-start) | collective-permute-done | bytes 53280 | tf_op jit(solution)/shard_map/ppermute | solution.py:253
  4.7 1.7 %collective-permute-start.1 = (bf16[208,128]{1,0:T(8,128)(2,1)S(1)}, bf16[208,128]{1,0:T(8,128)(2,1)S(1)}, u32[]{:S(2)}, u32[]{:S(2)}) collective-permute-start(bf16[208,128]{1,0:T(8,128)(2,1)S(1)} %maximum_bitcast_fusion), channel_id=1, source_target_pairs={{0,8},{4,12},{8,0},{12,4},{16,24},{20,28},{24,16},{28,20},{32,40},... | collective-permute-start | bytes 159752 | tf_op jit(solution)/shard_map/ppermute | solution.py:253
  6.4 2.6 %collective-permute-done.1 = bf16[208,128]{1,0:T(8,128)(2,1)S(1)} collective-permute-done((bf16[208,128]{1,0:T(8,128)(2,1)S(1)}, bf16[208,128]{1,0:T(8,128)(2,1)S(1)}, u32[]{:S(2)}, u32[]{:S(2)}) %collective-permute-start.1) | collective-permute-done | bytes 53280 | tf_op jit(solution)/shard_map/ppermute | solution.py:253
  9.0 0.1 fusion.138
  9.1 3.1 %collective-permute-start.2 = (bf16[208,128]{1,0:T(8,128)(2,1)S(1)}, bf16[208,128]{1,0:T(8,128)(2,1)S(1)}, u32[]{:S(2)}, u32[]{:S(2)}) collective-permute-start(bf16[208,128]{1,0:T(8,128)(2,1)S(1)} %maximum_bitcast_fusion.1), channel_id=1, source_target_pairs={{0,24},{4,28},{8,16},{12,20},{16,8},{20,12},{24,0},{28,4},{32,56},... | collective-permute-start | bytes 159752 | tf_op jit(solution)/shard_map/ppermute | solution.py:253
  12.2 2.3 %collective-permute-done.2 = bf16[208,128]{1,0:T(8,128)(2,1)S(1)} collective-permute-done((bf16[208,128]{1,0:T(8,128)(2,1)S(1)}, bf16[208,128]{1,0:T(8,128)(2,1)S(1)}, u32[]{:S(2)}, u32[]{:S(2)}) %collective-permute-start.2) | collective-permute-done | bytes 53280 | tf_op jit(solution)/shard_map/ppermute | solution.py:253
  14.7 1.6 %collective-permute-start.3 = (bf16[208,128]{1,0:T(8,128)(2,1)S(1)}, bf16[208,128]{1,0:T(8,128)(2,1)S(1)}, u32[]{:S(2)}, u32[]{:S(2)}) collective-permute-start(bf16[208,128]{1,0:T(8,128)(2,1)S(1)} %maximum_bitcast_fusion.2), channel_id=1, source_target_pairs={{0,32},{4,36},{8,40},{12,44},{16,48},{20,52},{24,56},{28,60},{32,0... | collective-permute-start | bytes 159752 | tf_op jit(solution)/shard_map/ppermute | solution.py:253
  16.3 2.6 %collective-permute-done.3 = bf16[208,128]{1,0:T(8,128)(2,1)S(1)} collective-permute-done((bf16[208,128]{1,0:T(8,128)(2,1)S(1)}, bf16[208,128]{1,0:T(8,128)(2,1)S(1)}, u32[]{:S(2)}, u32[]{:S(2)}) %collective-permute-start.3) | collective-permute-done | bytes 53280 | tf_op jit(solution)/shard_map/ppermute | solution.py:253
  19.0 0.1 fusion.136
  19.1 2.8 %collective-permute-start.4 = (bf16[208,128]{1,0:T(8,128)(2,1)S(1)}, bf16[208,128]{1,0:T(8,128)(2,1)S(1)}, u32[]{:S(2)}, u32[]{:S(2)}) collective-permute-start(bf16[208,128]{1,0:T(8,128)(2,1)S(1)} %maximum_bitcast_fusion.3), channel_id=1, source_target_pairs={{0,96},{4,100},{8,104},{12,108},{16,112},{20,116},{24,120},{28,124... | collective-permute-start | bytes 159752 | tf_op jit(solution)/shard_map/ppermute | solution.py:253
  22.0 2.5 %collective-permute-done.4 = bf16[208,128]{1,0:T(8,128)(2,1)S(1)} collective-permute-done((bf16[208,128]{1,0:T(8,128)(2,1)S(1)}, bf16[208,128]{1,0:T(8,128)(2,1)S(1)}, u32[]{:S(2)}, u32[]{:S(2)}) %collective-permute-start.4) | collective-permute-done | bytes 53280 | tf_op jit(solution)/shard_map/ppermute | solution.py:253
  24.7 6.4 %collective-permute-start.5 = (bf16[208,128]{1,0:T(8,128)(2,1)S(1)}, bf16[208,128]{1,0:T(8,128)(2,1)S(1)}, u32[]{:S(2)}, u32[]{:S(2)}) collective-permute-start(bf16[208,128]{1,0:T(8,128)(2,1)S(1)} %maximum_bitcast_fusion.4), channel_id=1, source_target_pairs={{0,128},{4,132},{8,136},{12,140},{16,144},{20,148},{24,152},{28,15... | collective-permute-start | bytes 159752 | tf_op jit(solution)/shard_map/ppermute | solution.py:253
  31.2 4.1 %shard_map.83 = (f32[256,1024]{1,0:T(8,128)S(1)}, f32[256,1024]{1,0:T(8,128)S(1)}, f32[128,128]{1,0:T(8,128)S(1)}, bf16[1024,4096]{1,0:T(8,128)(2,1)S(1)}) custom-call(bf16[256,1024]{1,0:T(8,128)(2,1)} %query_hbm.3, f32[16,1024]{1,0:T(8,128)} %bitcast.317, f32[8,128]{1,0:T(8,128)} %bitcast.319, bf16[1024,4096]{1,0:T(8,128)(2,1)} %weight_hbm.1, ...), custom_call_target="tpu_custom_call" | custom-call | flops 20000000 | bytes 6000000 | tf_op jit(solution)/shard_map/pallas_call | solution.py:328
  35.5 0.2 fusion.7
  35.8 2.6 %shard_map.85 = (bf16[64,4096]{1,0:T(8,128)(2,1)S(1)}, bf16[64,4096]{1,0:T(8,128)(2,1)S(1)}) custom-call(s32[2]{0:T(128)S(1)} %pad_add_fusion.1.place_ref, f32[256,1024]{1,0:T(8,128)S(1)} %get-tuple-element.21.local_ref, f32[256,1024]{1,0:T(8,128)S(1)} %get-tuple-element.22.query_ref, f32[128,128]{1,0:T(8,128)S(1)} %fusion.44.after_ref, ...), custom_call_target="tpu_custom_call" | custom-call | flops 1000000000 | bytes 10000000 | tf_op jit(solution)/shard_map/pallas_call | solution.py:365
  38.3 1.6 %collective-permute-start.6 = (bf16[64,4096]{1,0:T(8,128)(2,1)S(1)}, bf16[64,4096]{1,0:T(8,128)(2,1)S(1)}, u32[]{:S(2)}, u32[]{:S(2)}) collective-permute-start(bf16[64,4096]{1,0:T(8,128)(2,1)S(1)} %get-tuple-element.28), channel_id=1, source_target_pairs={{0,2},{1,3},{2,0},{3,1},{4,6},{5,7},{6,4},{7,5},{8,10},{9,11},{10,... | collective-permute-start | bytes 1572872 | tf_op jit(solution)/shard_map/ppermute | solution.py:389
  39.9 1.0 %collective-permute-start.7 = (bf16[64,4096]{1,0:T(8,128)(2,1)S(1)}, bf16[64,4096]{1,0:T(8,128)(2,1)S(1)}, u32[]{:S(2)}, u32[]{:S(2)}) collective-permute-start(bf16[64,4096]{1,0:T(8,128)(2,1)S(1)} %get-tuple-element.29), channel_id=1, source_target_pairs={{0,3},{1,2},{2,1},{3,0},{4,7},{5,6},{6,5},{7,4},{8,11},{9,10},{10,... | collective-permute-start | bytes 1572872 | tf_op jit(solution)/shard_map/ppermute | solution.py:389
  40.9 2.6 %shard_map.84 = (bf16[64,4096]{1,0:T(8,128)(2,1)S(1)}, f32[64,4096]{1,0:T(8,128)S(1)}) custom-call(s32[2]{0:T(128)S(1)} %pad_add_fusion.place_ref, f32[256,1024]{1,0:T(8,128)S(1)} %get-tuple-element.21.local_ref, f32[256,1024]{1,0:T(8,128)S(1)} %get-tuple-element.22.query_ref, f32[128,128]{1,0:T(8,128)S(1)} %fusion.44.after_ref, ...), custom_call_target="tpu_custom_call" | custom-call | flops 1000000000 | bytes 10000000 | tf_op jit(solution)/shard_map/pallas_call | solution.py:365
  43.5 2.0 %collective-permute-start.8 = (bf16[64,4096]{1,0:T(8,128)(2,1)S(1)}, bf16[64,4096]{1,0:T(8,128)(2,1)S(1)}, u32[]{:S(2)}, u32[]{:S(2)}) collective-permute-start(bf16[64,4096]{1,0:T(8,128)(2,1)S(1)} %get-tuple-element.30), channel_id=1, source_target_pairs={{0,1},{1,0},{2,3},{3,2},{4,5},{5,4},{6,7},{7,6},{8,9},{9,8},{10,11... | collective-permute-start | bytes 1572872 | tf_op jit(solution)/shard_map/ppermute | solution.py:389
  45.5 24.2 %collective-permute-done.6 = bf16[64,4096]{1,0:T(8,128)(2,1)S(1)} collective-permute-done((bf16[64,4096]{1,0:T(8,128)(2,1)S(1)}, bf16[64,4096]{1,0:T(8,128)(2,1)S(1)}, u32[]{:S(2)}, u32[]{:S(2)}) %collective-permute-start.6) | collective-permute-done | bytes 524320 | tf_op jit(solution)/shard_map/ppermute | solution.py:389
  69.7 12.1 %collective-permute-done.7 = bf16[64,4096]{1,0:T(8,128)(2,1)S(1)} collective-permute-done((bf16[64,4096]{1,0:T(8,128)(2,1)S(1)}, bf16[64,4096]{1,0:T(8,128)(2,1)S(1)}, u32[]{:S(2)}, u32[]{:S(2)}) %collective-permute-start.7) | collective-permute-done | bytes 524320 | tf_op jit(solution)/shard_map/ppermute | solution.py:389
  81.8 1.1 %add_convert_fusion = bf16[64,4096]{1,0:T(8,128)(2,1)} fusion(bf16[64,4096]{1,0:T(8,128)(2,1)S(1)} %collective-permute-done.8, bf16[64,4096]{1,0:T(8,128)(2,1)S(1)} %collective-permute-done.7, f32[64,4096]{1,0:T(8,128)S(1)} %get-tuple-element.27, bf16[64,4096]{1,0:T(8,128)(2,1)S(1)} %collective-permute-done.6), kind=kLoop, calls=%fused_computation | loop fusion | flops 1835008 | bytes 3145728 | tf_op jit(solution)/shard_map/convert_element_type | solution.py:392
  (51 shorter events, 0.7 us)
Async XLA Ops:
  0.0 35.4 %copy-start = (f32[1024]{0:T(1024)S(1)}, f32[1024]{0:T(1024)}, u32[]{:S(2)}) copy-start(f32[1024]{0:T(1024)} %param.14) | copy-start | bytes 12292
  3.3 1.3 %collective-permute-start = (bf16[208,128]{1,0:T(8,128)(2,1)S(1)}, bf16[208,128]{1,0:T(8,128)(2,1)S(1)}, u32[]{:S(2)}, u32[]{:S(2)}) collective-permute-start(bf16[208,128]{1,0:T(8,128)(2,1)S(1)} %get-tuple-element.23), channel_id=1, source_target_pairs={{0,4},{4,0},{8,12},{12,8},{16,20},{20,16},{24,28},{28,24},{32,36},... | collective-permute-start | bytes 159752 | tf_op jit(solution)/shard_map/ppermute | solution.py:253
  4.7 4.2 %collective-permute-start.1 = (bf16[208,128]{1,0:T(8,128)(2,1)S(1)}, bf16[208,128]{1,0:T(8,128)(2,1)S(1)}, u32[]{:S(2)}, u32[]{:S(2)}) collective-permute-start(bf16[208,128]{1,0:T(8,128)(2,1)S(1)} %maximum_bitcast_fusion), channel_id=1, source_target_pairs={{0,8},{4,12},{8,0},{12,4},{16,24},{20,28},{24,16},{28,20},{32,40},... | collective-permute-start | bytes 159752 | tf_op jit(solution)/shard_map/ppermute | solution.py:253
  9.1 5.4 %collective-permute-start.2 = (bf16[208,128]{1,0:T(8,128)(2,1)S(1)}, bf16[208,128]{1,0:T(8,128)(2,1)S(1)}, u32[]{:S(2)}, u32[]{:S(2)}) collective-permute-start(bf16[208,128]{1,0:T(8,128)(2,1)S(1)} %maximum_bitcast_fusion.1), channel_id=1, source_target_pairs={{0,24},{4,28},{8,16},{12,20},{16,8},{20,12},{24,0},{28,4},{32,56},... | collective-permute-start | bytes 159752 | tf_op jit(solution)/shard_map/ppermute | solution.py:253
  14.7 4.2 %collective-permute-start.3 = (bf16[208,128]{1,0:T(8,128)(2,1)S(1)}, bf16[208,128]{1,0:T(8,128)(2,1)S(1)}, u32[]{:S(2)}, u32[]{:S(2)}) collective-permute-start(bf16[208,128]{1,0:T(8,128)(2,1)S(1)} %maximum_bitcast_fusion.2), channel_id=1, source_target_pairs={{0,32},{4,36},{8,40},{12,44},{16,48},{20,52},{24,56},{28,60},{32,0... | collective-permute-start | bytes 159752 | tf_op jit(solution)/shard_map/ppermute | solution.py:253
  19.1 5.4 %collective-permute-start.4 = (bf16[208,128]{1,0:T(8,128)(2,1)S(1)}, bf16[208,128]{1,0:T(8,128)(2,1)S(1)}, u32[]{:S(2)}, u32[]{:S(2)}) collective-permute-start(bf16[208,128]{1,0:T(8,128)(2,1)S(1)} %maximum_bitcast_fusion.3), channel_id=1, source_target_pairs={{0,96},{4,100},{8,104},{12,108},{16,112},{20,116},{24,120},{28,124... | collective-permute-start | bytes 159752 | tf_op jit(solution)/shard_map/ppermute | solution.py:253
  24.7 10.6 %collective-permute-start.5 = (bf16[208,128]{1,0:T(8,128)(2,1)S(1)}, bf16[208,128]{1,0:T(8,128)(2,1)S(1)}, u32[]{:S(2)}, u32[]{:S(2)}) collective-permute-start(bf16[208,128]{1,0:T(8,128)(2,1)S(1)} %maximum_bitcast_fusion.4), channel_id=1, source_target_pairs={{0,128},{4,132},{8,136},{12,140},{16,144},{20,148},{24,152},{28,15... | collective-permute-start | bytes 159752 | tf_op jit(solution)/shard_map/ppermute | solution.py:253
  38.3 31.3 %collective-permute-start.6 = (bf16[64,4096]{1,0:T(8,128)(2,1)S(1)}, bf16[64,4096]{1,0:T(8,128)(2,1)S(1)}, u32[]{:S(2)}, u32[]{:S(2)}) collective-permute-start(bf16[64,4096]{1,0:T(8,128)(2,1)S(1)} %get-tuple-element.28), channel_id=1, source_target_pairs={{0,2},{1,3},{2,0},{3,1},{4,6},{5,7},{6,4},{7,5},{8,10},{9,11},{10,... | collective-permute-start | bytes 1572872 | tf_op jit(solution)/shard_map/ppermute | solution.py:389
  39.9 41.9 %collective-permute-start.7 = (bf16[64,4096]{1,0:T(8,128)(2,1)S(1)}, bf16[64,4096]{1,0:T(8,128)(2,1)S(1)}, u32[]{:S(2)}, u32[]{:S(2)}) collective-permute-start(bf16[64,4096]{1,0:T(8,128)(2,1)S(1)} %get-tuple-element.29), channel_id=1, source_target_pairs={{0,3},{1,2},{2,1},{3,0},{4,7},{5,6},{6,5},{7,4},{8,11},{9,10},{10,... | collective-permute-start | bytes 1572872 | tf_op jit(solution)/shard_map/ppermute | solution.py:389
  43.5 38.3 %collective-permute-start.8 = (bf16[64,4096]{1,0:T(8,128)(2,1)S(1)}, bf16[64,4096]{1,0:T(8,128)(2,1)S(1)}, u32[]{:S(2)}, u32[]{:S(2)}) collective-permute-start(bf16[64,4096]{1,0:T(8,128)(2,1)S(1)} %get-tuple-element.30), channel_id=1, source_target_pairs={{0,1},{1,0},{2,3},{3,2},{4,5},{5,4},{6,7},{7,6},{8,9},{9,8},{10,11... | collective-permute-start | bytes 1572872 | tf_op jit(solution)/shard_map/ppermute | solution.py:389

commit v3 on v2

--- a/solution.py
+++ b/solution.py
@@ -17,9 +17,9 @@
 TAILS = 6
 PAYLOAD = STATE_ROWS + SUB * (HEADS + TAILS)
 COLUMN_TILE = 512
+RIGHT_TILES = 5
 CUTS = 4
-WEIGHT_CUTS = 8
-VMEM_LIMIT = 28 * 1024 * 1024
+VMEM_LIMIT = 20 * 1024 * 1024
 HBM = pl.BlockSpec(memory_space=pltpu.HBM)
 VMEM = pl.BlockSpec(memory_space=pltpu.VMEM)
 SMEM = pl.BlockSpec(memory_space=pltpu.SMEM)
@@ -52,10 +52,21 @@
     return made
 
 
+def fetch_weight(weight_hbm, weight_buf, sems, first):
+    tiles, _, width = weight_buf.shape
+    made = [
+        pltpu.make_async_copy(weight_hbm.at[:, pl.ds(first + i * width, width)], weight_buf.at[i], sems.at[i])
+        for i in range(tiles)
+    ]
+    for one in made:
+        one.start()
+    return made
+
+
 def state_kernel(
-    query_hbm, key_hbm, value_hbm, taps_hbm, rate_hbm,
-    payload_ref, sent_ref, rate_ref, gated_ref, taps_ref,
-    key_buf, value_buf, query_buf, taps_buf, rate_buf, ext_key, ext_value, sems,
+    query_hbm, key_hbm, value_hbm, taps_hbm, rate_hbm, residue_hbm, skip_hbm,
+    payload_ref, sent_ref, rate_ref, gated_ref, taps_ref, residue_ref, skip_ref,
+    key_buf, value_buf, query_buf, taps_buf, rate_buf, residue_buf, ext_key, ext_value, sems,
 ):
     rows, channels = key_buf.shape
     pitch = rows + PAD
@@ -67,7 +78,7 @@
             for part in range(CUTS)
             for hbm, buf in ((key_hbm, key_buf), (value_hbm, value_buf))
         ]
-        + [(query_hbm.at[pl.ds(rows - 16, 16), :], query_buf)],
+        + [(query_hbm.at[pl.ds(rows - 16, 16), :], query_buf), (residue_hbm, residue_buf), (skip_hbm, skip_ref)],
         sems,
     )
     ext_key[0:PAD, :] = jnp.zeros((PAD, LANES), F32)
@@ -107,7 +118,9 @@
     final = lax.fori_loop(0, rows, step, tuple(jnp.zeros((SUB, LANES), F32) for _ in range(MODES)), unroll=8)
     for m in range(MODES):
         payload_ref[m * SUB : (m + 1) * SUB, :] = final[m]
-    made[2 + 2 * CUTS].wait()
+    for one in made[2 + 2 * CUTS :]:
+        one.wait()
+    to_rows(residue_buf, residue_ref)
     last = query_buf[...].astype(F32)
     for place, row in enumerate((14, 15)):
         for group in range(SUB):
@@ -121,25 +134,10 @@
                 taps_ref[at : at + 1, :] = taps_buf[stream, tap : tap + 1, group * LANES : (group + 1) * LANES]
 
 
-def local_kernel(
-    query_hbm, residue_hbm, skip_hbm, weight_hbm, gated_ref, rate_ref, taps_ref,
-    local_ref, query_ref, residue_ref, weight_ref,
-    query_buf, residue_buf, skip_buf, ext, conv, sems,
-):
-    rows = query_buf.shape[0]
+def local_kernel(gated_ref, rate_ref, residue_ref, skip_ref, local_ref, conv):
+    rows = local_ref.shape[0]
     pitch = rows + PAD
-    depth = weight_ref.shape[0] // WEIGHT_CUTS
-    made = copies(
-        [(residue_hbm, residue_buf), (query_hbm, query_buf), (skip_hbm, skip_buf)]
-        + [
-            (weight_hbm.at[pl.ds(i * depth, depth), :], weight_ref.at[pl.ds(i * depth, depth), :])
-            for i in range(WEIGHT_CUTS)
-        ],
-        sems,
-    )
     decay = [jnp.exp(-rate_ref[m * SUB : (m + 1) * SUB, :]) for m in range(MODES)]
-    made[0].wait()
-    to_rows(residue_buf, residue_ref)
 
     def step(t, carry):
         now = gated_ref[pl.ds(t, SUB, stride=pitch), :]
@@ -149,14 +147,20 @@
         )
         return fresh
 
-    lax.fori_loop(0, rows, step, tuple(jnp.zeros((SUB, LANES), F32) for _ in range(MODES)), unroll=4)
-    made[1].wait()
-    made[2].wait()
-    ext[0:PAD, :] = jnp.zeros((PAD, LANES), F32)
+    lax.fori_loop(0, rows, step, tuple(jnp.zeros((SUB, LANES), F32) for _ in range(MODES)), unroll=8)
     for group in range(SUB):
         lanes = slice(group * LANES, (group + 1) * LANES)
         spot = slice(group * pitch, group * pitch + rows)
-        local_ref[:, lanes] = conv[spot, :] + skip_buf[group : group + 1, :] * gated_ref[spot, :]
+        local_ref[:, lanes] = conv[spot, :] + skip_ref[group : group + 1, :] * gated_ref[spot, :]
+
+
+def query_kernel(query_hbm, taps_ref, query_ref, query_buf, ext, sems):
+    rows = query_ref.shape[0]
+    made = copies([(query_hbm, query_buf)], sems)
+    ext[0:PAD, :] = jnp.zeros((PAD, LANES), F32)
+    made[0].wait()
+    for group in range(SUB):
+        lanes = slice(group * LANES, (group + 1) * LANES)
         ext[PAD : PAD + rows, :] = query_buf[:, lanes].astype(F32)
         tap = [taps_ref[p * SUB + group : p * SUB + group + 1, :] for p in range(SHORT)]
         query_ref[:, lanes] = (
@@ -164,18 +168,52 @@
             + tap[1] * ext[PAD - 1 : PAD - 1 + rows, :]
             + tap[2] * ext[PAD - 2 : PAD - 2 + rows, :]
         )
-    for one in made[3:]:
+
+
+def ahead_kernel(weight_hbm, weight_ref, sems):
+    for one in fetch_weight(weight_hbm, weight_ref, sems, weight_hbm.shape[1] - RIGHT_TILES * COLUMN_TILE):
         one.wait()
 
 
-def mix_kernel(
+def project(mixed, weight_buf, fetched, outs):
+    piece = mixed.shape[0] // len(outs)
+    tiles, _, width = weight_buf.shape
+    for i in range(tiles):
+        if fetched is not None:
+            fetched[i].wait()
+        where = slice(i * width, (i + 1) * width)
+        product = jnp.dot(mixed[...], weight_buf[i], preferred_element_type=F32)
+        for place, out in enumerate(outs):
+            out[:, where] = product[place * piece : (place + 1) * piece].astype(out.dtype)
+
+
+def across_kernel(
     place_ref, local_ref, query_ref, after_ref, fix_ref, rate_ref, residue_ref, weight_ref,
-    first_ref, second_ref,
-    mixed, coef,
+    right_two, right_three, mixed_ref,
+    coef,
 ):
-    half_rows, depth = mixed.shape
+    mix(place_ref, local_ref, query_ref, after_ref, fix_ref, rate_ref, residue_ref, mixed_ref, coef)
+    project(mixed_ref, weight_ref, None, [right_two, right_three])
+
+
+def left_kernel(mixed_ref, weight_hbm, left_two, left_three, weight_buf, sems):
+    fetched = fetch_weight(weight_hbm, weight_buf, sems, 0)
+    project(mixed_ref, weight_buf, fetched, [left_two, left_three])
+
+
+def own_kernel(
+    place_ref, local_ref, query_ref, after_ref, fix_ref, rate_ref, residue_ref, weight_hbm,
+    beside_ref, own_ref,
+    mixed, coef, weight_buf, sems,
+):
+    fetched = fetch_weight(weight_hbm, weight_buf, sems, 0)
+    mix(place_ref, local_ref, query_ref, after_ref, fix_ref, rate_ref, residue_ref, mixed, coef)
+    project(mixed, weight_buf, fetched, [beside_ref, own_ref])
+
+
+def mix(place_ref, local_ref, query_ref, after_ref, fix_ref, rate_ref, residue_ref, mixed, coef):
+    half_rows = mixed.shape[0]
     piece = half_rows // 2
-    columns = weight_ref.shape[1]
     base = place_ref[0]
     swap = place_ref[1]
     before = (base - 1).astype(F32)
@@ -212,14 +250,9 @@
             block = tile // piece
             row = pl.multiple_of((block ^ swap) * piece + tile % piece, 2 * SUB)
             mixed[pl.ds(row, 2 * SUB), lanes] = jnp.concatenate(parts, axis=0).astype(BF16)
-    for i in range(columns // COLUMN_TILE):
-        where = slice(i * COLUMN_TILE, (i + 1) * COLUMN_TILE)
-        product = jnp.dot(mixed[...], weight_ref[:, where], preferred_element_type=F32)
-        first_ref[:, where] = product[:piece].astype(first_ref.dtype)
-        second_ref[:, where] = product[piece:].astype(second_ref.dtype)
-
-
-def scan_states(payload, sent, rate, taps, rows, place, count):
+
+
+def scan_states(payload, sent, rate, taps, rows, place, count, beside):
     tap = taps.reshape(3, SHORT, SUB, LANES)
 
     def head_gated(tail, head):
@@ -250,6 +283,7 @@
         mask = width
         if bit >= 2 and bit % 2 == 0 and bit < bits:
             mask = width | (width >> 1)
+        sent = beside(bit, sent)
         got = lax.ppermute(sent, "seq", [(j, j ^ mask) for j in range(count)])
         theirs = got.reshape(-1, SUB, LANES).astype(F32)
         upper = ((place >> bit) & 1) == 1
@@ -301,7 +335,7 @@
     )
     params = pltpu.CompilerParams(vmem_limit_bytes=VMEM_LIMIT)
     dma = pltpu.SemaphoreType.DMA
-    payload, sent, rate, gated, taps = pl.pallas_call(
+    payload, sent, rate, gated, taps, residue, skip = pl.pallas_call(
         state_kernel,
         out_shape=(
             jax.ShapeDtypeStruct((PAYLOAD, LANES), F32),
@@ -309,47 +343,86 @@
             jax.ShapeDtypeStruct((STATE_ROWS, LANES), F32),
             jax.ShapeDtypeStruct((SUB * pitch, LANES), F32),
             jax.ShapeDtypeStruct((3 * SHORT * SUB, LANES), F32),
+            jax.ShapeDtypeStruct((STATE_ROWS, LANES), F32),
+            jax.ShapeDtypeStruct((SUB, LANES), F32),
         ),
-        in_specs=[HBM] * 5,
-        out_specs=(VMEM,) * 5,
+        in_specs=[HBM] * 7,
+        out_specs=(VMEM,) * 7,
         scratch_shapes=[
             pltpu.VMEM((rows, channels), BF16),
             pltpu.VMEM((rows, channels), BF16),
             pltpu.VMEM((16, channels), BF16),
             pltpu.VMEM((3, SHORT, channels), F32),
             pltpu.VMEM((MODES, channels), F32),
+            pltpu.VMEM((MODES, channels), F32),
             pltpu.VMEM((pitch, LANES), F32),
             pltpu.VMEM((pitch, LANES), F32),
-            dma((3 + 2 * CUTS,)),
+            dma((5 + 2 * CUTS,)),
         ],
         compiler_params=params,
         cost_estimate=pl.CostEstimate(flops=20_000_000, bytes_accessed=3_000_000, transcendentals=0),
-    )(query_stream, key_stream, value_stream, short_filter, rates)
-    local, query, residue, weight = pl.pallas_call(
-        local_kernel,
-        out_shape=(
-            jax.ShapeDtypeStruct((rows, channels), F32),
-            jax.ShapeDtypeStruct((rows, channels), F32),
-            jax.ShapeDtypeStruct((STATE_ROWS, LANES), F32),
-            jax.ShapeDtypeStruct(out_weight.shape, BF16),
-        ),
-        in_specs=[HBM] * 4 + [VMEM] * 3,
-        out_specs=(VMEM,) * 4,
-        scratch_shapes=[
-            pltpu.VMEM((rows, channels), BF16),
-            pltpu.VMEM((MODES, channels), F32),
-            pltpu.VMEM((SUB, LANES), F32),
-            pltpu.VMEM((pitch, LANES), F32),
-            pltpu.VMEM((SUB * pitch, LANES), F32),
-            dma((3 + WEIGHT_CUTS,)),
-        ],
-        compiler_params=params,
-        cost_estimate=pl.CostEstimate(flops=20_000_000, bytes_accessed=6_000_000, transcendentals=0),
-    )(query_stream, residues, skips, out_weight, gated, rate, taps)
+    )(query_stream, key_stream, value_stream, short_filter, rates, residues, skips)
+    right_side = RIGHT_TILES * COLUMN_TILE
+    left_side = columns - right_side
+    aside = {}
+
+    light = pl.CostEstimate(flops=1_000_000, bytes_accessed=100_000, transcendentals=0)
+
+    def local_part(gated):
+        return pl.pallas_call(
+            local_kernel,
+            out_shape=jax.ShapeDtypeStruct((rows, channels), F32),
+            in_specs=[VMEM] * 4,
+            out_specs=VMEM,
+            scratch_shapes=[pltpu.VMEM((SUB * pitch, LANES), F32)],
+            compiler_params=params,
+            cost_estimate=light,
+        )(gated, rate, residue, skip)
+
+    def query_part(taps):
+        return pl.pallas_call(
+            query_kernel,
+            out_shape=jax.ShapeDtypeStruct((rows, channels), F32),
+            in_specs=[HBM, VMEM],
+            out_specs=VMEM,
+            scratch_shapes=[
+                pltpu.VMEM((rows, channels), BF16),
+                pltpu.VMEM((pitch, LANES), F32),
+                dma((1,)),
+            ],
+            compiler_params=params,
+            cost_estimate=pl.CostEstimate(flops=1_000_000, bytes_accessed=100_000, transcendentals=0),
+        )(query_stream, taps)
+
+    def weight_part(out_weight):
+        return pl.pallas_call(
+            ahead_kernel,
+            out_shape=jax.ShapeDtypeStruct((RIGHT_TILES, channels, COLUMN_TILE), BF16),
+            in_specs=[HBM],
+            out_specs=VMEM,
+            scratch_shapes=[dma((RIGHT_TILES,))],
+            compiler_params=params,
+            cost_estimate=light,
+        )(out_weight)
+
+    def beside_scan(bit, sent):
+        last = (count - 1).bit_length() - 1
+        if bit == last - 2:
+            sent, aside["local"] = lax.optimization_barrier((sent, gated))
+        elif bit == last - 1:
+            aside["local"] = local_part(aside["local"])
+            sent, aside["local"], aside["query"] = lax.optimization_barrier((sent, aside["local"], taps))
+        elif bit == last:
+            aside["query"] = query_part(aside["query"])
+            sent, aside["query"], weight = lax.optimization_barrier((sent, aside["query"], out_weight))
+            aside["right"] = weight_part(weight)
+        return sent
+
     rate_rows = rate.reshape(MODES, SUB, LANES)
+    start, border, gates, tap = scan_states(payload, sent, rate_rows, taps, rows, place, count, beside_scan)
+    local = aside["local"]
+    query = aside["query"]
     residue_rows = residue.reshape(MODES, SUB, LANES)
-    start, border, gates, tap = scan_states(payload, sent, rate_rows, taps, rows, place, count)
-    skip = skip_bias.reshape(SUB, LANES)
     after_zero = jnp.exp(-rate_rows) * start + gates[0]
     after_one = jnp.exp(-rate_rows) * after_zero + gates[1]
     fixes = jnp.concatenate(
@@ -361,34 +434,70 @@
         ]
     )
 
-    def mix(half, swap, second_type):
-        return pl.pallas_call(
-            mix_kernel,
-            out_shape=(
-                jax.ShapeDtypeStruct((piece, columns), BF16),
-                jax.ShapeDtypeStruct((piece, columns), second_type),
-            ),
-            in_specs=[SMEM] + [VMEM] * 7,
-            out_specs=(VMEM,) * 2,
-            scratch_shapes=[
-                pltpu.VMEM((2 * piece, channels), BF16),
-                pltpu.VMEM((STATE_ROWS, LANES), F32),
-            ],
-            compiler_params=params,
-            cost_estimate=pl.CostEstimate(flops=1_000_000_000, bytes_accessed=10_000_000, transcendentals=0),
-        )(
-            jnp.stack([half * 2 * piece, swap]).astype(jnp.int32),
-            local, query, after_one.reshape(STATE_ROWS, LANES), fixes, rate, residue, weight,
-        )
+    def half_inputs(half, swap):
+        at = jnp.stack([half * 2 * piece, swap]).astype(jnp.int32)
+        return at, local, query, after_one.reshape(STATE_ROWS, LANES), fixes, rate, residue
+
+    def sent_by(block, pairs):
+        return lax.ppermute(block, "chan", pairs)
+
+    def across(step):
+        return [(j, j ^ step) for j in range(parts)]
 
     own_half, odd = mine // 2, mine % 2
-    across_two, across_three = mix(1 - own_half, odd, BF16)
-    beside, own = mix(own_half, 1 - odd, F32)
-
-    def sent_by(block, step):
-        return lax.ppermute(block, "chan", [(j, j ^ step) for j in range(parts)]).astype(F32)
-
-    total = own + sent_by(across_two, 2) + sent_by(across_three, 3) + sent_by(beside, 1)
+    right_two, right_three, mixed = pl.pallas_call(
+        across_kernel,
+        out_shape=(
+            jax.ShapeDtypeStruct((piece, right_side), BF16),
+            jax.ShapeDtypeStruct((piece, right_side), BF16),
+            jax.ShapeDtypeStruct((2 * piece, channels), BF16),
+        ),
+        in_specs=[SMEM] + [VMEM] * 7,
+        out_specs=(VMEM,) * 3,
+        scratch_shapes=[pltpu.VMEM((STATE_ROWS, LANES), F32)],
+        compiler_params=params,
+        cost_estimate=light,
+    )(*half_inputs(1 - own_half, odd), aside["right"])
+    left_tiles, tiles = left_side // COLUMN_TILE, columns // COLUMN_TILE
+    left_two, left_three = pl.pallas_call(
+        left_kernel,
+        out_shape=(jax.ShapeDtypeStruct((piece, left_side), BF16),) * 2,
+        in_specs=[VMEM, HBM],
+        out_specs=(VMEM,) * 2,
+        scratch_shapes=[pltpu.VMEM((left_tiles, channels, COLUMN_TILE), BF16), dma((left_tiles,))],
+        compiler_params=params,
+        cost_estimate=light,
+    )(mixed, out_weight)
+    handed_three = sent_by(right_three, [(0, 1), (3, 2)])
+    handed_two = sent_by(right_two, [(0, 1), (3, 2)])
+    got_two, got_three = sent_by(left_two, across(2)), sent_by(left_three, across(3))
+    beside, own = pl.pallas_call(
+        own_kernel,
+        out_shape=(
+            jax.ShapeDtypeStruct((piece, columns), BF16),
+            jax.ShapeDtypeStruct((piece, columns), F32),
+        ),
+        in_specs=[SMEM] + [VMEM] * 6 + [HBM],
+        out_specs=(VMEM,) * 2,
+        scratch_shapes=[
+            pltpu.VMEM((2 * piece, channels), BF16),
+            pltpu.VMEM((STATE_ROWS, LANES), F32),
+            pltpu.VMEM((tiles, channels, COLUMN_TILE), BF16),
+            dma((tiles,)),
+        ],
+        compiler_params=params,
+        cost_estimate=light,
+    )(*half_inputs(own_half, 1 - odd), out_weight)
+    got_one = sent_by(beside, across(1))
+    handed_three, _ = lax.optimization_barrier((handed_three, beside))
+    joined_two = (right_two.astype(F32) + handed_three.astype(F32)).astype(BF16)
+    handed_two, _ = lax.optimization_barrier((handed_two, joined_two))
+    joined_three = (right_three.astype(F32) + handed_two.astype(F32)).astype(BF16)
+    far_two = sent_by(joined_two, [(1, 3), (2, 0)])
+    far_three = sent_by(joined_three, [(1, 2), (2, 1)])
+    left = got_two.astype(F32) + got_three.astype(F32)
+    far = far_two.astype(F32) + far_three.astype(F32)
+    total = own + got_one.astype(F32) + jnp.concatenate([left, far], axis=1)
     return total.astype(BF16)
 
 

time: 82.9 us -> 76.9 us (0.928)
  waiting for transfers between devices: 47.5 us -> 20.9 us
  starting transfers between devices: 20.2 us -> 31.2 us
  Pallas kernels: 12.5 us -> 19.5 us
  other arithmetic: 2.19 us -> 4.43 us
    ppermute x3 -> x7, waiting for transfers between devices: 36.3 us -> 13.7 us  [sent_by(): return lax.ppermute(block, 'chan', pairs)]
    ppermute x3 -> x7, starting transfers between devices: 4.56 us -> 15.5 us  [sent_by(): return lax.ppermute(block, 'chan', pairs)]
    pallas_call x3 -> x6, Pallas kernels: 9.26 us -> 16.2 us  [the longest x1 4.4 us: on_device(): pl.pallas_call(own_kernel, out_shape=(jax.ShapeDtypeStruct((piece, column...]
    ppermute x6, waiting for transfers between devices: 11.3 us -> 7.28 us  [scan_states(): got = lax.ppermute(sent, 'seq', [(j, j ^ mask) for j in range(count)])]
    convert_element_type x0 -> x2, other arithmetic: none -> 2.2 us  [the longest x1 1.15 us: on_device(): joined_two = (right_two.astype(F32) + handed_three.astype(F32)).astype(BF16)]
  transfers between devices with their start and end apart: 9 -> 13, of which waited for: 7 -> 6; matrix products, arithmetic and copies ran while one was open for 0% -> 3% of each run, Pallas kernels for 8% -> 17%
where the time goes in v3:
time: 76.9 us; the launch traced here: 76.6 us
  starting transfers between devices  31.2 us (41%)
  waiting for transfers between devices  20.9 us (27%)
  Pallas kernels  19.5 us (25%)
  other arithmetic  4.43 us (6%)
    ppermute x6, starting transfers between devices, scan_states(): got = lax.ppermute(sent, 'seq', [(j, j ^ mask) for j in range(count)])  15.7 us
    ppermute x7, starting transfers between devices, sent_by(): return lax.ppermute(block, 'chan', pairs)  15.5 us
    ppermute x7, waiting for transfers between devices, sent_by(): return lax.ppermute(block, 'chan', pairs)  13.7 us
    ppermute x6, waiting for transfers between devices, scan_states(): got = lax.ppermute(sent, 'seq', [(j, j ^ mask) for j in range(count)])  7.28 us
    pallas_call x1, Pallas kernels, on_device(): pl.pallas_call(own_kernel, out_shape=(jax.ShapeDtypeStruct((piece, column...  4.4 us
    pallas_call x1, Pallas kernels, on_device(): pl.pallas_call(state_kernel, out_shape=(jax.ShapeDtypeStruct((PAYLOAD, LA...  3.27 us
    pallas_call x1, Pallas kernels, on_device(): pl.pallas_call(across_kernel, out_shape=(jax.ShapeDtypeStruct((piece, rig...  2.98 us
    pallas_call x1, Pallas kernels, local_part(): pl.pallas_call(local_kernel, out_shape=jax.ShapeDtypeStruct((rows, channe...  2.62 us
  transfers between devices with their start and end apart: 13, of which 6 were waited for; matrix products, arithmetic and copies ran while one was open for 3% of the time, Pallas kernels for 17%

profile of v3, /device:TPU:32, one launch (start us, length us, event | category | flops | bytes accessed | tf_op | source)
XLA Modules:
  0.0 76.6 jit_solution(6940302661815702579)
XLA Ops:
  0.0 3.3 %shard_map.82 = (f32[208,128]{1,0:T(8,128)S(1)}, bf16[208,128]{1,0:T(8,128)(2,1)S(1)}, f32[128,128]{1,0:T(8,128)S(1)}, f32[2112,128]{1,0:T(8,128)S(1)}, f32[72,1...) custom-call(bf16[256,1024]{1,0:T(8,128)(2,1)} %query_hbm.3, bf16[256,1024]{1,0:T(8,128)(2,1)} %key_hbm.1, ...), custom_call_target="tpu_custom_call" | custom-call | flops 20000000 | bytes 3000000 | tf_op jit(solution)/shard_map/pallas_call | solution.py:338
  3.4 1.2 %collective-permute-done = bf16[208,128]{1,0:T(8,128)(2,1)S(1)} collective-permute-done((bf16[208,128]{1,0:T(8,128)(2,1)S(1)}, bf16[208,128]{1,0:T(8,128)(2,1)S(1)}, u32[]{:S(2)}, u32[]{:S(2)}) %collective-permute-start) | collective-permute-done | bytes 53280 | tf_op jit(solution)/shard_map/ppermute | solution.py:287
  4.8 1.7 %collective-permute-start.1 = (bf16[208,128]{1,0:T(8,128)(2,1)S(1)}, bf16[208,128]{1,0:T(8,128)(2,1)S(1)}, u32[]{:S(2)}, u32[]{:S(2)}) collective-permute-start(bf16[208,128]{1,0:T(8,128)(2,1)S(1)} %maximum_bitcast_fusion), channel_id=1, source_target_pairs={{0,8},{4,12},{8,0},{12,4},{16,24},{20,28},{24,16},{28,20},{32,40},... | collective-permute-start | bytes 159752 | tf_op jit(solution)/shard_map/ppermute | solution.py:287
  6.4 2.6 %collective-permute-done.1 = bf16[208,128]{1,0:T(8,128)(2,1)S(1)} collective-permute-done((bf16[208,128]{1,0:T(8,128)(2,1)S(1)}, bf16[208,128]{1,0:T(8,128)(2,1)S(1)}, u32[]{:S(2)}, u32[]{:S(2)}) %collective-permute-start.1) | collective-permute-done | bytes 53280 | tf_op jit(solution)/shard_map/ppermute | solution.py:287
  9.2 3.1 %collective-permute-start.2 = (bf16[208,128]{1,0:T(8,128)(2,1)S(1)}, bf16[208,128]{1,0:T(8,128)(2,1)S(1)}, u32[]{:S(2)}, u32[]{:S(2)}) collective-permute-start(bf16[208,128]{1,0:T(8,128)(2,1)S(1)} %maximum_bitcast_fusion.1), channel_id=1, source_target_pairs={{0,24},{4,28},{8,16},{12,20},{16,8},{20,12},{24,0},{28,4},{32,56},... | collective-permute-start | bytes 159752 | tf_op jit(solution)/shard_map/ppermute | solution.py:287
  12.3 2.3 %collective-permute-done.2 = bf16[208,128]{1,0:T(8,128)(2,1)S(1)} collective-permute-done((bf16[208,128]{1,0:T(8,128)(2,1)S(1)}, bf16[208,128]{1,0:T(8,128)(2,1)S(1)}, u32[]{:S(2)}, u32[]{:S(2)}) %collective-permute-start.2) | collective-permute-done | bytes 53280 | tf_op jit(solution)/shard_map/ppermute | solution.py:287
  14.8 1.6 %collective-permute-start.3 = (bf16[208,128]{1,0:T(8,128)(2,1)S(1)}, bf16[208,128]{1,0:T(8,128)(2,1)S(1)}, u32[]{:S(2)}, u32[]{:S(2)}) collective-permute-start(bf16[208,128]{1,0:T(8,128)(2,1)S(1)} %maximum_bitcast_fusion.2), channel_id=1, source_target_pairs={{0,32},{4,36},{8,40},{12,44},{16,48},{20,52},{24,56},{28,60},{32,0... | collective-permute-start | bytes 159752 | tf_op jit(solution)/shard_map/ppermute | solution.py:287
  16.4 2.6 %shard_map.83.local_ref = f32[256,1024]{1,0:T(8,128)S(1)} custom-call(f32[2112,128]{1,0:T(8,128)S(1)} %get-tuple-element.35.gated_ref, f32[128,128]{1,0:T(8,128)S(1)} %get-tuple-element.29.rate_ref, f32[128,128]{1,0:T(8,128)S(1)} %get-tuple-element.36.residue_ref, f32[8,128]{1,0:T(8,128)S(1)} %get-tuple-element.37.skip_ref), custom_call_target="tpu_custom_call" | custom-call | flops 1000000 | bytes 100000 | tf_op jit(solution)/shard_map/pallas_call | solution.py:372
  19.2 2.8 %collective-permute-start.4 = (bf16[208,128]{1,0:T(8,128)(2,1)S(1)}, bf16[208,128]{1,0:T(8,128)(2,1)S(1)}, u32[]{:S(2)}, u32[]{:S(2)}) collective-permute-start(bf16[208,128]{1,0:T(8,128)(2,1)S(1)} %maximum_bitcast_fusion.3), channel_id=1, source_target_pairs={{0,96},{4,100},{8,104},{12,108},{16,112},{20,116},{24,120},{28,124... | collective-permute-start | bytes 159752 | tf_op jit(solution)/shard_map/ppermute | solution.py:287
  22.0 1.4 %shard_map.84.query_ref = f32[256,1024]{1,0:T(8,128)S(1)} custom-call(bf16[256,1024]{1,0:T(8,128)(2,1)} %query_hbm.3, f32[72,128]{1,0:T(8,128)S(1)} %get-tuple-element.40.taps_ref), custom_call_target="tpu_custom_call" | custom-call | flops 1000000 | bytes 100000 | tf_op jit(solution)/shard_map/pallas_call | solution.py:383
  23.4 1.2 %collective-permute-done.4 = bf16[208,128]{1,0:T(8,128)(2,1)S(1)} collective-permute-done((bf16[208,128]{1,0:T(8,128)(2,1)S(1)}, bf16[208,128]{1,0:T(8,128)(2,1)S(1)}, u32[]{:S(2)}, u32[]{:S(2)}) %collective-permute-start.4) | collective-permute-done | bytes 53280 | tf_op jit(solution)/shard_map/ppermute | solution.py:287
  24.8 6.4 %collective-permute-start.5 = (bf16[208,128]{1,0:T(8,128)(2,1)S(1)}, bf16[208,128]{1,0:T(8,128)(2,1)S(1)}, u32[]{:S(2)}, u32[]{:S(2)}) collective-permute-start(bf16[208,128]{1,0:T(8,128)(2,1)S(1)} %maximum_bitcast_fusion.4), channel_id=1, source_target_pairs={{0,128},{4,132},{8,136},{12,140},{16,144},{20,148},{24,152},{28,15... | collective-permute-start | bytes 159752 | tf_op jit(solution)/shard_map/ppermute | solution.py:287
  31.2 2.6 %shard_map.86.weight_ref = bf16[5,1024,512]{2,1,0:T(8,128)(2,1)S(1)} custom-call(bf16[1024,4096]{1,0:T(8,128)(2,1)} %weight_hbm.4), custom_call_target="tpu_custom_call" | custom-call | flops 1000000 | bytes 100000 | tf_op jit(solution)/shard_map/pallas_call | solution.py:398
  34.3 3.0 %shard_map.87 = (bf16[64,2560]{1,0:T(8,128)(2,1)}, bf16[64,2560]{1,0:T(8,128)(2,1)}, bf16[128,1024]{1,0:T(8,128)(2,1)S(1)}) custom-call(s32[2]{0:T(128)S(1)} %pad_add_fusion.1.place_ref, f32[256,1024]{1,0:T(8,128)S(1)} %shard_map.83.local_ref, f32[256,1024]{1,0:T(8,128)S(1)} %shard_map.84.query_ref, f32[128,128]{1,0:T(8,128)S(1)} %fusion.43.after_ref, ...), custom_call_target="tpu_custom_call" | custom-call | flops 1000000 | bytes 100000 | tf_op jit(solution)/shard_map/pallas_call | solution.py:448
  37.3 1.3 %collective-permute-start.9 = (bf16[64,2560]{1,0:T(8,128)(2,1)}, bf16[64,2560]{1,0:T(8,128)(2,1)}, u32[]{:S(2)}, u32[]{:S(2)}) collective-permute-start(bf16[64,2560]{1,0:T(8,128)(2,1)} %get-tuple-element.50), channel_id=1, source_target_pairs={{0,1},{3,2},{4,5},{7,6},{8,9},{11,10},{12,13},{15,14},{16,17},{19,... | collective-permute-start | bytes 983048 | tf_op jit(solution)/shard_map/ppermute | solution.py:442
  38.7 2.2 %shard_map.88 = (bf16[64,1536]{1,0:T(8,128)(2,1)S(1)}, bf16[64,1536]{1,0:T(8,128)(2,1)S(1)}) custom-call(bf16[128,1024]{1,0:T(8,128)(2,1)S(1)} %get-tuple-element.46.mixed_ref, bf16[1024,4096]{1,0:T(8,128)(2,1)} %weight_hbm.4), custom_call_target="tpu_custom_call" | custom-call | flops 1000000 | bytes 100000 | tf_op jit(solution)/shard_map/pallas_call | solution.py:462
  40.9 3.9 %collective-permute-start.7 = (bf16[64,1536]{1,0:T(8,128)(2,1)S(1)}, bf16[64,1536]{1,0:T(8,128)(2,1)S(1)}, u32[]{:S(2)}, u32[]{:S(2)}) collective-permute-start(bf16[64,1536]{1,0:T(8,128)(2,1)S(1)} %get-tuple-element.47), channel_id=1, source_target_pairs={{0,2},{1,3},{2,0},{3,1},{4,6},{5,7},{6,4},{7,5},{8,10},{9,11},{10,... | collective-permute-start | bytes 589832 | tf_op jit(solution)/shard_map/ppermute | solution.py:442
  45.8 1.3 %collective-permute-start.11 = (bf16[64,2560]{1,0:T(8,128)(2,1)}, bf16[64,2560]{1,0:T(8,128)(2,1)S(1)}, u32[]{:S(2)}, u32[]{:S(2)}) collective-permute-start(bf16[64,2560]{1,0:T(8,128)(2,1)} %get-tuple-element.49), channel_id=1, source_target_pairs={{0,1},{3,2},{4,5},{7,6},{8,9},{11,10},{12,13},{15,14},{16,17},{19,... | collective-permute-start | bytes 983048 | tf_op jit(solution)/shard_map/ppermute | solution.py:442
  47.1 4.4 %shard_map.85 = (bf16[64,4096]{1,0:T(8,128)(2,1)S(1)}, f32[64,4096]{1,0:T(8,128)S(1)}) custom-call(s32[2]{0:T(128)S(1)} %pad_add_fusion.place_ref, f32[256,1024]{1,0:T(8,128)S(1)} %shard_map.83.local_ref, f32[256,1024]{1,0:T(8,128)S(1)} %shard_map.84.query_ref, f32[128,128]{1,0:T(8,128)S(1)} %fusion.43.after_ref, f32[32,128]{1,0:T(8,128)S(1)} %pad_maximum_fusion.fix_ref, ...), custom_call_target="tpu_custom_call" | custom-call | flops 1000000 | bytes 100000 | tf_op jit(solution)/shard_map/pallas_call | solution.py:474
  51.5 2.7 %collective-permute-start.6 = (bf16[64,4096]{1,0:T(8,128)(2,1)S(1)}, bf16[64,4096]{1,0:T(8,128)(2,1)S(1)}, u32[]{:S(2)}, u32[]{:S(2)}) collective-permute-start(bf16[64,4096]{1,0:T(8,128)(2,1)S(1)} %get-tuple-element.44), channel_id=1, source_target_pairs={{0,1},{1,0},{2,3},{3,2},{4,5},{5,4},{6,7},{7,6},{8,9},{9,8},{10,11... | collective-permute-start | bytes 1572872 | tf_op jit(solution)/shard_map/ppermute | solution.py:442
  55.4 2.4 %collective-permute-start.10 = (bf16[64,2560]{1,0:T(8,128)(2,1)S(1)}, bf16[64,2560]{1,0:T(8,128)(2,1)S(1)}, u32[]{:S(2)}, u32[]{:S(2)}) collective-permute-start(bf16[64,2560]{1,0:T(8,128)(2,1)S(1)} %add_convert_fusion.1), channel_id=1, source_target_pairs={{1,3},{2,0},{5,7},{6,4},{9,11},{10,8},{13,15},{14,12},{17,19},{18,... | collective-permute-start | bytes 983048 | tf_op jit(solution)/shard_map/ppermute | solution.py:442
  57.8 7.7 %collective-permute-done.11 = bf16[64,2560]{1,0:T(8,128)(2,1)S(1)} collective-permute-done((bf16[64,2560]{1,0:T(8,128)(2,1)}, bf16[64,2560]{1,0:T(8,128)(2,1)S(1)}, u32[]{:S(2)}, u32[]{:S(2)}) %collective-permute-start.11) | collective-permute-done | bytes 327712 | tf_op jit(solution)/shard_map/ppermute | solution.py:442
  66.6 2.9 %collective-permute-start.12 = (bf16[64,2560]{1,0:T(8,128)(2,1)S(1)}, bf16[64,2560]{1,0:T(8,128)(2,1)S(1)}, u32[]{:S(2)}, u32[]{:S(2)}) collective-permute-start(bf16[64,2560]{1,0:T(8,128)(2,1)S(1)} %add_convert_fusion), channel_id=1, source_target_pairs={{1,2},{2,1},{5,6},{6,5},{9,10},{10,9},{13,14},{14,13},{17,18},{18,... | collective-permute-start | bytes 983048 | tf_op jit(solution)/shard_map/ppermute | solution.py:442
  69.6 6.0 %collective-permute-done.12 = bf16[64,2560]{1,0:T(8,128)(2,1)S(1)} collective-permute-done((bf16[64,2560]{1,0:T(8,128)(2,1)S(1)}, bf16[64,2560]{1,0:T(8,128)(2,1)S(1)}, u32[]{:S(2)}, u32[]{:S(2)}) %collective-permute-start.12) | collective-permute-done | bytes 327712 | tf_op jit(solution)/shard_map/ppermute | solution.py:442
  (76 shorter events, 5.6 us)
Async XLA Ops:
  3.3 1.3 %collective-permute-start = (bf16[208,128]{1,0:T(8,128)(2,1)S(1)}, bf16[208,128]{1,0:T(8,128)(2,1)S(1)}, u32[]{:S(2)}, u32[]{:S(2)}) collective-permute-start(bf16[208,128]{1,0:T(8,128)(2,1)S(1)} %get-tuple-element.30), channel_id=1, source_target_pairs={{0,4},{4,0},{8,12},{12,8},{16,20},{20,16},{24,28},{28,24},{32,36},... | collective-permute-start | bytes 159752 | tf_op jit(solution)/shard_map/ppermute | solution.py:287
  4.6 11.7 %copy-start = (f32[208,128]{1,0:T(8,128)}, f32[208,128]{1,0:T(8,128)S(1)}, u32[]{:S(2)}) copy-start(f32[208,128]{1,0:T(8,128)S(1)} %convert_element_type.195) | copy-start | bytes 319492
  4.8 4.2 %collective-permute-start.1 = (bf16[208,128]{1,0:T(8,128)(2,1)S(1)}, bf16[208,128]{1,0:T(8,128)(2,1)S(1)}, u32[]{:S(2)}, u32[]{:S(2)}) collective-permute-start(bf16[208,128]{1,0:T(8,128)(2,1)S(1)} %maximum_bitcast_fusion), channel_id=1, source_target_pairs={{0,8},{4,12},{8,0},{12,4},{16,24},{20,28},{24,16},{28,20},{32,40},... | collective-permute-start | bytes 159752 | tf_op jit(solution)/shard_map/ppermute | solution.py:287
  9.0 7.4 %copy-start.4 = (f32[208,128]{1,0:T(8,128)}, f32[208,128]{1,0:T(8,128)S(1)}, u32[]{:S(2)}) copy-start(f32[208,128]{1,0:T(8,128)S(1)} %convert_element_type.201) | copy-start | bytes 319492
  9.2 5.4 %collective-permute-start.2 = (bf16[208,128]{1,0:T(8,128)(2,1)S(1)}, bf16[208,128]{1,0:T(8,128)(2,1)S(1)}, u32[]{:S(2)}, u32[]{:S(2)}) collective-permute-start(bf16[208,128]{1,0:T(8,128)(2,1)S(1)} %maximum_bitcast_fusion.1), channel_id=1, source_target_pairs={{0,24},{4,28},{8,16},{12,20},{16,8},{20,12},{24,0},{28,4},{32,56},... | collective-permute-start | bytes 159752 | tf_op jit(solution)/shard_map/ppermute | solution.py:287
  14.6 7.4 %copy-start.2 = (f32[208,128]{1,0:T(8,128)}, f32[208,128]{1,0:T(8,128)S(1)}, u32[]{:S(2)}) copy-start(f32[208,128]{1,0:T(8,128)S(1)} %convert_element_type.207) | copy-start | bytes 319492
  14.8 4.2 %collective-permute-start.3 = (bf16[208,128]{1,0:T(8,128)(2,1)S(1)}, bf16[208,128]{1,0:T(8,128)(2,1)S(1)}, u32[]{:S(2)}, u32[]{:S(2)}) collective-permute-start(bf16[208,128]{1,0:T(8,128)(2,1)S(1)} %maximum_bitcast_fusion.2), channel_id=1, source_target_pairs={{0,32},{4,36},{8,40},{12,44},{16,48},{20,52},{24,56},{28,60},{32,0... | collective-permute-start | bytes 159752 | tf_op jit(solution)/shard_map/ppermute | solution.py:287
  19.2 5.4 %collective-permute-start.4 = (bf16[208,128]{1,0:T(8,128)(2,1)S(1)}, bf16[208,128]{1,0:T(8,128)(2,1)S(1)}, u32[]{:S(2)}, u32[]{:S(2)}) collective-permute-start(bf16[208,128]{1,0:T(8,128)(2,1)S(1)} %maximum_bitcast_fusion.3), channel_id=1, source_target_pairs={{0,96},{4,100},{8,104},{12,108},{16,112},{20,116},{24,120},{28,124... | collective-permute-start | bytes 159752 | tf_op jit(solution)/shard_map/ppermute | solution.py:287
  24.8 9.1 %collective-permute-start.5 = (bf16[208,128]{1,0:T(8,128)(2,1)S(1)}, bf16[208,128]{1,0:T(8,128)(2,1)S(1)}, u32[]{:S(2)}, u32[]{:S(2)}) collective-permute-start(bf16[208,128]{1,0:T(8,128)(2,1)S(1)} %maximum_bitcast_fusion.4), channel_id=1, source_target_pairs={{0,128},{4,132},{8,136},{12,140},{16,144},{20,148},{24,152},{28,15... | collective-permute-start | bytes 159752 | tf_op jit(solution)/shard_map/ppermute | solution.py:287
  31.2 2.7 %copy-start.1 = (f32[208,128]{1,0:T(8,128)S(1)}, f32[208,128]{1,0:T(8,128)}, u32[]{:S(2)}) copy-start(f32[208,128]{1,0:T(8,128)} %copy-done) | copy-start | bytes 319492
  31.2 2.7 %copy-start.3 = (f32[208,128]{1,0:T(8,128)S(1)}, f32[208,128]{1,0:T(8,128)}, u32[]{:S(2)}) copy-start(f32[208,128]{1,0:T(8,128)} %copy-done.2) | copy-start | bytes 319492
  31.2 2.7 %copy-start.5 = (f32[208,128]{1,0:T(8,128)S(1)}, f32[208,128]{1,0:T(8,128)}, u32[]{:S(2)}) copy-start(f32[208,128]{1,0:T(8,128)} %copy-done.4) | copy-start | bytes 319492
  37.3 17.0 %collective-permute-start.9 = (bf16[64,2560]{1,0:T(8,128)(2,1)}, bf16[64,2560]{1,0:T(8,128)(2,1)}, u32[]{:S(2)}, u32[]{:S(2)}) collective-permute-start(bf16[64,2560]{1,0:T(8,128)(2,1)} %get-tuple-element.50), channel_id=1, source_target_pairs={{0,1},{3,2},{4,5},{7,6},{8,9},{11,10},{12,13},{15,14},{16,17},{19,... | collective-permute-start | bytes 983048 | tf_op jit(solution)/shard_map/ppermute | solution.py:442
  40.9 28.6 %collective-permute-start.7 = (bf16[64,1536]{1,0:T(8,128)(2,1)S(1)}, bf16[64,1536]{1,0:T(8,128)(2,1)S(1)}, u32[]{:S(2)}, u32[]{:S(2)}) collective-permute-start(bf16[64,1536]{1,0:T(8,128)(2,1)S(1)} %get-tuple-element.47), channel_id=1, source_target_pairs={{0,2},{1,3},{2,0},{3,1},{4,6},{5,7},{6,4},{7,5},{8,10},{9,11},{10,... | collective-permute-start | bytes 589832 | tf_op jit(solution)/shard_map/ppermute | solution.py:442
  44.8 24.7 %collective-permute-start.8 = (bf16[64,1536]{1,0:T(8,128)(2,1)S(1)}, bf16[64,1536]{1,0:T(8,128)(2,1)S(1)}, u32[]{:S(2)}, u32[]{:S(2)}) collective-permute-start(bf16[64,1536]{1,0:T(8,128)(2,1)S(1)} %get-tuple-element.48), channel_id=1, source_target_pairs={{0,3},{1,2},{2,1},{3,0},{4,7},{5,6},{6,5},{7,4},{8,11},{9,10},{10,... | collective-permute-start | bytes 589832 | tf_op jit(solution)/shard_map/ppermute | solution.py:442
  45.8 19.7 %collective-permute-start.11 = (bf16[64,2560]{1,0:T(8,128)(2,1)}, bf16[64,2560]{1,0:T(8,128)(2,1)S(1)}, u32[]{:S(2)}, u32[]{:S(2)}) collective-permute-start(bf16[64,2560]{1,0:T(8,128)(2,1)} %get-tuple-element.49), channel_id=1, source_target_pairs={{0,1},{3,2},{4,5},{7,6},{8,9},{11,10},{12,13},{15,14},{16,17},{19,... | collective-permute-start | bytes 983048 | tf_op jit(solution)/shard_map/ppermute | solution.py:442
  51.5 24.1 %collective-permute-start.6 = (bf16[64,4096]{1,0:T(8,128)(2,1)S(1)}, bf16[64,4096]{1,0:T(8,128)(2,1)S(1)}, u32[]{:S(2)}, u32[]{:S(2)}) collective-permute-start(bf16[64,4096]{1,0:T(8,128)(2,1)S(1)} %get-tuple-element.44), channel_id=1, source_target_pairs={{0,1},{1,0},{2,3},{3,2},{4,5},{5,4},{6,7},{7,6},{8,9},{9,8},{10,11... | collective-permute-start | bytes 1572872 | tf_op jit(solution)/shard_map/ppermute | solution.py:442
  55.4 20.1 %collective-permute-start.10 = (bf16[64,2560]{1,0:T(8,128)(2,1)S(1)}, bf16[64,2560]{1,0:T(8,128)(2,1)S(1)}, u32[]{:S(2)}, u32[]{:S(2)}) collective-permute-start(bf16[64,2560]{1,0:T(8,128)(2,1)S(1)} %add_convert_fusion.1), channel_id=1, source_target_pairs={{1,3},{2,0},{5,7},{6,4},{9,11},{10,8},{13,15},{14,12},{17,19},{18,... | collective-permute-start | bytes 983048 | tf_op jit(solution)/shard_map/ppermute | solution.py:442
  66.6 9.0 %collective-permute-start.12 = (bf16[64,2560]{1,0:T(8,128)(2,1)S(1)}, bf16[64,2560]{1,0:T(8,128)(2,1)S(1)}, u32[]{:S(2)}, u32[]{:S(2)}) collective-permute-start(bf16[64,2560]{1,0:T(8,128)(2,1)S(1)} %add_convert_fusion), channel_id=1, source_target_pairs={{1,2},{2,1},{5,6},{6,5},{9,10},{10,9},{13,14},{14,13},{17,18},{18,... | collective-permute-start | bytes 983048 | tf_op jit(solution)/shard_map/ppermute | solution.py:442

commit v4 on v3

--- a/solution.py
+++ b/solution.py
@@ -189,11 +189,11 @@
 
 def across_kernel(
     place_ref, local_ref, query_ref, after_ref, fix_ref, rate_ref, residue_ref, weight_ref,
-    right_two, right_three, mixed_ref,
+    right_ref, mixed_ref,
     coef,
 ):
     mix(place_ref, local_ref, query_ref, after_ref, fix_ref, rate_ref, residue_ref, mixed_ref, coef)
-    project(mixed_ref, weight_ref, None, [right_two, right_three])
+    project(mixed_ref, weight_ref, None, [right_ref])
 
 
 def left_kernel(mixed_ref, weight_hbm, left_two, left_three, weight_buf, sems):
@@ -445,15 +445,14 @@
         return [(j, j ^ step) for j in range(parts)]
 
     own_half, odd = mine // 2, mine % 2
-    right_two, right_three, mixed = pl.pallas_call(
+    right, mixed = pl.pallas_call(
         across_kernel,
         out_shape=(
-            jax.ShapeDtypeStruct((piece, right_side), BF16),
-            jax.ShapeDtypeStruct((piece, right_side), BF16),
+            jax.ShapeDtypeStruct((2 * piece, right_side), BF16),
             jax.ShapeDtypeStruct((2 * piece, channels), BF16),
         ),
         in_specs=[SMEM] + [VMEM] * 7,
-        out_specs=(VMEM,) * 3,
+        out_specs=(VMEM,) * 2,
         scratch_shapes=[pltpu.VMEM((STATE_ROWS, LANES), F32)],
         compiler_params=params,
         cost_estimate=light,
@@ -468,8 +467,7 @@
         compiler_params=params,
         cost_estimate=light,
     )(mixed, out_weight)
-    handed_three = sent_by(right_three, [(0, 1), (3, 2)])
-    handed_two = sent_by(right_two, [(0, 1), (3, 2)])
+    handed = sent_by(right, [(0, 1), (3, 2)])
     got_two, got_three = sent_by(left_two, across(2)), sent_by(left_three, across(3))
     beside, own = pl.pallas_call(
         own_kernel,
@@ -489,10 +487,9 @@
         cost_estimate=light,
     )(*half_inputs(own_half, 1 - odd), out_weight)
     got_one = sent_by(beside, across(1))
-    handed_three, _ = lax.optimization_barrier((handed_three, beside))
-    joined_two = (right_two.astype(F32) + handed_three.astype(F32)).astype(BF16)
-    handed_two, _ = lax.optimization_barrier((handed_two, joined_two))
-    joined_three = (right_three.astype(F32) + handed_two.astype(F32)).astype(BF16)
+    handed, _ = lax.optimization_barrier((handed, beside))
+    joined_two = (right[:piece].astype(F32) + handed[piece:].astype(F32)).astype(BF16)
+    joined_three = (right[piece:].astype(F32) + handed[:piece].astype(F32)).astype(BF16)
     far_two = sent_by(joined_two, [(1, 3), (2, 0)])
     far_three = sent_by(joined_three, [(1, 2), (2, 1)])
     left = got_two.astype(F32) + got_three.astype(F32)

time: 76.9 us -> 75.5 us (0.982)
  starting transfers between devices: 31.2 us -> 27.5 us
  waiting for transfers between devices: 20.9 us -> 24.1 us
  other arithmetic: 4.43 us -> 3.65 us
    ppermute x7 -> x6, starting transfers between devices: 15.5 us -> 11.8 us  [sent_by(): return lax.ppermute(block, 'chan', pairs)]
    ppermute x7 -> x6, waiting for transfers between devices: 13.7 us -> 16.8 us  [sent_by(): return lax.ppermute(block, 'chan', pairs)]
    convert_element_type x2 -> x1, other arithmetic: 2.2 us -> 1.42 us  [on_device(): (right[:piece].astype(F32) + handed[piece:].astype(F32)).astype(BF16)]
  transfers between devices with their start and end apart: 13 -> 12, of which waited for: 6 -> 7; matrix products, arithmetic and copies ran while one was open for 3% -> 2% of each run, Pallas kernels for 17% -> 18%
where the time goes in v4:
time: 75.5 us; the launch traced here: 75.3 us
  starting transfers between devices  27.5 us (36%)
  waiting for transfers between devices  24.1 us (32%)
  Pallas kernels  19.5 us (26%)
  other arithmetic  3.65 us (5%)
    ppermute x6, waiting for transfers between devices, sent_by(): return lax.ppermute(block, 'chan', pairs)  16.8 us
    ppermute x6, starting transfers between devices, scan_states(): got = lax.ppermute(sent, 'seq', [(j, j ^ mask) for j in range(count)])  15.7 us
    ppermute x6, starting transfers between devices, sent_by(): return lax.ppermute(block, 'chan', pairs)  11.8 us
    ppermute x6, waiting for transfers between devices, scan_states(): got = lax.ppermute(sent, 'seq', [(j, j ^ mask) for j in range(count)])  7.28 us
    pallas_call x1, Pallas kernels, on_device(): pl.pallas_call(own_kernel, out_shape=(jax.ShapeDtypeStruct((piece, column...  4.4 us
    pallas_call x1, Pallas kernels, on_device(): pl.pallas_call(state_kernel, out_shape=(jax.ShapeDtypeStruct((PAYLOAD, LA...  3.27 us
    pallas_call x1, Pallas kernels, on_device(): pl.pallas_call(across_kernel, out_shape=(jax.ShapeDtypeStruct((2 * piece,...  3.01 us
    pallas_call x1, Pallas kernels, local_part(): pl.pallas_call(local_kernel, out_shape=jax.ShapeDtypeStruct((rows, channe...  2.62 us
  transfers between devices with their start and end apart: 12, of which 7 were waited for; matrix products, arithmetic and copies ran while one was open for 2% of the time, Pallas kernels for 18%

profile of v4, /device:TPU:32, one launch (start us, length us, event | category | flops | bytes accessed | tf_op | source)
XLA Modules:
  0.0 75.3 jit_solution(4165303640490954608)
XLA Ops:
  0.0 3.3 %shard_map.82 = (f32[208,128]{1,0:T(8,128)S(1)}, bf16[208,128]{1,0:T(8,128)(2,1)S(1)}, f32[128,128]{1,0:T(8,128)S(1)}, f32[2112,128]{1,0:T(8,128)S(1)}, f32[72,1...) custom-call(bf16[256,1024]{1,0:T(8,128)(2,1)} %query_hbm.3, bf16[256,1024]{1,0:T(8,128)(2,1)} %key_hbm.1, ...), custom_call_target="tpu_custom_call" | custom-call | flops 20000000 | bytes 3000000 | tf_op jit(solution)/shard_map/pallas_call | solution.py:338
  3.4 1.2 %collective-permute-done = bf16[208,128]{1,0:T(8,128)(2,1)S(1)} collective-permute-done((bf16[208,128]{1,0:T(8,128)(2,1)S(1)}, bf16[208,128]{1,0:T(8,128)(2,1)S(1)}, u32[]{:S(2)}, u32[]{:S(2)}) %collective-permute-start) | collective-permute-done | bytes 53280 | tf_op jit(solution)/shard_map/ppermute | solution.py:287
  4.8 1.7 %collective-permute-start.1 = (bf16[208,128]{1,0:T(8,128)(2,1)S(1)}, bf16[208,128]{1,0:T(8,128)(2,1)S(1)}, u32[]{:S(2)}, u32[]{:S(2)}) collective-permute-start(bf16[208,128]{1,0:T(8,128)(2,1)S(1)} %maximum_bitcast_fusion), channel_id=1, source_target_pairs={{0,8},{4,12},{8,0},{12,4},{16,24},{20,28},{24,16},{28,20},{32,40},... | collective-permute-start | bytes 159752 | tf_op jit(solution)/shard_map/ppermute | solution.py:287
  6.4 2.6 %collective-permute-done.1 = bf16[208,128]{1,0:T(8,128)(2,1)S(1)} collective-permute-done((bf16[208,128]{1,0:T(8,128)(2,1)S(1)}, bf16[208,128]{1,0:T(8,128)(2,1)S(1)}, u32[]{:S(2)}, u32[]{:S(2)}) %collective-permute-start.1) | collective-permute-done | bytes 53280 | tf_op jit(solution)/shard_map/ppermute | solution.py:287
  9.2 3.1 %collective-permute-start.2 = (bf16[208,128]{1,0:T(8,128)(2,1)S(1)}, bf16[208,128]{1,0:T(8,128)(2,1)S(1)}, u32[]{:S(2)}, u32[]{:S(2)}) collective-permute-start(bf16[208,128]{1,0:T(8,128)(2,1)S(1)} %maximum_bitcast_fusion.1), channel_id=1, source_target_pairs={{0,24},{4,28},{8,16},{12,20},{16,8},{20,12},{24,0},{28,4},{32,56},... | collective-permute-start | bytes 159752 | tf_op jit(solution)/shard_map/ppermute | solution.py:287
  12.3 2.3 %collective-permute-done.2 = bf16[208,128]{1,0:T(8,128)(2,1)S(1)} collective-permute-done((bf16[208,128]{1,0:T(8,128)(2,1)S(1)}, bf16[208,128]{1,0:T(8,128)(2,1)S(1)}, u32[]{:S(2)}, u32[]{:S(2)}) %collective-permute-start.2) | collective-permute-done | bytes 53280 | tf_op jit(solution)/shard_map/ppermute | solution.py:287
  14.8 1.6 %collective-permute-start.3 = (bf16[208,128]{1,0:T(8,128)(2,1)S(1)}, bf16[208,128]{1,0:T(8,128)(2,1)S(1)}, u32[]{:S(2)}, u32[]{:S(2)}) collective-permute-start(bf16[208,128]{1,0:T(8,128)(2,1)S(1)} %maximum_bitcast_fusion.2), channel_id=1, source_target_pairs={{0,32},{4,36},{8,40},{12,44},{16,48},{20,52},{24,56},{28,60},{32,0... | collective-permute-start | bytes 159752 | tf_op jit(solution)/shard_map/ppermute | solution.py:287
  16.4 2.6 %shard_map.83.local_ref = f32[256,1024]{1,0:T(8,128)S(1)} custom-call(f32[2112,128]{1,0:T(8,128)S(1)} %get-tuple-element.33.gated_ref, f32[128,128]{1,0:T(8,128)S(1)} %get-tuple-element.27.rate_ref, f32[128,128]{1,0:T(8,128)S(1)} %get-tuple-element.34.residue_ref, f32[8,128]{1,0:T(8,128)S(1)} %get-tuple-element.35.skip_ref), custom_call_target="tpu_custom_call" | custom-call | flops 1000000 | bytes 100000 | tf_op jit(solution)/shard_map/pallas_call | solution.py:372
  19.2 2.8 %collective-permute-start.4 = (bf16[208,128]{1,0:T(8,128)(2,1)S(1)}, bf16[208,128]{1,0:T(8,128)(2,1)S(1)}, u32[]{:S(2)}, u32[]{:S(2)}) collective-permute-start(bf16[208,128]{1,0:T(8,128)(2,1)S(1)} %maximum_bitcast_fusion.3), channel_id=1, source_target_pairs={{0,96},{4,100},{8,104},{12,108},{16,112},{20,116},{24,120},{28,124... | collective-permute-start | bytes 159752 | tf_op jit(solution)/shard_map/ppermute | solution.py:287
  22.0 1.4 %shard_map.84.query_ref = f32[256,1024]{1,0:T(8,128)S(1)} custom-call(bf16[256,1024]{1,0:T(8,128)(2,1)} %query_hbm.3, f32[72,128]{1,0:T(8,128)S(1)} %get-tuple-element.38.taps_ref), custom_call_target="tpu_custom_call" | custom-call | flops 1000000 | bytes 100000 | tf_op jit(solution)/shard_map/pallas_call | solution.py:383
  23.4 1.2 %collective-permute-done.4 = bf16[208,128]{1,0:T(8,128)(2,1)S(1)} collective-permute-done((bf16[208,128]{1,0:T(8,128)(2,1)S(1)}, bf16[208,128]{1,0:T(8,128)(2,1)S(1)}, u32[]{:S(2)}, u32[]{:S(2)}) %collective-permute-start.4) | collective-permute-done | bytes 53280 | tf_op jit(solution)/shard_map/ppermute | solution.py:287
  24.8 6.4 %collective-permute-start.5 = (bf16[208,128]{1,0:T(8,128)(2,1)S(1)}, bf16[208,128]{1,0:T(8,128)(2,1)S(1)}, u32[]{:S(2)}, u32[]{:S(2)}) collective-permute-start(bf16[208,128]{1,0:T(8,128)(2,1)S(1)} %maximum_bitcast_fusion.4), channel_id=1, source_target_pairs={{0,128},{4,132},{8,136},{12,140},{16,144},{20,148},{24,152},{28,15... | collective-permute-start | bytes 159752 | tf_op jit(solution)/shard_map/ppermute | solution.py:287
  31.2 2.6 %shard_map.86.weight_ref = bf16[5,1024,512]{2,1,0:T(8,128)(2,1)S(1)} custom-call(bf16[1024,4096]{1,0:T(8,128)(2,1)} %weight_hbm.4), custom_call_target="tpu_custom_call" | custom-call | flops 1000000 | bytes 100000 | tf_op jit(solution)/shard_map/pallas_call | solution.py:398
  34.3 3.0 %shard_map.87 = (bf16[128,2560]{1,0:T(8,128)(2,1)}, bf16[128,1024]{1,0:T(8,128)(2,1)S(1)}) custom-call(s32[2]{0:T(128)S(1)} %pad_add_fusion.1.place_ref, f32[256,1024]{1,0:T(8,128)S(1)} %shard_map.83.local_ref, f32[256,1024]{1,0:T(8,128)S(1)} %shard_map.84.query_ref, f32[128,128]{1,0:T(8,128)S(1)} %fusion.43.after_ref, ...), custom_call_target="tpu_custom_call" | custom-call | flops 1000000 | bytes 100000 | tf_op jit(solution)/shard_map/pallas_call | solution.py:448
  37.3 1.3 %collective-permute-start.9 = (bf16[128,2560]{1,0:T(8,128)(2,1)}, bf16[128,2560]{1,0:T(8,128)(2,1)}, u32[]{:S(2)}, u32[]{:S(2)}) collective-permute-start(bf16[128,2560]{1,0:T(8,128)(2,1)} %get-tuple-element.47), channel_id=1, source_target_pairs={{0,1},{3,2},{4,5},{7,6},{8,9},{11,10},{12,13},{15,14},{16,17},{19,... | collective-permute-start | bytes 1966088 | tf_op jit(solution)/shard_map/ppermute | solution.py:442
  38.7 2.2 %shard_map.88 = (bf16[64,1536]{1,0:T(8,128)(2,1)S(1)}, bf16[64,1536]{1,0:T(8,128)(2,1)S(1)}) custom-call(bf16[128,1024]{1,0:T(8,128)(2,1)S(1)} %get-tuple-element.44.mixed_ref, bf16[1024,4096]{1,0:T(8,128)(2,1)} %weight_hbm.4), custom_call_target="tpu_custom_call" | custom-call | flops 1000000 | bytes 100000 | tf_op jit(solution)/shard_map/pallas_call | solution.py:461
  40.9 4.0 %collective-permute-start.7 = (bf16[64,1536]{1,0:T(8,128)(2,1)S(1)}, bf16[64,1536]{1,0:T(8,128)(2,1)S(1)}, u32[]{:S(2)}, u32[]{:S(2)}) collective-permute-start(bf16[64,1536]{1,0:T(8,128)(2,1)S(1)} %get-tuple-element.45), channel_id=1, source_target_pairs={{0,2},{1,3},{2,0},{3,1},{4,6},{5,7},{6,4},{7,5},{8,10},{9,11},{10,... | collective-permute-start | bytes 589832 | tf_op jit(solution)/shard_map/ppermute | solution.py:442
  46.0 4.4 %shard_map.85 = (bf16[64,4096]{1,0:T(8,128)(2,1)S(1)}, f32[64,4096]{1,0:T(8,128)S(1)}) custom-call(s32[2]{0:T(128)S(1)} %pad_add_fusion.place_ref, f32[256,1024]{1,0:T(8,128)S(1)} %shard_map.83.local_ref, f32[256,1024]{1,0:T(8,128)S(1)} %shard_map.84.query_ref, f32[128,128]{1,0:T(8,128)S(1)} %fusion.43.after_ref, f32[32,128]{1,0:T(8,128)S(1)} %pad_maximum_fusion.fix_ref, ...), custom_call_target="tpu_custom_call" | custom-call | flops 1000000 | bytes 100000 | tf_op jit(solution)/shard_map/pallas_call | solution.py:472
  51.0 6.2 %collective-permute-done.9 = bf16[128,2560]{1,0:T(8,128)(2,1)} collective-permute-done((bf16[128,2560]{1,0:T(8,128)(2,1)}, bf16[128,2560]{1,0:T(8,128)(2,1)}, u32[]{:S(2)}, u32[]{:S(2)}) %collective-permute-start.9) | collective-permute-done | bytes 655392 | tf_op jit(solution)/shard_map/ppermute | solution.py:442
  57.2 1.4 %add_convert_fusion.1 = (bf16[64,2560]{1,0:T(8,128)(2,1)S(1)}, bf16[64,2560]{1,0:T(8,128)(2,1)S(1)}) fusion(bf16[128,2560]{1,0:T(8,128)(2,1)} %collective-permute-done.9, bf16[128,2560]{1,0:T(8,128)(2,1)} %get-tuple-element.47), kind=kLoop, calls=%fused_computation.4 | loop fusion | flops 1310720 | bytes 1966080 | tf_op jit(solution)/shard_map/convert_element_type | solution.py:491
  58.6 1.9 %collective-permute-start.10 = (bf16[64,2560]{1,0:T(8,128)(2,1)S(1)}, bf16[64,2560]{1,0:T(8,128)(2,1)S(1)}, u32[]{:S(2)}, u32[]{:S(2)}) collective-permute-start(bf16[64,2560]{1,0:T(8,128)(2,1)S(1)} %get-tuple-element.75), channel_id=1, source_target_pairs={{1,3},{2,0},{5,7},{6,4},{9,11},{10,8},{13,15},{14,12},{17,19},{18,... | collective-permute-start | bytes 983048 | tf_op jit(solution)/shard_map/ppermute | solution.py:442
  60.6 2.9 %collective-permute-start.11 = (bf16[64,2560]{1,0:T(8,128)(2,1)S(1)}, bf16[64,2560]{1,0:T(8,128)(2,1)S(1)}, u32[]{:S(2)}, u32[]{:S(2)}) collective-permute-start(bf16[64,2560]{1,0:T(8,128)(2,1)S(1)} %get-tuple-element.76), channel_id=1, source_target_pairs={{1,2},{2,1},{5,6},{6,5},{9,10},{10,9},{13,14},{14,13},{17,18},{18,... | collective-permute-start | bytes 983048 | tf_op jit(solution)/shard_map/ppermute | solution.py:442
  63.6 5.7 %collective-permute-done.10 = bf16[64,2560]{1,0:T(8,128)(2,1)S(1)} collective-permute-done((bf16[64,2560]{1,0:T(8,128)(2,1)S(1)}, bf16[64,2560]{1,0:T(8,128)(2,1)S(1)}, u32[]{:S(2)}, u32[]{:S(2)}) %collective-permute-start.10) | collective-permute-done | bytes 327712 | tf_op jit(solution)/shard_map/ppermute | solution.py:442
  69.2 5.0 %collective-permute-done.11 = bf16[64,2560]{1,0:T(8,128)(2,1)S(1)} collective-permute-done((bf16[64,2560]{1,0:T(8,128)(2,1)S(1)}, bf16[64,2560]{1,0:T(8,128)(2,1)S(1)}, u32[]{:S(2)}, u32[]{:S(2)}) %collective-permute-start.11) | collective-permute-done | bytes 327712 | tf_op jit(solution)/shard_map/ppermute | solution.py:442
  (73 shorter events, 4.0 us)
Async XLA Ops:
  3.3 1.3 %collective-permute-start = (bf16[208,128]{1,0:T(8,128)(2,1)S(1)}, bf16[208,128]{1,0:T(8,128)(2,1)S(1)}, u32[]{:S(2)}, u32[]{:S(2)}) collective-permute-start(bf16[208,128]{1,0:T(8,128)(2,1)S(1)} %get-tuple-element.28), channel_id=1, source_target_pairs={{0,4},{4,0},{8,12},{12,8},{16,20},{20,16},{24,28},{28,24},{32,36},... | collective-permute-start | bytes 159752 | tf_op jit(solution)/shard_map/ppermute | solution.py:287
  4.6 11.7 %copy-start = (f32[208,128]{1,0:T(8,128)}, f32[208,128]{1,0:T(8,128)S(1)}, u32[]{:S(2)}) copy-start(f32[208,128]{1,0:T(8,128)S(1)} %convert_element_type.195) | copy-start | bytes 319492
  4.8 4.2 %collective-permute-start.1 = (bf16[208,128]{1,0:T(8,128)(2,1)S(1)}, bf16[208,128]{1,0:T(8,128)(2,1)S(1)}, u32[]{:S(2)}, u32[]{:S(2)}) collective-permute-start(bf16[208,128]{1,0:T(8,128)(2,1)S(1)} %maximum_bitcast_fusion), channel_id=1, source_target_pairs={{0,8},{4,12},{8,0},{12,4},{16,24},{20,28},{24,16},{28,20},{32,40},... | collective-permute-start | bytes 159752 | tf_op jit(solution)/shard_map/ppermute | solution.py:287
  9.0 7.4 %copy-start.4 = (f32[208,128]{1,0:T(8,128)}, f32[208,128]{1,0:T(8,128)S(1)}, u32[]{:S(2)}) copy-start(f32[208,128]{1,0:T(8,128)S(1)} %convert_element_type.201) | copy-start | bytes 319492
  9.2 5.4 %collective-permute-start.2 = (bf16[208,128]{1,0:T(8,128)(2,1)S(1)}, bf16[208,128]{1,0:T(8,128)(2,1)S(1)}, u32[]{:S(2)}, u32[]{:S(2)}) collective-permute-start(bf16[208,128]{1,0:T(8,128)(2,1)S(1)} %maximum_bitcast_fusion.1), channel_id=1, source_target_pairs={{0,24},{4,28},{8,16},{12,20},{16,8},{20,12},{24,0},{28,4},{32,56},... | collective-permute-start | bytes 159752 | tf_op jit(solution)/shard_map/ppermute | solution.py:287
  14.6 7.4 %copy-start.2 = (f32[208,128]{1,0:T(8,128)}, f32[208,128]{1,0:T(8,128)S(1)}, u32[]{:S(2)}) copy-start(f32[208,128]{1,0:T(8,128)S(1)} %convert_element_type.207) | copy-start | bytes 319492
  14.8 4.2 %collective-permute-start.3 = (bf16[208,128]{1,0:T(8,128)(2,1)S(1)}, bf16[208,128]{1,0:T(8,128)(2,1)S(1)}, u32[]{:S(2)}, u32[]{:S(2)}) collective-permute-start(bf16[208,128]{1,0:T(8,128)(2,1)S(1)} %maximum_bitcast_fusion.2), channel_id=1, source_target_pairs={{0,32},{4,36},{8,40},{12,44},{16,48},{20,52},{24,56},{28,60},{32,0... | collective-permute-start | bytes 159752 | tf_op jit(solution)/shard_map/ppermute | solution.py:287
  19.2 5.4 %collective-permute-start.4 = (bf16[208,128]{1,0:T(8,128)(2,1)S(1)}, bf16[208,128]{1,0:T(8,128)(2,1)S(1)}, u32[]{:S(2)}, u32[]{:S(2)}) collective-permute-start(bf16[208,128]{1,0:T(8,128)(2,1)S(1)} %maximum_bitcast_fusion.3), channel_id=1, source_target_pairs={{0,96},{4,100},{8,104},{12,108},{16,112},{20,116},{24,120},{28,124... | collective-permute-start | bytes 159752 | tf_op jit(solution)/shard_map/ppermute | solution.py:287
  24.8 9.1 %collective-permute-start.5 = (bf16[208,128]{1,0:T(8,128)(2,1)S(1)}, bf16[208,128]{1,0:T(8,128)(2,1)S(1)}, u32[]{:S(2)}, u32[]{:S(2)}) collective-permute-start(bf16[208,128]{1,0:T(8,128)(2,1)S(1)} %maximum_bitcast_fusion.4), channel_id=1, source_target_pairs={{0,128},{4,132},{8,136},{12,140},{16,144},{20,148},{24,152},{28,15... | collective-permute-start | bytes 159752 | tf_op jit(solution)/shard_map/ppermute | solution.py:287
  31.2 2.7 %copy-start.1 = (f32[208,128]{1,0:T(8,128)S(1)}, f32[208,128]{1,0:T(8,128)}, u32[]{:S(2)}) copy-start(f32[208,128]{1,0:T(8,128)} %copy-done) | copy-start | bytes 319492
  31.2 2.7 %copy-start.3 = (f32[208,128]{1,0:T(8,128)S(1)}, f32[208,128]{1,0:T(8,128)}, u32[]{:S(2)}) copy-start(f32[208,128]{1,0:T(8,128)} %copy-done.2) | copy-start | bytes 319492
  31.2 2.7 %copy-start.5 = (f32[208,128]{1,0:T(8,128)S(1)}, f32[208,128]{1,0:T(8,128)}, u32[]{:S(2)}) copy-start(f32[208,128]{1,0:T(8,128)} %copy-done.4) | copy-start | bytes 319492
  37.3 19.9 %collective-permute-start.9 = (bf16[128,2560]{1,0:T(8,128)(2,1)}, bf16[128,2560]{1,0:T(8,128)(2,1)}, u32[]{:S(2)}, u32[]{:S(2)}) collective-permute-start(bf16[128,2560]{1,0:T(8,128)(2,1)} %get-tuple-element.47), channel_id=1, source_target_pairs={{0,1},{3,2},{4,5},{7,6},{8,9},{11,10},{12,13},{15,14},{16,17},{19,... | collective-permute-start | bytes 1966088 | tf_op jit(solution)/shard_map/ppermute | solution.py:442
  40.9 22.6 %collective-permute-start.7 = (bf16[64,1536]{1,0:T(8,128)(2,1)S(1)}, bf16[64,1536]{1,0:T(8,128)(2,1)S(1)}, u32[]{:S(2)}, u32[]{:S(2)}) collective-permute-start(bf16[64,1536]{1,0:T(8,128)(2,1)S(1)} %get-tuple-element.45), channel_id=1, source_target_pairs={{0,2},{1,3},{2,0},{3,1},{4,6},{5,7},{6,4},{7,5},{8,10},{9,11},{10,... | collective-permute-start | bytes 589832 | tf_op jit(solution)/shard_map/ppermute | solution.py:442
  45.0 18.5 %collective-permute-start.8 = (bf16[64,1536]{1,0:T(8,128)(2,1)S(1)}, bf16[64,1536]{1,0:T(8,128)(2,1)S(1)}, u32[]{:S(2)}, u32[]{:S(2)}) collective-permute-start(bf16[64,1536]{1,0:T(8,128)(2,1)S(1)} %get-tuple-element.46), channel_id=1, source_target_pairs={{0,3},{1,2},{2,1},{3,0},{4,7},{5,6},{6,5},{7,4},{8,11},{9,10},{10,... | collective-permute-start | bytes 589832 | tf_op jit(solution)/shard_map/ppermute | solution.py:442
  50.4 23.9 %collective-permute-start.6 = (bf16[64,4096]{1,0:T(8,128)(2,1)S(1)}, bf16[64,4096]{1,0:T(8,128)(2,1)S(1)}, u32[]{:S(2)}, u32[]{:S(2)}) collective-permute-start(bf16[64,4096]{1,0:T(8,128)(2,1)S(1)} %get-tuple-element.42), channel_id=1, source_target_pairs={{0,1},{1,0},{2,3},{3,2},{4,5},{5,4},{6,7},{7,6},{8,9},{9,8},{10,11... | collective-permute-start | bytes 1572872 | tf_op jit(solution)/shard_map/ppermute | solution.py:442
  58.6 10.6 %collective-permute-start.10 = (bf16[64,2560]{1,0:T(8,128)(2,1)S(1)}, bf16[64,2560]{1,0:T(8,128)(2,1)S(1)}, u32[]{:S(2)}, u32[]{:S(2)}) collective-permute-start(bf16[64,2560]{1,0:T(8,128)(2,1)S(1)} %get-tuple-element.75), channel_id=1, source_target_pairs={{1,3},{2,0},{5,7},{6,4},{9,11},{10,8},{13,15},{14,12},{17,19},{18,... | collective-permute-start | bytes 983048 | tf_op jit(solution)/shard_map/ppermute | solution.py:442
  60.6 13.6 %collective-permute-start.11 = (bf16[64,2560]{1,0:T(8,128)(2,1)S(1)}, bf16[64,2560]{1,0:T(8,128)(2,1)S(1)}, u32[]{:S(2)}, u32[]{:S(2)}) collective-permute-start(bf16[64,2560]{1,0:T(8,128)(2,1)S(1)} %get-tuple-element.76), channel_id=1, source_target_pairs={{1,2},{2,1},{5,6},{6,5},{9,10},{10,9},{13,14},{14,13},{17,18},{18,... | collective-permute-start | bytes 983048 | tf_op jit(solution)/shard_map/ppermute | solution.py:442

commit v5 on v4

--- a/solution.py
+++ b/solution.py
@@ -487,8 +487,8 @@
         cost_estimate=light,
     )(*half_inputs(own_half, 1 - odd), out_weight)
     got_one = sent_by(beside, across(1))
-    handed, _ = lax.optimization_barrier((handed, beside))
     joined_two = (right[:piece].astype(F32) + handed[piece:].astype(F32)).astype(BF16)
+    handed, _ = lax.optimization_barrier((handed, joined_two))
     joined_three = (right[piece:].astype(F32) + handed[:piece].astype(F32)).astype(BF16)
     far_two = sent_by(joined_two, [(1, 3), (2, 0)])
     far_three = sent_by(joined_three, [(1, 2), (2, 1)])

time: 75.5 us -> 75.1 us (level)
  waiting for transfers between devices: 24.1 us -> 22 us
  other arithmetic: 3.65 us -> 4.53 us
    ppermute x6, waiting for transfers between devices: 16.8 us -> 14.8 us  [sent_by(): return lax.ppermute(block, 'chan', pairs)]
    convert_element_type x0 -> x1, other arithmetic: none -> 1.15 us  [on_device(): (right[piece:].astype(F32) + handed[:piece].astype(F32)).astype(BF16)]
  transfers between devices with their start and end apart: 12 -> 12, of which waited for: 7 -> 7; matrix products, arithmetic and copies ran while one was open for 2% -> 3% of each run, Pallas kernels for 18% -> 18%
where the time goes in v5:
time: 75.1 us; the launch traced here: 74.4 us
  starting transfers between devices  27.8 us (37%)
  waiting for transfers between devices  22 us (29%)
  Pallas kernels  19.5 us (26%)
  other arithmetic  4.53 us (6%)
    ppermute x6, starting transfers between devices, scan_states(): got = lax.ppermute(sent, 'seq', [(j, j ^ mask) for j in range(count)])  15.7 us
    ppermute x6, waiting for transfers between devices, sent_by(): return lax.ppermute(block, 'chan', pairs)  14.8 us
    ppermute x6, starting transfers between devices, sent_by(): return lax.ppermute(block, 'chan', pairs)  12.2 us
    ppermute x6, waiting for transfers between devices, scan_states(): got = lax.ppermute(sent, 'seq', [(j, j ^ mask) for j in range(count)])  7.28 us
    pallas_call x1, Pallas kernels, on_device(): pl.pallas_call(own_kernel, out_shape=(jax.ShapeDtypeStruct((piece, column...  4.4 us
    pallas_call x1, Pallas kernels, on_device(): pl.pallas_call(state_kernel, out_shape=(jax.ShapeDtypeStruct((PAYLOAD, LA...  3.27 us
    pallas_call x1, Pallas kernels, on_device(): pl.pallas_call(across_kernel, out_shape=(jax.ShapeDtypeStruct((2 * piece,...  2.99 us
    pallas_call x1, Pallas kernels, local_part(): pl.pallas_call(local_kernel, out_shape=jax.ShapeDtypeStruct((rows, channe...  2.62 us
  transfers between devices with their start and end apart: 12, of which 7 were waited for; matrix products, arithmetic and copies ran while one was open for 3% of the time, Pallas kernels for 18%

profile of v5, /device:TPU:32, one launch (start us, length us, event | category | flops | bytes accessed | tf_op | source)
XLA Modules:
  0.0 74.4 jit_solution(12731850430596236780)
XLA Ops:
  0.0 3.3 %shard_map.82 = (f32[208,128]{1,0:T(8,128)S(1)}, bf16[208,128]{1,0:T(8,128)(2,1)S(1)}, f32[128,128]{1,0:T(8,128)S(1)}, f32[2112,128]{1,0:T(8,128)S(1)}, f32[72,1...) custom-call(bf16[256,1024]{1,0:T(8,128)(2,1)} %query_hbm.3, bf16[256,1024]{1,0:T(8,128)(2,1)} %key_hbm.1, ...), custom_call_target="tpu_custom_call" | custom-call | flops 20000000 | bytes 3000000 | tf_op jit(solution)/shard_map/pallas_call | solution.py:338
  3.4 1.2 %collective-permute-done = bf16[208,128]{1,0:T(8,128)(2,1)S(1)} collective-permute-done((bf16[208,128]{1,0:T(8,128)(2,1)S(1)}, bf16[208,128]{1,0:T(8,128)(2,1)S(1)}, u32[]{:S(2)}, u32[]{:S(2)}) %collective-permute-start) | collective-permute-done | bytes 53280 | tf_op jit(solution)/shard_map/ppermute | solution.py:287
  4.8 1.7 %collective-permute-start.1 = (bf16[208,128]{1,0:T(8,128)(2,1)S(1)}, bf16[208,128]{1,0:T(8,128)(2,1)S(1)}, u32[]{:S(2)}, u32[]{:S(2)}) collective-permute-start(bf16[208,128]{1,0:T(8,128)(2,1)S(1)} %maximum_bitcast_fusion), channel_id=1, source_target_pairs={{0,8},{4,12},{8,0},{12,4},{16,24},{20,28},{24,16},{28,20},{32,40},... | collective-permute-start | bytes 159752 | tf_op jit(solution)/shard_map/ppermute | solution.py:287
  6.4 2.6 %collective-permute-done.1 = bf16[208,128]{1,0:T(8,128)(2,1)S(1)} collective-permute-done((bf16[208,128]{1,0:T(8,128)(2,1)S(1)}, bf16[208,128]{1,0:T(8,128)(2,1)S(1)}, u32[]{:S(2)}, u32[]{:S(2)}) %collective-permute-start.1) | collective-permute-done | bytes 53280 | tf_op jit(solution)/shard_map/ppermute | solution.py:287
  9.2 3.1 %collective-permute-start.2 = (bf16[208,128]{1,0:T(8,128)(2,1)S(1)}, bf16[208,128]{1,0:T(8,128)(2,1)S(1)}, u32[]{:S(2)}, u32[]{:S(2)}) collective-permute-start(bf16[208,128]{1,0:T(8,128)(2,1)S(1)} %maximum_bitcast_fusion.1), channel_id=1, source_target_pairs={{0,24},{4,28},{8,16},{12,20},{16,8},{20,12},{24,0},{28,4},{32,56},... | collective-permute-start | bytes 159752 | tf_op jit(solution)/shard_map/ppermute | solution.py:287
  12.3 2.3 %collective-permute-done.2 = bf16[208,128]{1,0:T(8,128)(2,1)S(1)} collective-permute-done((bf16[208,128]{1,0:T(8,128)(2,1)S(1)}, bf16[208,128]{1,0:T(8,128)(2,1)S(1)}, u32[]{:S(2)}, u32[]{:S(2)}) %collective-permute-start.2) | collective-permute-done | bytes 53280 | tf_op jit(solution)/shard_map/ppermute | solution.py:287
  14.8 1.6 %collective-permute-start.3 = (bf16[208,128]{1,0:T(8,128)(2,1)S(1)}, bf16[208,128]{1,0:T(8,128)(2,1)S(1)}, u32[]{:S(2)}, u32[]{:S(2)}) collective-permute-start(bf16[208,128]{1,0:T(8,128)(2,1)S(1)} %maximum_bitcast_fusion.2), channel_id=1, source_target_pairs={{0,32},{4,36},{8,40},{12,44},{16,48},{20,52},{24,56},{28,60},{32,0... | collective-permute-start | bytes 159752 | tf_op jit(solution)/shard_map/ppermute | solution.py:287
  16.4 2.6 %shard_map.83.local_ref = f32[256,1024]{1,0:T(8,128)S(1)} custom-call(f32[2112,128]{1,0:T(8,128)S(1)} %get-tuple-element.33.gated_ref, f32[128,128]{1,0:T(8,128)S(1)} %get-tuple-element.27.rate_ref, f32[128,128]{1,0:T(8,128)S(1)} %get-tuple-element.34.residue_ref, f32[8,128]{1,0:T(8,128)S(1)} %get-tuple-element.35.skip_ref), custom_call_target="tpu_custom_call" | custom-call | flops 1000000 | bytes 100000 | tf_op jit(solution)/shard_map/pallas_call | solution.py:372
  19.2 2.8 %collective-permute-start.4 = (bf16[208,128]{1,0:T(8,128)(2,1)S(1)}, bf16[208,128]{1,0:T(8,128)(2,1)S(1)}, u32[]{:S(2)}, u32[]{:S(2)}) collective-permute-start(bf16[208,128]{1,0:T(8,128)(2,1)S(1)} %maximum_bitcast_fusion.3), channel_id=1, source_target_pairs={{0,96},{4,100},{8,104},{12,108},{16,112},{20,116},{24,120},{28,124... | collective-permute-start | bytes 159752 | tf_op jit(solution)/shard_map/ppermute | solution.py:287
  22.0 1.4 %shard_map.84.query_ref = f32[256,1024]{1,0:T(8,128)S(1)} custom-call(bf16[256,1024]{1,0:T(8,128)(2,1)} %query_hbm.3, f32[72,128]{1,0:T(8,128)S(1)} %get-tuple-element.38.taps_ref), custom_call_target="tpu_custom_call" | custom-call | flops 1000000 | bytes 100000 | tf_op jit(solution)/shard_map/pallas_call | solution.py:383
  23.4 1.2 %collective-permute-done.4 = bf16[208,128]{1,0:T(8,128)(2,1)S(1)} collective-permute-done((bf16[208,128]{1,0:T(8,128)(2,1)S(1)}, bf16[208,128]{1,0:T(8,128)(2,1)S(1)}, u32[]{:S(2)}, u32[]{:S(2)}) %collective-permute-start.4) | collective-permute-done | bytes 53280 | tf_op jit(solution)/shard_map/ppermute | solution.py:287
  24.8 6.4 %collective-permute-start.5 = (bf16[208,128]{1,0:T(8,128)(2,1)S(1)}, bf16[208,128]{1,0:T(8,128)(2,1)S(1)}, u32[]{:S(2)}, u32[]{:S(2)}) collective-permute-start(bf16[208,128]{1,0:T(8,128)(2,1)S(1)} %maximum_bitcast_fusion.4), channel_id=1, source_target_pairs={{0,128},{4,132},{8,136},{12,140},{16,144},{20,148},{24,152},{28,15... | collective-permute-start | bytes 159752 | tf_op jit(solution)/shard_map/ppermute | solution.py:287
  31.2 2.6 %shard_map.86.weight_ref = bf16[5,1024,512]{2,1,0:T(8,128)(2,1)S(1)} custom-call(bf16[1024,4096]{1,0:T(8,128)(2,1)} %weight_hbm.4), custom_call_target="tpu_custom_call" | custom-call | flops 1000000 | bytes 100000 | tf_op jit(solution)/shard_map/pallas_call | solution.py:398
  34.3 3.0 %shard_map.87 = (bf16[128,2560]{1,0:T(8,128)(2,1)}, bf16[128,1024]{1,0:T(8,128)(2,1)S(1)}) custom-call(s32[2]{0:T(128)S(1)} %pad_add_fusion.1.place_ref, f32[256,1024]{1,0:T(8,128)S(1)} %shard_map.83.local_ref, f32[256,1024]{1,0:T(8,128)S(1)} %shard_map.84.query_ref, f32[128,128]{1,0:T(8,128)S(1)} %fusion.43.after_ref, ...), custom_call_target="tpu_custom_call" | custom-call | flops 1000000 | bytes 100000 | tf_op jit(solution)/shard_map/pallas_call | solution.py:448
  37.3 1.3 %collective-permute-start.9 = (bf16[128,2560]{1,0:T(8,128)(2,1)}, bf16[128,2560]{1,0:T(8,128)(2,1)}, u32[]{:S(2)}, u32[]{:S(2)}) collective-permute-start(bf16[128,2560]{1,0:T(8,128)(2,1)} %get-tuple-element.47), channel_id=1, source_target_pairs={{0,1},{3,2},{4,5},{7,6},{8,9},{11,10},{12,13},{15,14},{16,17},{19,... | collective-permute-start | bytes 1966088 | tf_op jit(solution)/shard_map/ppermute | solution.py:442
  38.7 2.2 %shard_map.88 = (bf16[64,1536]{1,0:T(8,128)(2,1)S(1)}, bf16[64,1536]{1,0:T(8,128)(2,1)S(1)}) custom-call(bf16[128,1024]{1,0:T(8,128)(2,1)S(1)} %get-tuple-element.44.mixed_ref, bf16[1024,4096]{1,0:T(8,128)(2,1)} %weight_hbm.4), custom_call_target="tpu_custom_call" | custom-call | flops 1000000 | bytes 100000 | tf_op jit(solution)/shard_map/pallas_call | solution.py:461
  42.0 4.8 %collective-permute-start.7 = (bf16[64,1536]{1,0:T(8,128)(2,1)S(1)}, bf16[64,1536]{1,0:T(8,128)(2,1)S(1)}, u32[]{:S(2)}, u32[]{:S(2)}) collective-permute-start(bf16[64,1536]{1,0:T(8,128)(2,1)S(1)} %get-tuple-element.45), channel_id=1, source_target_pairs={{0,2},{1,3},{2,0},{3,1},{4,6},{5,7},{6,4},{7,5},{8,10},{9,11},{10,... | collective-permute-start | bytes 589832 | tf_op jit(solution)/shard_map/ppermute | solution.py:442
  46.9 4.4 %shard_map.85 = (bf16[64,4096]{1,0:T(8,128)(2,1)S(1)}, f32[64,4096]{1,0:T(8,128)S(1)}) custom-call(s32[2]{0:T(128)S(1)} %pad_add_fusion.place_ref, f32[256,1024]{1,0:T(8,128)S(1)} %shard_map.83.local_ref, f32[256,1024]{1,0:T(8,128)S(1)} %shard_map.84.query_ref, f32[128,128]{1,0:T(8,128)S(1)} %fusion.43.after_ref, f32[32,128]{1,0:T(8,128)S(1)} %pad_maximum_fusion.fix_ref, ...), custom_call_target="tpu_custom_call" | custom-call | flops 1000000 | bytes 100000 | tf_op jit(solution)/shard_map/pallas_call | solution.py:472
  51.4 5.8 %collective-permute-done.9 = bf16[128,2560]{1,0:T(8,128)(2,1)} collective-permute-done((bf16[128,2560]{1,0:T(8,128)(2,1)}, bf16[128,2560]{1,0:T(8,128)(2,1)}, u32[]{:S(2)}, u32[]{:S(2)}) %collective-permute-start.9) | collective-permute-done | bytes 655392 | tf_op jit(solution)/shard_map/ppermute | solution.py:442
  58.3 1.9 %collective-permute-start.10 = (bf16[64,2560]{1,0:T(8,128)(2,1)S(1)}, bf16[64,2560]{1,0:T(8,128)(2,1)S(1)}, u32[]{:S(2)}, u32[]{:S(2)}) collective-permute-start(bf16[64,2560]{1,0:T(8,128)(2,1)S(1)} %add_convert_fusion.1), channel_id=1, source_target_pairs={{1,3},{2,0},{5,7},{6,4},{9,11},{10,8},{13,15},{14,12},{17,19},{18,... | collective-permute-start | bytes 983048 | tf_op jit(solution)/shard_map/ppermute | solution.py:442
  60.3 1.2 %add_convert_fusion = bf16[64,2560]{1,0:T(8,128)(2,1)S(1)} fusion(bf16[128,2560]{1,0:T(8,128)(2,1)} %collective-permute-done.9, bf16[128,2560]{1,0:T(8,128)(2,1)} %get-tuple-element.47), kind=kLoop, calls=%fused_computation.3 | loop fusion | flops 655360 | bytes 983040 | tf_op jit(solution)/shard_map/convert_element_type | solution.py:492
  61.4 2.9 %collective-permute-start.11 = (bf16[64,2560]{1,0:T(8,128)(2,1)S(1)}, bf16[64,2560]{1,0:T(8,128)(2,1)S(1)}, u32[]{:S(2)}, u32[]{:S(2)}) collective-permute-start(bf16[64,2560]{1,0:T(8,128)(2,1)S(1)} %add_convert_fusion), channel_id=1, source_target_pairs={{1,2},{2,1},{5,6},{6,5},{9,10},{10,9},{13,14},{14,13},{17,18},{18,... | collective-permute-start | bytes 983048 | tf_op jit(solution)/shard_map/ppermute | solution.py:442
  64.4 1.6 %collective-permute-done.7 = bf16[64,1536]{1,0:T(8,128)(2,1)S(1)} collective-permute-done((bf16[64,1536]{1,0:T(8,128)(2,1)S(1)}, bf16[64,1536]{1,0:T(8,128)(2,1)S(1)}, u32[]{:S(2)}, u32[]{:S(2)}) %collective-permute-start.7) | collective-permute-done | bytes 196640 | tf_op jit(solution)/shard_map/ppermute | solution.py:442
  66.0 7.3 %collective-permute-done.11 = bf16[64,2560]{1,0:T(8,128)(2,1)S(1)} collective-permute-done((bf16[64,2560]{1,0:T(8,128)(2,1)S(1)}, bf16[64,2560]{1,0:T(8,128)(2,1)S(1)}, u32[]{:S(2)}, u32[]{:S(2)}) %collective-permute-start.11) | collective-permute-done | bytes 327712 | tf_op jit(solution)/shard_map/ppermute | solution.py:442
  (74 shorter events, 4.7 us)
Async XLA Ops:
  3.3 1.3 %collective-permute-start = (bf16[208,128]{1,0:T(8,128)(2,1)S(1)}, bf16[208,128]{1,0:T(8,128)(2,1)S(1)}, u32[]{:S(2)}, u32[]{:S(2)}) collective-permute-start(bf16[208,128]{1,0:T(8,128)(2,1)S(1)} %get-tuple-element.28), channel_id=1, source_target_pairs={{0,4},{4,0},{8,12},{12,8},{16,20},{20,16},{24,28},{28,24},{32,36},... | collective-permute-start | bytes 159752 | tf_op jit(solution)/shard_map/ppermute | solution.py:287
  4.6 11.7 %copy-start = (f32[208,128]{1,0:T(8,128)}, f32[208,128]{1,0:T(8,128)S(1)}, u32[]{:S(2)}) copy-start(f32[208,128]{1,0:T(8,128)S(1)} %convert_element_type.195) | copy-start | bytes 319492
  4.8 4.2 %collective-permute-start.1 = (bf16[208,128]{1,0:T(8,128)(2,1)S(1)}, bf16[208,128]{1,0:T(8,128)(2,1)S(1)}, u32[]{:S(2)}, u32[]{:S(2)}) collective-permute-start(bf16[208,128]{1,0:T(8,128)(2,1)S(1)} %maximum_bitcast_fusion), channel_id=1, source_target_pairs={{0,8},{4,12},{8,0},{12,4},{16,24},{20,28},{24,16},{28,20},{32,40},... | collective-permute-start | bytes 159752 | tf_op jit(solution)/shard_map/ppermute | solution.py:287
  9.0 7.4 %copy-start.4 = (f32[208,128]{1,0:T(8,128)}, f32[208,128]{1,0:T(8,128)S(1)}, u32[]{:S(2)}) copy-start(f32[208,128]{1,0:T(8,128)S(1)} %convert_element_type.201) | copy-start | bytes 319492
  9.2 5.4 %collective-permute-start.2 = (bf16[208,128]{1,0:T(8,128)(2,1)S(1)}, bf16[208,128]{1,0:T(8,128)(2,1)S(1)}, u32[]{:S(2)}, u32[]{:S(2)}) collective-permute-start(bf16[208,128]{1,0:T(8,128)(2,1)S(1)} %maximum_bitcast_fusion.1), channel_id=1, source_target_pairs={{0,24},{4,28},{8,16},{12,20},{16,8},{20,12},{24,0},{28,4},{32,56},... | collective-permute-start | bytes 159752 | tf_op jit(solution)/shard_map/ppermute | solution.py:287
  14.6 7.4 %copy-start.2 = (f32[208,128]{1,0:T(8,128)}, f32[208,128]{1,0:T(8,128)S(1)}, u32[]{:S(2)}) copy-start(f32[208,128]{1,0:T(8,128)S(1)} %convert_element_type.207) | copy-start | bytes 319492
  14.8 4.2 %collective-permute-start.3 = (bf16[208,128]{1,0:T(8,128)(2,1)S(1)}, bf16[208,128]{1,0:T(8,128)(2,1)S(1)}, u32[]{:S(2)}, u32[]{:S(2)}) collective-permute-start(bf16[208,128]{1,0:T(8,128)(2,1)S(1)} %maximum_bitcast_fusion.2), channel_id=1, source_target_pairs={{0,32},{4,36},{8,40},{12,44},{16,48},{20,52},{24,56},{28,60},{32,0... | collective-permute-start | bytes 159752 | tf_op jit(solution)/shard_map/ppermute | solution.py:287
  19.2 5.4 %collective-permute-start.4 = (bf16[208,128]{1,0:T(8,128)(2,1)S(1)}, bf16[208,128]{1,0:T(8,128)(2,1)S(1)}, u32[]{:S(2)}, u32[]{:S(2)}) collective-permute-start(bf16[208,128]{1,0:T(8,128)(2,1)S(1)} %maximum_bitcast_fusion.3), channel_id=1, source_target_pairs={{0,96},{4,100},{8,104},{12,108},{16,112},{20,116},{24,120},{28,124... | collective-permute-start | bytes 159752 | tf_op jit(solution)/shard_map/ppermute | solution.py:287
  24.8 9.1 %collective-permute-start.5 = (bf16[208,128]{1,0:T(8,128)(2,1)S(1)}, bf16[208,128]{1,0:T(8,128)(2,1)S(1)}, u32[]{:S(2)}, u32[]{:S(2)}) collective-permute-start(bf16[208,128]{1,0:T(8,128)(2,1)S(1)} %maximum_bitcast_fusion.4), channel_id=1, source_target_pairs={{0,128},{4,132},{8,136},{12,140},{16,144},{20,148},{24,152},{28,15... | collective-permute-start | bytes 159752 | tf_op jit(solution)/shard_map/ppermute | solution.py:287
  31.2 2.7 %copy-start.1 = (f32[208,128]{1,0:T(8,128)S(1)}, f32[208,128]{1,0:T(8,128)}, u32[]{:S(2)}) copy-start(f32[208,128]{1,0:T(8,128)} %copy-done) | copy-start | bytes 319492
  31.2 2.7 %copy-start.3 = (f32[208,128]{1,0:T(8,128)S(1)}, f32[208,128]{1,0:T(8,128)}, u32[]{:S(2)}) copy-start(f32[208,128]{1,0:T(8,128)} %copy-done.2) | copy-start | bytes 319492
  31.2 2.7 %copy-start.5 = (f32[208,128]{1,0:T(8,128)S(1)}, f32[208,128]{1,0:T(8,128)}, u32[]{:S(2)}) copy-start(f32[208,128]{1,0:T(8,128)} %copy-done.4) | copy-start | bytes 319492
  37.3 19.9 %collective-permute-start.9 = (bf16[128,2560]{1,0:T(8,128)(2,1)}, bf16[128,2560]{1,0:T(8,128)(2,1)}, u32[]{:S(2)}, u32[]{:S(2)}) collective-permute-start(bf16[128,2560]{1,0:T(8,128)(2,1)} %get-tuple-element.47), channel_id=1, source_target_pairs={{0,1},{3,2},{4,5},{7,6},{8,9},{11,10},{12,13},{15,14},{16,17},{19,... | collective-permute-start | bytes 1966088 | tf_op jit(solution)/shard_map/ppermute | solution.py:442
  40.9 23.4 %collective-permute-start.8 = (bf16[64,1536]{1,0:T(8,128)(2,1)S(1)}, bf16[64,1536]{1,0:T(8,128)(2,1)S(1)}, u32[]{:S(2)}, u32[]{:S(2)}) collective-permute-start(bf16[64,1536]{1,0:T(8,128)(2,1)S(1)} %get-tuple-element.46), channel_id=1, source_target_pairs={{0,3},{1,2},{2,1},{3,0},{4,7},{5,6},{6,5},{7,4},{8,11},{9,10},{10,... | collective-permute-start | bytes 589832 | tf_op jit(solution)/shard_map/ppermute | solution.py:442
  42.0 23.9 %collective-permute-start.7 = (bf16[64,1536]{1,0:T(8,128)(2,1)S(1)}, bf16[64,1536]{1,0:T(8,128)(2,1)S(1)}, u32[]{:S(2)}, u32[]{:S(2)}) collective-permute-start(bf16[64,1536]{1,0:T(8,128)(2,1)S(1)} %get-tuple-element.45), channel_id=1, source_target_pairs={{0,2},{1,3},{2,0},{3,1},{4,6},{5,7},{6,4},{7,5},{8,10},{9,11},{10,... | collective-permute-start | bytes 589832 | tf_op jit(solution)/shard_map/ppermute | solution.py:442
  51.3 22.2 %collective-permute-start.6 = (bf16[64,4096]{1,0:T(8,128)(2,1)S(1)}, bf16[64,4096]{1,0:T(8,128)(2,1)S(1)}, u32[]{:S(2)}, u32[]{:S(2)}) collective-permute-start(bf16[64,4096]{1,0:T(8,128)(2,1)S(1)} %get-tuple-element.42), channel_id=1, source_target_pairs={{0,1},{1,0},{2,3},{3,2},{4,5},{5,4},{6,7},{7,6},{8,9},{9,8},{10,11... | collective-permute-start | bytes 1572872 | tf_op jit(solution)/shard_map/ppermute | solution.py:442
  58.3 15.0 %collective-permute-start.10 = (bf16[64,2560]{1,0:T(8,128)(2,1)S(1)}, bf16[64,2560]{1,0:T(8,128)(2,1)S(1)}, u32[]{:S(2)}, u32[]{:S(2)}) collective-permute-start(bf16[64,2560]{1,0:T(8,128)(2,1)S(1)} %add_convert_fusion.1), channel_id=1, source_target_pairs={{1,3},{2,0},{5,7},{6,4},{9,11},{10,8},{13,15},{14,12},{17,19},{18,... | collective-permute-start | bytes 983048 | tf_op jit(solution)/shard_map/ppermute | solution.py:442
  61.4 11.9 %collective-permute-start.11 = (bf16[64,2560]{1,0:T(8,128)(2,1)S(1)}, bf16[64,2560]{1,0:T(8,128)(2,1)S(1)}, u32[]{:S(2)}, u32[]{:S(2)}) collective-permute-start(bf16[64,2560]{1,0:T(8,128)(2,1)S(1)} %add_convert_fusion), channel_id=1, source_target_pairs={{1,2},{2,1},{5,6},{6,5},{9,10},{10,9},{13,14},{14,13},{17,18},{18,... | collective-permute-start | bytes 983048 | tf_op jit(solution)/shard_map/ppermute | solution.py:442

commit v6 on v5

--- a/solution.py
+++ b/solution.py
@@ -217,8 +217,11 @@
     base = place_ref[0]
     swap = place_ref[1]
     before = (base - 1).astype(F32)
-    coef[...] = residue_ref[...] * after_ref[...] * jnp.exp(-rate_ref[...] * before)
+    coef[0:STATE_ROWS, :] = residue_ref[...] * after_ref[...] * jnp.exp(-rate_ref[...] * before)
+    for k in range(4):
+        coef[(k + 1) * STATE_ROWS : (k + 2) * STATE_ROWS, :] = jnp.exp(-rate_ref[...] * float(1 << k))
     phase = lax.broadcasted_iota(jnp.int32, (SUB, LANES), 0)
+    bits = [((phase >> k) & 1) == 1 for k in range(3)]
     at_start = base == 0
     row_zero = jnp.logical_and(phase == 0, at_start)
     row_one = jnp.logical_and(phase == 1, at_start)
@@ -228,9 +231,13 @@
         carry, decay = [], []
         for m in range(MODES):
             line = slice(m * SUB + group, m * SUB + group + 1)
-            rate = rate_ref[line, :]
-            carry.append(jnp.exp(-rate * phase.astype(F32)) * coef[line, :])
-            decay.append(jnp.broadcast_to(jnp.exp(-rate * float(SUB)), (SUB, LANES)))
+            head = jnp.broadcast_to(coef[line, :], (SUB, LANES))
+            for k in range(3):
+                row = (k + 1) * STATE_ROWS + m * SUB + group
+                head = jnp.where(bits[k], head * coef[row : row + 1, :], head)
+            carry.append(head)
+            row = 4 * STATE_ROWS + m * SUB + group
+            decay.append(jnp.broadcast_to(coef[row : row + 1, :], (SUB, LANES)))
 
         def fix(i):
             return jnp.broadcast_to(fix_ref[i * SUB + group : i * SUB + group + 1, :], (SUB, LANES))
@@ -453,7 +460,7 @@
         ),
         in_specs=[SMEM] + [VMEM] * 7,
         out_specs=(VMEM,) * 2,
-        scratch_shapes=[pltpu.VMEM((STATE_ROWS, LANES), F32)],
+        scratch_shapes=[pltpu.VMEM((5 * STATE_ROWS, LANES), F32)],
         compiler_params=params,
         cost_estimate=light,
     )(*half_inputs(1 - own_half, odd), aside["right"])
@@ -479,7 +486,7 @@
         out_specs=(VMEM,) * 2,
         scratch_shapes=[
             pltpu.VMEM((2 * piece, channels), BF16),
-            pltpu.VMEM((STATE_ROWS, LANES), F32),
+            pltpu.VMEM((5 * STATE_ROWS, LANES), F32),
             pltpu.VMEM((tiles, channels, COLUMN_TILE), BF16),
             dma((tiles,)),
         ],

time: 75.1 us -> 75 us (level)
  no operation moved by 1% of the time
where the time goes in v6:
time: 75 us; the launch traced here: 74.3 us
  starting transfers between devices  27.8 us (37%)
  waiting for transfers between devices  22 us (29%)
  Pallas kernels  19.5 us (26%)
  other arithmetic  4.53 us (6%)
    ppermute x6, starting transfers between devices, scan_states(): got = lax.ppermute(sent, 'seq', [(j, j ^ mask) for j in range(count)])  15.7 us
    ppermute x6, waiting for transfers between devices, sent_by(): return lax.ppermute(block, 'chan', pairs)  14.7 us
    ppermute x6, starting transfers between devices, sent_by(): return lax.ppermute(block, 'chan', pairs)  12.2 us
    ppermute x6, waiting for transfers between devices, scan_states(): got = lax.ppermute(sent, 'seq', [(j, j ^ mask) for j in range(count)])  7.28 us
    pallas_call x1, Pallas kernels, on_device(): pl.pallas_call(own_kernel, out_shape=(jax.ShapeDtypeStruct((piece, column...  4.4 us
    pallas_call x1, Pallas kernels, on_device(): pl.pallas_call(state_kernel, out_shape=(jax.ShapeDtypeStruct((PAYLOAD, LA...  3.27 us
    pallas_call x1, Pallas kernels, on_device(): pl.pallas_call(across_kernel, out_shape=(jax.ShapeDtypeStruct((2 * piece,...  2.96 us
    pallas_call x1, Pallas kernels, local_part(): pl.pallas_call(local_kernel, out_shape=jax.ShapeDtypeStruct((rows, channe...  2.62 us
  transfers between devices with their start and end apart: 12, of which 7 were waited for; matrix products, arithmetic and copies ran while one was open for 3% of the time, Pallas kernels for 18%

profile of v6, /device:TPU:32, one launch (start us, length us, event | category | flops | bytes accessed | tf_op | source)
XLA Modules:
  0.0 74.3 jit_solution(2624275678199625349)
XLA Ops:
  0.0 3.3 %shard_map.82 = (f32[208,128]{1,0:T(8,128)S(1)}, bf16[208,128]{1,0:T(8,128)(2,1)S(1)}, f32[128,128]{1,0:T(8,128)S(1)}, f32[2112,128]{1,0:T(8,128)S(1)}, f32[72,1...) custom-call(bf16[256,1024]{1,0:T(8,128)(2,1)} %query_hbm.3, bf16[256,1024]{1,0:T(8,128)(2,1)} %key_hbm.1, ...), custom_call_target="tpu_custom_call" | custom-call | flops 20000000 | bytes 3000000 | tf_op jit(solution)/shard_map/pallas_call | solution.py:345
  3.4 1.2 %collective-permute-done = bf16[208,128]{1,0:T(8,128)(2,1)S(1)} collective-permute-done((bf16[208,128]{1,0:T(8,128)(2,1)S(1)}, bf16[208,128]{1,0:T(8,128)(2,1)S(1)}, u32[]{:S(2)}, u32[]{:S(2)}) %collective-permute-start) | collective-permute-done | bytes 53280 | tf_op jit(solution)/shard_map/ppermute | solution.py:294
  4.8 1.7 %collective-permute-start.1 = (bf16[208,128]{1,0:T(8,128)(2,1)S(1)}, bf16[208,128]{1,0:T(8,128)(2,1)S(1)}, u32[]{:S(2)}, u32[]{:S(2)}) collective-permute-start(bf16[208,128]{1,0:T(8,128)(2,1)S(1)} %maximum_bitcast_fusion), channel_id=1, source_target_pairs={{0,8},{4,12},{8,0},{12,4},{16,24},{20,28},{24,16},{28,20},{32,40},... | collective-permute-start | bytes 159752 | tf_op jit(solution)/shard_map/ppermute | solution.py:294
  6.4 2.6 %collective-permute-done.1 = bf16[208,128]{1,0:T(8,128)(2,1)S(1)} collective-permute-done((bf16[208,128]{1,0:T(8,128)(2,1)S(1)}, bf16[208,128]{1,0:T(8,128)(2,1)S(1)}, u32[]{:S(2)}, u32[]{:S(2)}) %collective-permute-start.1) | collective-permute-done | bytes 53280 | tf_op jit(solution)/shard_map/ppermute | solution.py:294
  9.2 3.1 %collective-permute-start.2 = (bf16[208,128]{1,0:T(8,128)(2,1)S(1)}, bf16[208,128]{1,0:T(8,128)(2,1)S(1)}, u32[]{:S(2)}, u32[]{:S(2)}) collective-permute-start(bf16[208,128]{1,0:T(8,128)(2,1)S(1)} %maximum_bitcast_fusion.1), channel_id=1, source_target_pairs={{0,24},{4,28},{8,16},{12,20},{16,8},{20,12},{24,0},{28,4},{32,56},... | collective-permute-start | bytes 159752 | tf_op jit(solution)/shard_map/ppermute | solution.py:294
  12.3 2.3 %collective-permute-done.2 = bf16[208,128]{1,0:T(8,128)(2,1)S(1)} collective-permute-done((bf16[208,128]{1,0:T(8,128)(2,1)S(1)}, bf16[208,128]{1,0:T(8,128)(2,1)S(1)}, u32[]{:S(2)}, u32[]{:S(2)}) %collective-permute-start.2) | collective-permute-done | bytes 53280 | tf_op jit(solution)/shard_map/ppermute | solution.py:294
  14.8 1.6 %collective-permute-start.3 = (bf16[208,128]{1,0:T(8,128)(2,1)S(1)}, bf16[208,128]{1,0:T(8,128)(2,1)S(1)}, u32[]{:S(2)}, u32[]{:S(2)}) collective-permute-start(bf16[208,128]{1,0:T(8,128)(2,1)S(1)} %maximum_bitcast_fusion.2), channel_id=1, source_target_pairs={{0,32},{4,36},{8,40},{12,44},{16,48},{20,52},{24,56},{28,60},{32,0... | collective-permute-start | bytes 159752 | tf_op jit(solution)/shard_map/ppermute | solution.py:294
  16.4 2.6 %shard_map.83.local_ref = f32[256,1024]{1,0:T(8,128)S(1)} custom-call(f32[2112,128]{1,0:T(8,128)S(1)} %get-tuple-element.33.gated_ref, f32[128,128]{1,0:T(8,128)S(1)} %get-tuple-element.27.rate_ref, f32[128,128]{1,0:T(8,128)S(1)} %get-tuple-element.34.residue_ref, f32[8,128]{1,0:T(8,128)S(1)} %get-tuple-element.35.skip_ref), custom_call_target="tpu_custom_call" | custom-call | flops 1000000 | bytes 100000 | tf_op jit(solution)/shard_map/pallas_call | solution.py:379
  19.2 2.8 %collective-permute-start.4 = (bf16[208,128]{1,0:T(8,128)(2,1)S(1)}, bf16[208,128]{1,0:T(8,128)(2,1)S(1)}, u32[]{:S(2)}, u32[]{:S(2)}) collective-permute-start(bf16[208,128]{1,0:T(8,128)(2,1)S(1)} %maximum_bitcast_fusion.3), channel_id=1, source_target_pairs={{0,96},{4,100},{8,104},{12,108},{16,112},{20,116},{24,120},{28,124... | collective-permute-start | bytes 159752 | tf_op jit(solution)/shard_map/ppermute | solution.py:294
  22.0 1.4 %shard_map.84.query_ref = f32[256,1024]{1,0:T(8,128)S(1)} custom-call(bf16[256,1024]{1,0:T(8,128)(2,1)} %query_hbm.3, f32[72,128]{1,0:T(8,128)S(1)} %get-tuple-element.38.taps_ref), custom_call_target="tpu_custom_call" | custom-call | flops 1000000 | bytes 100000 | tf_op jit(solution)/shard_map/pallas_call | solution.py:390
  23.4 1.2 %collective-permute-done.4 = bf16[208,128]{1,0:T(8,128)(2,1)S(1)} collective-permute-done((bf16[208,128]{1,0:T(8,128)(2,1)S(1)}, bf16[208,128]{1,0:T(8,128)(2,1)S(1)}, u32[]{:S(2)}, u32[]{:S(2)}) %collective-permute-start.4) | collective-permute-done | bytes 53280 | tf_op jit(solution)/shard_map/ppermute | solution.py:294
  24.8 6.4 %collective-permute-start.5 = (bf16[208,128]{1,0:T(8,128)(2,1)S(1)}, bf16[208,128]{1,0:T(8,128)(2,1)S(1)}, u32[]{:S(2)}, u32[]{:S(2)}) collective-permute-start(bf16[208,128]{1,0:T(8,128)(2,1)S(1)} %maximum_bitcast_fusion.4), channel_id=1, source_target_pairs={{0,128},{4,132},{8,136},{12,140},{16,144},{20,148},{24,152},{28,15... | collective-permute-start | bytes 159752 | tf_op jit(solution)/shard_map/ppermute | solution.py:294
  31.2 2.6 %shard_map.86.weight_ref = bf16[5,1024,512]{2,1,0:T(8,128)(2,1)S(1)} custom-call(bf16[1024,4096]{1,0:T(8,128)(2,1)} %weight_hbm.4), custom_call_target="tpu_custom_call" | custom-call | flops 1000000 | bytes 100000 | tf_op jit(solution)/shard_map/pallas_call | solution.py:405
  34.3 3.0 %shard_map.87 = (bf16[128,2560]{1,0:T(8,128)(2,1)}, bf16[128,1024]{1,0:T(8,128)(2,1)S(1)}) custom-call(s32[2]{0:T(128)S(1)} %pad_add_fusion.1.place_ref, f32[256,1024]{1,0:T(8,128)S(1)} %shard_map.83.local_ref, f32[256,1024]{1,0:T(8,128)S(1)} %shard_map.84.query_ref, f32[128,128]{1,0:T(8,128)S(1)} %fusion.43.after_ref, ...), custom_call_target="tpu_custom_call" | custom-call | flops 1000000 | bytes 100000 | tf_op jit(solution)/shard_map/pallas_call | solution.py:455
  37.3 1.3 %collective-permute-start.9 = (bf16[128,2560]{1,0:T(8,128)(2,1)}, bf16[128,2560]{1,0:T(8,128)(2,1)}, u32[]{:S(2)}, u32[]{:S(2)}) collective-permute-start(bf16[128,2560]{1,0:T(8,128)(2,1)} %get-tuple-element.47), channel_id=1, source_target_pairs={{0,1},{3,2},{4,5},{7,6},{8,9},{11,10},{12,13},{15,14},{16,17},{19,... | collective-permute-start | bytes 1966088 | tf_op jit(solution)/shard_map/ppermute | solution.py:449
  38.7 2.2 %shard_map.88 = (bf16[64,1536]{1,0:T(8,128)(2,1)S(1)}, bf16[64,1536]{1,0:T(8,128)(2,1)S(1)}) custom-call(bf16[128,1024]{1,0:T(8,128)(2,1)S(1)} %get-tuple-element.44.mixed_ref, bf16[1024,4096]{1,0:T(8,128)(2,1)} %weight_hbm.4), custom_call_target="tpu_custom_call" | custom-call | flops 1000000 | bytes 100000 | tf_op jit(solution)/shard_map/pallas_call | solution.py:468
  42.0 4.8 %collective-permute-start.7 = (bf16[64,1536]{1,0:T(8,128)(2,1)S(1)}, bf16[64,1536]{1,0:T(8,128)(2,1)S(1)}, u32[]{:S(2)}, u32[]{:S(2)}) collective-permute-start(bf16[64,1536]{1,0:T(8,128)(2,1)S(1)} %get-tuple-element.45), channel_id=1, source_target_pairs={{0,2},{1,3},{2,0},{3,1},{4,6},{5,7},{6,4},{7,5},{8,10},{9,11},{10,... | collective-permute-start | bytes 589832 | tf_op jit(solution)/shard_map/ppermute | solution.py:449
  46.8 4.4 %shard_map.85 = (bf16[64,4096]{1,0:T(8,128)(2,1)S(1)}, f32[64,4096]{1,0:T(8,128)S(1)}) custom-call(s32[2]{0:T(128)S(1)} %pad_add_fusion.place_ref, f32[256,1024]{1,0:T(8,128)S(1)} %shard_map.83.local_ref, f32[256,1024]{1,0:T(8,128)S(1)} %shard_map.84.query_ref, f32[128,128]{1,0:T(8,128)S(1)} %fusion.43.after_ref, f32[32,128]{1,0:T(8,128)S(1)} %pad_maximum_fusion.fix_ref, ...), custom_call_target="tpu_custom_call" | custom-call | flops 1000000 | bytes 100000 | tf_op jit(solution)/shard_map/pallas_call | solution.py:479
  51.3 5.8 %collective-permute-done.9 = bf16[128,2560]{1,0:T(8,128)(2,1)} collective-permute-done((bf16[128,2560]{1,0:T(8,128)(2,1)}, bf16[128,2560]{1,0:T(8,128)(2,1)}, u32[]{:S(2)}, u32[]{:S(2)}) %collective-permute-start.9) | collective-permute-done | bytes 655392 | tf_op jit(solution)/shard_map/ppermute | solution.py:449
  58.3 1.9 %collective-permute-start.10 = (bf16[64,2560]{1,0:T(8,128)(2,1)S(1)}, bf16[64,2560]{1,0:T(8,128)(2,1)S(1)}, u32[]{:S(2)}, u32[]{:S(2)}) collective-permute-start(bf16[64,2560]{1,0:T(8,128)(2,1)S(1)} %add_convert_fusion.1), channel_id=1, source_target_pairs={{1,3},{2,0},{5,7},{6,4},{9,11},{10,8},{13,15},{14,12},{17,19},{18,... | collective-permute-start | bytes 983048 | tf_op jit(solution)/shard_map/ppermute | solution.py:449
  60.2 1.2 %add_convert_fusion = bf16[64,2560]{1,0:T(8,128)(2,1)S(1)} fusion(bf16[128,2560]{1,0:T(8,128)(2,1)} %collective-permute-done.9, bf16[128,2560]{1,0:T(8,128)(2,1)} %get-tuple-element.47), kind=kLoop, calls=%fused_computation.3 | loop fusion | flops 655360 | bytes 983040 | tf_op jit(solution)/shard_map/convert_element_type | solution.py:499
  61.4 2.9 %collective-permute-start.11 = (bf16[64,2560]{1,0:T(8,128)(2,1)S(1)}, bf16[64,2560]{1,0:T(8,128)(2,1)S(1)}, u32[]{:S(2)}, u32[]{:S(2)}) collective-permute-start(bf16[64,2560]{1,0:T(8,128)(2,1)S(1)} %add_convert_fusion), channel_id=1, source_target_pairs={{1,2},{2,1},{5,6},{6,5},{9,10},{10,9},{13,14},{14,13},{17,18},{18,... | collective-permute-start | bytes 983048 | tf_op jit(solution)/shard_map/ppermute | solution.py:449
  64.3 1.6 %collective-permute-done.7 = bf16[64,1536]{1,0:T(8,128)(2,1)S(1)} collective-permute-done((bf16[64,1536]{1,0:T(8,128)(2,1)S(1)}, bf16[64,1536]{1,0:T(8,128)(2,1)S(1)}, u32[]{:S(2)}, u32[]{:S(2)}) %collective-permute-start.7) | collective-permute-done | bytes 196640 | tf_op jit(solution)/shard_map/ppermute | solution.py:449
  66.0 7.3 %collective-permute-done.11 = bf16[64,2560]{1,0:T(8,128)(2,1)S(1)} collective-permute-done((bf16[64,2560]{1,0:T(8,128)(2,1)S(1)}, bf16[64,2560]{1,0:T(8,128)(2,1)S(1)}, u32[]{:S(2)}, u32[]{:S(2)}) %collective-permute-start.11) | collective-permute-done | bytes 327712 | tf_op jit(solution)/shard_map/ppermute | solution.py:449
  (74 shorter events, 4.7 us)
Async XLA Ops:
  3.3 1.3 %collective-permute-start = (bf16[208,128]{1,0:T(8,128)(2,1)S(1)}, bf16[208,128]{1,0:T(8,128)(2,1)S(1)}, u32[]{:S(2)}, u32[]{:S(2)}) collective-permute-start(bf16[208,128]{1,0:T(8,128)(2,1)S(1)} %get-tuple-element.28), channel_id=1, source_target_pairs={{0,4},{4,0},{8,12},{12,8},{16,20},{20,16},{24,28},{28,24},{32,36},... | collective-permute-start | bytes 159752 | tf_op jit(solution)/shard_map/ppermute | solution.py:294
  4.6 11.7 %copy-start = (f32[208,128]{1,0:T(8,128)}, f32[208,128]{1,0:T(8,128)S(1)}, u32[]{:S(2)}) copy-start(f32[208,128]{1,0:T(8,128)S(1)} %convert_element_type.195) | copy-start | bytes 319492
  4.8 4.2 %collective-permute-start.1 = (bf16[208,128]{1,0:T(8,128)(2,1)S(1)}, bf16[208,128]{1,0:T(8,128)(2,1)S(1)}, u32[]{:S(2)}, u32[]{:S(2)}) collective-permute-start(bf16[208,128]{1,0:T(8,128)(2,1)S(1)} %maximum_bitcast_fusion), channel_id=1, source_target_pairs={{0,8},{4,12},{8,0},{12,4},{16,24},{20,28},{24,16},{28,20},{32,40},... | collective-permute-start | bytes 159752 | tf_op jit(solution)/shard_map/ppermute | solution.py:294
  9.0 7.4 %copy-start.4 = (f32[208,128]{1,0:T(8,128)}, f32[208,128]{1,0:T(8,128)S(1)}, u32[]{:S(2)}) copy-start(f32[208,128]{1,0:T(8,128)S(1)} %convert_element_type.201) | copy-start | bytes 319492
  9.2 5.4 %collective-permute-start.2 = (bf16[208,128]{1,0:T(8,128)(2,1)S(1)}, bf16[208,128]{1,0:T(8,128)(2,1)S(1)}, u32[]{:S(2)}, u32[]{:S(2)}) collective-permute-start(bf16[208,128]{1,0:T(8,128)(2,1)S(1)} %maximum_bitcast_fusion.1), channel_id=1, source_target_pairs={{0,24},{4,28},{8,16},{12,20},{16,8},{20,12},{24,0},{28,4},{32,56},... | collective-permute-start | bytes 159752 | tf_op jit(solution)/shard_map/ppermute | solution.py:294
  14.6 7.4 %copy-start.2 = (f32[208,128]{1,0:T(8,128)}, f32[208,128]{1,0:T(8,128)S(1)}, u32[]{:S(2)}) copy-start(f32[208,128]{1,0:T(8,128)S(1)} %convert_element_type.207) | copy-start | bytes 319492
  14.8 4.2 %collective-permute-start.3 = (bf16[208,128]{1,0:T(8,128)(2,1)S(1)}, bf16[208,128]{1,0:T(8,128)(2,1)S(1)}, u32[]{:S(2)}, u32[]{:S(2)}) collective-permute-start(bf16[208,128]{1,0:T(8,128)(2,1)S(1)} %maximum_bitcast_fusion.2), channel_id=1, source_target_pairs={{0,32},{4,36},{8,40},{12,44},{16,48},{20,52},{24,56},{28,60},{32,0... | collective-permute-start | bytes 159752 | tf_op jit(solution)/shard_map/ppermute | solution.py:294
  19.2 5.4 %collective-permute-start.4 = (bf16[208,128]{1,0:T(8,128)(2,1)S(1)}, bf16[208,128]{1,0:T(8,128)(2,1)S(1)}, u32[]{:S(2)}, u32[]{:S(2)}) collective-permute-start(bf16[208,128]{1,0:T(8,128)(2,1)S(1)} %maximum_bitcast_fusion.3), channel_id=1, source_target_pairs={{0,96},{4,100},{8,104},{12,108},{16,112},{20,116},{24,120},{28,124... | collective-permute-start | bytes 159752 | tf_op jit(solution)/shard_map/ppermute | solution.py:294
  24.8 9.1 %collective-permute-start.5 = (bf16[208,128]{1,0:T(8,128)(2,1)S(1)}, bf16[208,128]{1,0:T(8,128)(2,1)S(1)}, u32[]{:S(2)}, u32[]{:S(2)}) collective-permute-start(bf16[208,128]{1,0:T(8,128)(2,1)S(1)} %maximum_bitcast_fusion.4), channel_id=1, source_target_pairs={{0,128},{4,132},{8,136},{12,140},{16,144},{20,148},{24,152},{28,15... | collective-permute-start | bytes 159752 | tf_op jit(solution)/shard_map/ppermute | solution.py:294
  31.2 2.7 %copy-start.1 = (f32[208,128]{1,0:T(8,128)S(1)}, f32[208,128]{1,0:T(8,128)}, u32[]{:S(2)}) copy-start(f32[208,128]{1,0:T(8,128)} %copy-done) | copy-start | bytes 319492
  31.2 2.7 %copy-start.3 = (f32[208,128]{1,0:T(8,128)S(1)}, f32[208,128]{1,0:T(8,128)}, u32[]{:S(2)}) copy-start(f32[208,128]{1,0:T(8,128)} %copy-done.2) | copy-start | bytes 319492
  31.2 2.7 %copy-start.5 = (f32[208,128]{1,0:T(8,128)S(1)}, f32[208,128]{1,0:T(8,128)}, u32[]{:S(2)}) copy-start(f32[208,128]{1,0:T(8,128)} %copy-done.4) | copy-start | bytes 319492
  37.3 19.9 %collective-permute-start.9 = (bf16[128,2560]{1,0:T(8,128)(2,1)}, bf16[128,2560]{1,0:T(8,128)(2,1)}, u32[]{:S(2)}, u32[]{:S(2)}) collective-permute-start(bf16[128,2560]{1,0:T(8,128)(2,1)} %get-tuple-element.47), channel_id=1, source_target_pairs={{0,1},{3,2},{4,5},{7,6},{8,9},{11,10},{12,13},{15,14},{16,17},{19,... | collective-permute-start | bytes 1966088 | tf_op jit(solution)/shard_map/ppermute | solution.py:449
  40.9 23.4 %collective-permute-start.8 = (bf16[64,1536]{1,0:T(8,128)(2,1)S(1)}, bf16[64,1536]{1,0:T(8,128)(2,1)S(1)}, u32[]{:S(2)}, u32[]{:S(2)}) collective-permute-start(bf16[64,1536]{1,0:T(8,128)(2,1)S(1)} %get-tuple-element.46), channel_id=1, source_target_pairs={{0,3},{1,2},{2,1},{3,0},{4,7},{5,6},{6,5},{7,4},{8,11},{9,10},{10,... | collective-permute-start | bytes 589832 | tf_op jit(solution)/shard_map/ppermute | solution.py:449
  42.0 23.9 %collective-permute-start.7 = (bf16[64,1536]{1,0:T(8,128)(2,1)S(1)}, bf16[64,1536]{1,0:T(8,128)(2,1)S(1)}, u32[]{:S(2)}, u32[]{:S(2)}) collective-permute-start(bf16[64,1536]{1,0:T(8,128)(2,1)S(1)} %get-tuple-element.45), channel_id=1, source_target_pairs={{0,2},{1,3},{2,0},{3,1},{4,6},{5,7},{6,4},{7,5},{8,10},{9,11},{10,... | collective-permute-start | bytes 589832 | tf_op jit(solution)/shard_map/ppermute | solution.py:449
  51.2 22.1 %collective-permute-start.6 = (bf16[64,4096]{1,0:T(8,128)(2,1)S(1)}, bf16[64,4096]{1,0:T(8,128)(2,1)S(1)}, u32[]{:S(2)}, u32[]{:S(2)}) collective-permute-start(bf16[64,4096]{1,0:T(8,128)(2,1)S(1)} %get-tuple-element.42), channel_id=1, source_target_pairs={{0,1},{1,0},{2,3},{3,2},{4,5},{5,4},{6,7},{7,6},{8,9},{9,8},{10,11... | collective-permute-start | bytes 1572872 | tf_op jit(solution)/shard_map/ppermute | solution.py:449
  58.3 14.9 %collective-permute-start.10 = (bf16[64,2560]{1,0:T(8,128)(2,1)S(1)}, bf16[64,2560]{1,0:T(8,128)(2,1)S(1)}, u32[]{:S(2)}, u32[]{:S(2)}) collective-permute-start(bf16[64,2560]{1,0:T(8,128)(2,1)S(1)} %add_convert_fusion.1), channel_id=1, source_target_pairs={{1,3},{2,0},{5,7},{6,4},{9,11},{10,8},{13,15},{14,12},{17,19},{18,... | collective-permute-start | bytes 983048 | tf_op jit(solution)/shard_map/ppermute | solution.py:449
  61.4 11.9 %collective-permute-start.11 = (bf16[64,2560]{1,0:T(8,128)(2,1)S(1)}, bf16[64,2560]{1,0:T(8,128)(2,1)S(1)}, u32[]{:S(2)}, u32[]{:S(2)}) collective-permute-start(bf16[64,2560]{1,0:T(8,128)(2,1)S(1)} %add_convert_fusion), channel_id=1, source_target_pairs={{1,2},{2,1},{5,6},{6,5},{9,10},{10,9},{13,14},{14,13},{17,18},{18,... | collective-permute-start | bytes 983048 | tf_op jit(solution)/shard_map/ppermute | solution.py:449
